TPU v7x, 32 devices: a whole 2x2x4 slice. The times are simulated.
32 devices in a mesh: dp: 2 (over core), seq: 4 (over y, x), tp: 4 (over z).
Axes of the slice: x: 2, y: 2, z: 4, core: 2. Of those that a mesh axis runs over, the one named last changes fastest.
Arguments:
- tokens: bfloat16 [4, 1024, 2048], P('dp', 'seq'), may hold values from -6 to 6
- w_query: bfloat16 [2048, 2048], P(('dp', 'seq'), 'tp'), as said below
- w_key: bfloat16 [2048, 2048], P(('dp', 'seq'), 'tp'), as said below
- w_value: bfloat16 [2048, 2048], P(('dp', 'seq'), 'tp'), may hold values from -0.125 to 0.125
- w_out: bfloat16 [2048, 2048], P('tp', ('dp', 'seq')), may hold values from -0.125 to 0.125
- w_gate: bfloat16 [2048, 8192], P(('dp', 'seq'), 'tp'), may hold values from -0.125 to 0.125
- w_up: bfloat16 [2048, 8192], P(('dp', 'seq'), 'tp'), may hold values from -0.125 to 0.125
- w_down: bfloat16 [8192, 2048], P('tp', ('dp', 'seq')), may hold values from -0.0625 to 0.0625
- q_gain: bfloat16 [16, 128], P('tp', ('dp', 'seq')), may hold values from 1 to 2
- k_gain: bfloat16 [16, 128], P('tp', ('dp', 'seq')), may hold values from 0.5 to 1.5
- attn_gain: bfloat16 [16, 128], P(None, ('dp', 'seq')), may hold values from 0.5 to 1.5
- mlp_gain: bfloat16 [16, 128], P(None, ('dp', 'seq')), may hold values from 0.5 to 1.5
- cotangent: bfloat16 [4, 1024, 2048], P('dp', ('seq', 'tp')), may hold values from -6 to 6
Outputs:
- outputs: bfloat16 [4, 1024, 2048], P('dp', ('seq', 'tp'))
- grad_tokens: float32 [4, 1024, 2048], P('dp', ('seq', 'tp'))
- grad_w_query: float32 [2048, 2048], P(('dp', 'seq'), 'tp')
- grad_w_key: float32 [2048, 2048], P(('dp', 'seq'), 'tp')
- grad_w_value: float32 [2048, 2048], P(('dp', 'seq'), 'tp')
- grad_w_out: float32 [2048, 2048], P('tp', ('dp', 'seq'))
- grad_w_gate: float32 [2048, 8192], P(('dp', 'seq'), 'tp')
- grad_w_up: float32 [2048, 8192], P(('dp', 'seq'), 'tp')
- grad_w_down: float32 [8192, 2048], P('tp', ('dp', 'seq'))
- grad_q_gain: float32 [16, 128], P('tp', ('dp', 'seq'))
- grad_k_gain: float32 [16, 128], P('tp', ('dp', 'seq'))
- grad_attn_gain: float32 [16, 128], P('tp', ('dp', 'seq'))
- grad_mlp_gain: float32 [16, 128], P('tp', ('dp', 'seq'))
Inputs may be any that keep to these rules, and one draw needn't show every extreme that they name: `w_query`: entries at most 7 / sqrt(2048) in magnitude. `w_key`: entries at most 7 / sqrt(2048) in magnitude.
All inputs are finite; a program needn't handle non-finite values.
Results may differ from a plain program's by a relative error of at most 0.02.
Values may be sent and summed in bfloat16 or wider, within the bound.
No kernel may reach another device: no remote copies, remote signals or barrier semaphores. Data moves between devices by JAX's collectives and lax.ppermute only.
A program may use at most 192 MiB of HBM per device.

v0:
```python
import math

import jax
import jax.numpy as jnp
from jax import lax
from jax.sharding import PartitionSpec as P

NORM_EPS = 1e-06
ROPE_BASE = 500000.0
MASKED = -1e30


def project(left, right):
    return jnp.dot(left, right, preferred_element_type=jnp.float32)


def project_back(left, right):
    return lax.dot_general(
        left, right, (((left.ndim - 1,), (1,)), ((), ())), preferred_element_type=jnp.float32
    )


def outer_sum(left, right):
    return lax.dot_general(
        left, right, (((0, 1), (0, 1)), ((), ())), preferred_element_type=jnp.float32
    )


def rope_tables(positions, head_dim):
    steps = jnp.arange(head_dim // 2, dtype=jnp.float32)
    freqs = jnp.exp(steps * (-2.0 * math.log(ROPE_BASE) / head_dim))
    angles = positions.astype(jnp.float32)[:, None] * freqs[None, :]
    return (jnp.cos(angles)[:, None, :], jnp.sin(angles)[:, None, :])


def rotate(values, cosines, sines):
    half = values.shape[-1] // 2
    first = values[..., :half]
    second = values[..., half:]
    return jnp.concatenate(
        [first * cosines - second * sines, second * cosines + first * sines], axis=-1
    )


def unrotate(grads, cosines, sines):
    half = grads.shape[-1] // 2
    first = grads[..., :half]
    second = grads[..., half:]
    return jnp.concatenate(
        [first * cosines + second * sines, second * cosines - first * sines], axis=-1
    )


def norm_back(normed, grad_normed, inv_scale, total_dot, d_model):
    return inv_scale * (grad_normed - normed * (total_dot / d_model)[..., None])


def on_device(
    tokens,
    w_query,
    w_key,
    w_value,
    w_out,
    w_gate,
    w_up,
    w_down,
    q_gain,
    k_gain,
    attn_gain,
    mlp_gain,
    cotangent,
):
    seq_count, local_len, d_model = tokens.shape
    seq_rank = lax.axis_index("seq")
    tp_rank = lax.axis_index("tp")
    own_rows = local_len // lax.axis_size("tp")
    weights_in = (
        lax.all_gather(w_query, ("dp", "seq"), axis=0, tiled=True),
        lax.all_gather(w_key, ("dp", "seq"), axis=0, tiled=True),
        lax.all_gather(w_value, ("dp", "seq"), axis=0, tiled=True),
        lax.all_gather(w_out, ("dp", "seq"), axis=1, tiled=True),
        lax.all_gather(w_gate, ("dp", "seq"), axis=0, tiled=True),
        lax.all_gather(w_up, ("dp", "seq"), axis=0, tiled=True),
        lax.all_gather(w_down, ("dp", "seq"), axis=1, tiled=True),
        lax.all_gather(q_gain, ("dp", "seq"), axis=1, tiled=True),
        lax.all_gather(k_gain, ("dp", "seq"), axis=1, tiled=True),
        lax.all_gather(attn_gain, ("dp", "seq"), axis=1, tiled=True),
        lax.all_gather(mlp_gain, ("dp", "seq"), axis=1, tiled=True),
    )
    (
        full_query,
        full_key,
        full_value,
        full_out,
        full_gate,
        full_up,
        full_down,
        full_qgain,
        full_kgain,
        full_again,
        full_mgain,
    ) = weights_in
    local_heads = full_qgain.shape[0]
    head_dim = full_qgain.shape[1]
    head_span = local_heads * head_dim
    score_scale = head_dim ** (-0.5)
    query_gain = full_qgain.astype(jnp.float32).reshape(head_span)
    key_gain = full_kgain.astype(jnp.float32).reshape(head_span)
    attn_scale_gain = full_again.astype(jnp.float32).reshape(d_model)
    mlp_scale_gain = full_mgain.astype(jnp.float32).reshape(d_model)
    query_raw = project(tokens, full_query)
    key_raw = project(tokens, full_key)
    value_raw = project(tokens, full_value)
    query_sq, key_sq = lax.psum(
        (jnp.sum(query_raw * query_raw, axis=-1), jnp.sum(key_raw * key_raw, axis=-1)), "tp"
    )
    query_inv = lax.rsqrt(query_sq / d_model + NORM_EPS)[..., None]
    key_inv = lax.rsqrt(key_sq / d_model + NORM_EPS)[..., None]
    query_unit = query_raw * query_inv
    key_unit = key_raw * key_inv
    positions = seq_rank * local_len + jnp.arange(local_len, dtype=jnp.int32)
    cosines, sines = rope_tables(positions, head_dim)
    heads_shape = (seq_count, local_len, local_heads, head_dim)
    queries = rotate((query_unit * query_gain).reshape(heads_shape), cosines, sines).astype(
        jnp.bfloat16
    )
    keys_local = (
        rotate((key_unit * key_gain).reshape(heads_shape), cosines, sines)
        .astype(jnp.bfloat16)
        .reshape(seq_count, local_len, head_span)
    )
    values_local = value_raw.astype(jnp.bfloat16)
    all_keys, all_values = (
        lax.all_gather(keys_local, "seq", axis=1, tiled=True),
        lax.all_gather(values_local, "seq", axis=1, tiled=True),
    )
    length = all_keys.shape[1]
    keys_full = all_keys.reshape(seq_count, length, local_heads, head_dim)
    values_full = all_values.reshape(seq_count, length, local_heads, head_dim)
    key_rows = min(512, length)
    block_ids = jnp.arange(length // key_rows, dtype=jnp.int32)

    def key_block(block_index):
        first_key = block_index * key_rows
        key_part = lax.dynamic_slice_in_dim(keys_full, first_key, key_rows, 1)
        value_part = lax.dynamic_slice_in_dim(values_full, first_key, key_rows, 1)
        scores = (
            jnp.einsum("mqhd,mkhd->mhqk", queries, key_part, preferred_element_type=jnp.float32)
            * score_scale
        )
        allowed = (first_key + jnp.arange(key_rows, dtype=jnp.int32))[None, :] <= positions[:, None]
        return (key_part, value_part, jnp.where(allowed, scores, MASKED), allowed)

    def max_step(state, block_index):
        running_max, running_sum = state
        key_part, value_part, scores, allowed = key_block(block_index)
        new_max = jnp.maximum(running_max, jnp.max(scores, axis=-1))
        weights_now = jnp.where(allowed, jnp.exp(scores - new_max[..., None]), 0.0)
        return (
            (new_max, running_sum * jnp.exp(running_max - new_max) + jnp.sum(weights_now, axis=-1)),
            None,
        )

    stat_shape = (seq_count, local_heads, local_len)
    final_state, unused = lax.scan(
        max_step,
        (jnp.full(stat_shape, MASKED, jnp.float32), jnp.zeros(stat_shape, jnp.float32)),
        block_ids,
    )
    log_total = (final_state[0] + jnp.log(final_state[1]))[..., None]

    def context_step(context, block_index):
        key_part, value_part, scores, allowed = key_block(block_index)
        probs = jnp.where(allowed, jnp.exp(scores - log_total), 0.0).astype(jnp.bfloat16)
        return (
            context
            + jnp.einsum("mhqk,mkhd->mqhd", probs, value_part, preferred_element_type=jnp.float32),
            None,
        )

    context, unused = lax.scan(context_step, jnp.zeros(heads_shape, jnp.float32), block_ids)
    context_low = context.astype(jnp.bfloat16).reshape(seq_count, local_len, head_span)
    attn_out = lax.psum_scatter(
        project(context_low, full_out), "tp", scatter_dimension=1, tiled=True
    )
    attn_inv = lax.rsqrt(jnp.mean(attn_out * attn_out, axis=-1, keepdims=True) + NORM_EPS)
    attn_unit = attn_out * attn_inv
    own_tokens = lax.dynamic_slice_in_dim(tokens, tp_rank * own_rows, own_rows, 1).astype(
        jnp.float32
    )
    hidden = own_tokens + attn_unit * attn_scale_gain
    hidden_all = lax.all_gather(hidden.astype(jnp.bfloat16), "tp", axis=1, tiled=True)
    gate_act = project(hidden_all, full_gate)
    up_act = project(hidden_all, full_up)
    gate_sig = jax.nn.sigmoid(gate_act)
    mixed = (gate_act * gate_sig * up_act).astype(jnp.bfloat16)
    mlp_out = lax.psum_scatter(project(mixed, full_down), "tp", scatter_dimension=1, tiled=True)
    mlp_inv = lax.rsqrt(jnp.mean(mlp_out * mlp_out, axis=-1, keepdims=True) + NORM_EPS)
    mlp_unit = mlp_out * mlp_inv
    outputs = (hidden + mlp_unit * mlp_scale_gain).astype(jnp.bfloat16)
    weights_back = (
        lax.all_gather(w_query, ("dp", "seq"), axis=0, tiled=True),
        lax.all_gather(w_key, ("dp", "seq"), axis=0, tiled=True),
        lax.all_gather(w_value, ("dp", "seq"), axis=0, tiled=True),
        lax.all_gather(w_out, ("dp", "seq"), axis=1, tiled=True),
        lax.all_gather(w_gate, ("dp", "seq"), axis=0, tiled=True),
        lax.all_gather(w_up, ("dp", "seq"), axis=0, tiled=True),
        lax.all_gather(w_down, ("dp", "seq"), axis=1, tiled=True),
    )
    back_query, back_key, back_value, back_out, back_gate, back_up, back_down = weights_back
    grad_out = cotangent.astype(jnp.float32)
    grad_mgain = jnp.sum(grad_out * mlp_unit, axis=(0, 1))
    mlp_scaled = grad_out * mlp_scale_gain
    grad_mlp = norm_back(
        mlp_unit, mlp_scaled, mlp_inv, jnp.sum(mlp_scaled * mlp_unit, axis=-1), d_model
    ).astype(jnp.bfloat16)
    grad_mlp_all = lax.all_gather(grad_mlp, "tp", axis=1, tiled=True)
    grad_wdown = outer_sum(mixed, grad_mlp_all)
    grad_mixed = project_back(grad_mlp_all, back_down)
    grad_gate = (grad_mixed * up_act * gate_sig * (1.0 + gate_act * (1.0 - gate_sig))).astype(
        jnp.bfloat16
    )
    grad_up = (grad_mixed * gate_act * gate_sig).astype(jnp.bfloat16)
    grad_wgate = outer_sum(hidden_all, grad_gate)
    grad_wup = outer_sum(hidden_all, grad_up)
    hidden_part = project_back(grad_gate, back_gate) + project_back(grad_up, back_up)
    hidden_sum, grad_mgain_part = (
        lax.psum_scatter(hidden_part, "tp", scatter_dimension=1, tiled=True),
        lax.psum_scatter(grad_mgain.reshape(-1, head_dim), "tp", scatter_dimension=0, tiled=True),
    )
    grad_hidden = grad_out + hidden_sum
    grad_again = jnp.sum(grad_hidden * attn_unit, axis=(0, 1))
    attn_scaled = grad_hidden * attn_scale_gain
    grad_attn = norm_back(
        attn_unit, attn_scaled, attn_inv, jnp.sum(attn_scaled * attn_unit, axis=-1), d_model
    ).astype(jnp.bfloat16)
    grad_attn_all = lax.all_gather(grad_attn, "tp", axis=1, tiled=True)
    grad_wout = outer_sum(context_low, grad_attn_all)
    grad_context = project_back(grad_attn_all, back_out).astype(jnp.bfloat16).reshape(heads_shape)

    def delta_step(delta, block_index):
        key_part, value_part, scores, allowed = key_block(block_index)
        probs = jnp.exp(scores - log_total)
        grad_probs = jnp.einsum(
            "mqhd,mkhd->mhqk", grad_context, value_part, preferred_element_type=jnp.float32
        )
        return (delta + jnp.sum(probs * grad_probs, axis=-1), None)

    delta, unused = lax.scan(delta_step, jnp.zeros(stat_shape, jnp.float32), block_ids)

    def score_grads(block_index):
        key_part, value_part, scores, allowed = key_block(block_index)
        probs = jnp.exp(scores - log_total)
        grad_probs = jnp.einsum(
            "mqhd,mkhd->mhqk", grad_context, value_part, preferred_element_type=jnp.float32
        )
        grad_scores = (probs * (grad_probs - delta[..., None])).astype(jnp.bfloat16)
        return (key_part, probs, grad_scores)

    def grad_step(grad_queries, block_index):
        key_part, probs, grad_scores = score_grads(block_index)
        grad_queries = grad_queries + jnp.einsum(
            "mhqk,mkhd->mqhd", grad_scores, key_part, preferred_element_type=jnp.float32
        )
        grad_keys = (
            jnp.einsum("mhqk,mqhd->kmhd", grad_scores, queries, preferred_element_type=jnp.float32)
            * score_scale
        )
        grad_values = jnp.einsum(
            "mhqk,mqhd->kmhd",
            probs.astype(jnp.bfloat16),
            grad_context,
            preferred_element_type=jnp.float32,
        )
        both_terms = jnp.concatenate(
            [
                grad_keys.reshape(key_rows, seq_count, head_span),
                grad_values.reshape(key_rows, seq_count, head_span),
            ],
            axis=-1,
        )
        return (grad_queries, both_terms)

    grad_queries, key_terms = lax.scan(grad_step, jnp.zeros(heads_shape, jnp.float32), block_ids)
    key_value_grads = lax.psum_scatter(
        key_terms.reshape(length, seq_count, 2 * head_span).astype(jnp.bfloat16),
        "seq",
        scatter_dimension=0,
        tiled=True,
    ).astype(jnp.float32)
    key_value_grads = jnp.transpose(key_value_grads, (1, 0, 2))
    grad_keys_own = key_value_grads[..., :head_span].reshape(heads_shape)
    grad_values_own = key_value_grads[..., head_span:].astype(jnp.bfloat16)
    query_grad_unit = unrotate(grad_queries * score_scale, cosines, sines).reshape(
        seq_count, local_len, head_span
    )
    key_grad_unit = unrotate(grad_keys_own, cosines, sines).reshape(seq_count, local_len, head_span)
    grad_qgain = jnp.sum(query_grad_unit * query_unit, axis=(0, 1))
    grad_kgain = jnp.sum(key_grad_unit * key_unit, axis=(0, 1))
    query_scaled = query_grad_unit * query_gain
    key_scaled = key_grad_unit * key_gain
    query_dot, key_dot = lax.psum(
        (jnp.sum(query_scaled * query_unit, axis=-1), jnp.sum(key_scaled * key_unit, axis=-1)), "tp"
    )
    grad_qraw = norm_back(query_unit, query_scaled, query_inv, query_dot, d_model).astype(
        jnp.bfloat16
    )
    grad_kraw = norm_back(key_unit, key_scaled, key_inv, key_dot, d_model).astype(jnp.bfloat16)
    grad_wquery = outer_sum(tokens, grad_qraw)
    grad_wkey = outer_sum(tokens, grad_kraw)
    grad_wvalue = outer_sum(tokens, grad_values_own)
    token_part = (
        project_back(grad_qraw, back_query)
        + project_back(grad_kraw, back_key)
        + project_back(grad_values_own, back_value)
    )
    token_sum, grad_again_part = (
        lax.psum_scatter(
            token_part.astype(jnp.bfloat16), "tp", scatter_dimension=1, tiled=True
        ).astype(jnp.float32),
        lax.psum_scatter(
            grad_again.reshape(-1, head_dim).astype(jnp.bfloat16),
            "tp",
            scatter_dimension=0,
            tiled=True,
        ).astype(jnp.float32),
    )
    grad_tokens = grad_hidden + token_sum
    summed = (
        lax.psum_scatter(
            grad_wquery.astype(jnp.bfloat16), ("dp", "seq"), scatter_dimension=0, tiled=True
        ).astype(jnp.float32),
        lax.psum_scatter(
            grad_wkey.astype(jnp.bfloat16), ("dp", "seq"), scatter_dimension=0, tiled=True
        ).astype(jnp.float32),
        lax.psum_scatter(
            grad_wvalue.astype(jnp.bfloat16), ("dp", "seq"), scatter_dimension=0, tiled=True
        ).astype(jnp.float32),
        lax.psum_scatter(
            grad_wout.astype(jnp.bfloat16), ("dp", "seq"), scatter_dimension=1, tiled=True
        ).astype(jnp.float32),
        lax.psum_scatter(
            grad_wgate.astype(jnp.bfloat16), ("dp", "seq"), scatter_dimension=0, tiled=True
        ).astype(jnp.float32),
        lax.psum_scatter(
            grad_wup.astype(jnp.bfloat16), ("dp", "seq"), scatter_dimension=0, tiled=True
        ).astype(jnp.float32),
        lax.psum_scatter(
            grad_wdown.astype(jnp.bfloat16), ("dp", "seq"), scatter_dimension=1, tiled=True
        ).astype(jnp.float32),
        lax.psum_scatter(
            grad_qgain.reshape(local_heads, head_dim).astype(jnp.bfloat16),
            ("dp", "seq"),
            scatter_dimension=1,
            tiled=True,
        ).astype(jnp.float32),
        lax.psum_scatter(
            grad_kgain.reshape(local_heads, head_dim).astype(jnp.bfloat16),
            ("dp", "seq"),
            scatter_dimension=1,
            tiled=True,
        ).astype(jnp.float32),
        lax.psum_scatter(
            grad_again_part.astype(jnp.bfloat16), ("dp", "seq"), scatter_dimension=1, tiled=True
        ).astype(jnp.float32),
        lax.psum_scatter(
            grad_mgain_part.astype(jnp.bfloat16), ("dp", "seq"), scatter_dimension=1, tiled=True
        ).astype(jnp.float32),
    )
    (
        sum_query,
        sum_key,
        sum_value,
        sum_out,
        sum_gate,
        sum_up,
        sum_down,
        sum_qgain,
        sum_kgain,
        sum_again,
        sum_mgain,
    ) = summed
    return (
        outputs,
        grad_tokens,
        sum_query,
        sum_key,
        sum_value,
        sum_out,
        sum_gate,
        sum_up,
        sum_down,
        sum_qgain,
        sum_kgain,
        sum_again,
        sum_mgain,
    )


def solution(mesh):
    return jax.shard_map(
        on_device,
        mesh=mesh,
        in_specs=(
            P("dp", "seq", None),
            P(("dp", "seq"), "tp"),
            P(("dp", "seq"), "tp"),
            P(("dp", "seq"), "tp"),
            P("tp", ("dp", "seq")),
            P(("dp", "seq"), "tp"),
            P(("dp", "seq"), "tp"),
            P("tp", ("dp", "seq")),
            P("tp", ("dp", "seq")),
            P("tp", ("dp", "seq")),
            P(None, ("dp", "seq")),
            P(None, ("dp", "seq")),
            P("dp", ("seq", "tp"), None),
        ),
        out_specs=(
            P("dp", ("seq", "tp"), None),
            P("dp", ("seq", "tp"), None),
            P(("dp", "seq"), "tp"),
            P(("dp", "seq"), "tp"),
            P(("dp", "seq"), "tp"),
            P("tp", ("dp", "seq")),
            P(("dp", "seq"), "tp"),
            P(("dp", "seq"), "tp"),
            P("tp", ("dp", "seq")),
            P("tp", ("dp", "seq")),
            P("tp", ("dp", "seq")),
            P("tp", ("dp", "seq")),
            P("tp", ("dp", "seq")),
        ),
        check_vma=False,
    )
```

profile of v0, /device:TPU:0, one launch (start us, length us, event | category | flops | bytes accessed | tf_op | source)
XLA Modules:
  0.0 1499.3 jit_solution(16688796056236179675)
XLA Ops:
  9.4 15.1 %all-gather = bf16[8,16,4]{1,2,0:T(4,128)(2,1)S(1)} all-gather(bf16[1,16,4]{1,2,0:T(4,128)(2,1)} %bitcast.347), channel_id=1, replica_groups=mesh['dp'=2,'seq'=4,'tp'=4] {'dp','seq'}, dimensions={0}, use_global_device_ids=true | all-gather | bytes 1152 | tf_op jit(solution)/shard_map/all_gather | solution.py:86
  24.6 13.5 all-gather.1
  44.1 26.3 %all-gather.23.cloned.1.call-done = bf16[2048,512]{1,0:T(8,128)(2,1)} async-done(((bf16[256,512]{1,0:T(8,128)(2,1)}), bf16[2048,512]{1,0:T(8,128)(2,1)}) %all-gather.23.cloned.1.call-update) | async-done | bytes 2097168 | tf_op jit(solution)/shard_map/all_gather | solution.py:78
  105.5 32.2 %all-gather.21.cloned.1.call-done = bf16[2,1024,512]{1,2,0:T(8,128)(2,1)} async-done(((bf16[2,256,512]{1,2,0:T(8,128)(2,1)}), bf16[2,1024,512]{1,2,0:T(8,128)(2,1)}) %all-gather.21.cloned.1.call-update) | async-done | bytes 2097168 | tf_op jit(solution)/shard_map/all_gather | solution.py:134
  140.7 15.0 %while.48 = (s32[]{:T(128)}, f32[2,4,256]{2,1,0:T(4,128)S(1)}, f32[2,4,256]{2,1,0:T(4,128)S(1)}, s32[2]{0:T(128)S(1)}, bf16[2,1024,4,128]{3,1,2,0:T(8,128)(2,1)S...) while((s32[]{:T(128)}, f32[2,4,256]{2,1,0:T(4,128)S(1)}, ...), condition=%wide.region_7.8_spmd.clone, body=%wide.region_4.7_spmd.clone.sunk | while | flops 276966144 | bytes 10467518 | solution.py:165
  155.7 19.6 %all-gather.17.cloned.1.call-done = bf16[2,1024,512]{2,1,0:T(8,128)(2,1)} async-done(((bf16[2,256,512]{2,1,0:T(8,128)(2,1)}), bf16[2,1024,512]{2,1,0:T(8,128)(2,1)}) %all-gather.17.cloned.1.call-update) | async-done | bytes 2097168 | tf_op jit(solution)/shard_map/all_gather | solution.py:135
  179.2 15.9 %while.49 = (s32[]{:T(128)}, f32[2,256,4,128]{1,3,2,0:T(8,128)}, s32[2]{0:T(128)S(1)}, bf16[2,1024,4,128]{3,2,1,0:T(4,128)(2,1)}, bf16[2,1024,4,128]{3,1,2,0:T(8...) while((s32[]{:T(128)}, f32[2,256,4,128]{1,3,2,0:T(8,128)}, ...), condition=%wide.region_9.10_spmd.clone, body=%wide.region_8.9_spmd.clone.sunk | while | flops 542769920 | bytes 7092425 | solution.py:181
  211.3 23.0 %all_gather.63 = bf16[16,128]{0,1:T(8,128)(2,1)S(1)} all-gather(bf16[16,16]{0,1:T(8,128)(2,1)S(1)} %copy.196), channel_id=1, replica_groups=mesh['dp'=2,'seq'=4,'tp'=4] {'dp','seq'}, dimensions={1}, use_global_device_ids=true | all-gather | bytes 4608 | tf_op jit(solution)/shard_map/all_gather | solution.py:87
  234.3 53.0 %reduce-scatter.25.cloned.1.call-done = f32[2,64,2048]{2,1,0:T(8,128)} async-done(((f32[2,256,2048]{2,1,0:T(8,128)}), f32[2,64,2048]{2,1,0:T(8,128)}) %reduce-scatter.25.cloned.1.call-update) | async-done | bytes 1048592 | tf_op jit(solution)/shard_map/reduce_scatter | solution.py:183
  292.7 51.6 %all-gather.29.cloned.1.call-done = bf16[2048,2048]{1,0:T(8,128)(2,1)} async-done(((bf16[256,2048]{1,0:T(8,128)(2,1)}), bf16[2048,2048]{1,0:T(8,128)(2,1)}) %all-gather.29.cloned.1.call-update) | async-done | bytes 8388624 | tf_op jit(solution)/shard_map/all_gather | solution.py:82
  344.3 48.2 %all-gather.27.cloned.1.call-done = bf16[2,256,2048]{2,1,0:T(8,128)(2,1)} async-done(((bf16[2,64,2048]{2,1,0:T(8,128)(2,1)}), bf16[2,256,2048]{2,1,0:T(8,128)(2,1)}) %all-gather.27.cloned.1.call-update) | async-done | bytes 2097168 | tf_op jit(solution)/shard_map/all_gather | solution.py:192
  403.1 44.4 %all-gather.31.cloned.1.call-done = bf16[2048,2048]{1,0:T(8,128)(2,1)} async-done(((bf16[256,2048]{1,0:T(8,128)(2,1)}), bf16[2048,2048]{1,0:T(8,128)(2,1)}) %all-gather.31.cloned.1.call-update) | async-done | bytes 8388624 | tf_op jit(solution)/shard_map/all_gather | solution.py:83
  447.5 12.5 multiply_convert_fusion.2
  460.0 45.5 %all-gather.33.cloned.1.call-done = bf16[2048,2048]{1,0:T(8,128)(2,1)} async-done(((bf16[2048,256]{1,0:T(8,128)(2,1)}), bf16[2048,2048]{1,0:T(8,128)(2,1)}) %all-gather.33.cloned.1.call-update) | async-done | bytes 8388624 | tf_op jit(solution)/shard_map/all_gather | solution.py:84
  516.9 22.3 %all_gather.68 = bf16[16,128]{0,1:T(8,128)(2,1)S(1)} all-gather(bf16[16,16]{0,1:T(8,128)(2,1)S(1)} %copy.198), channel_id=1, replica_groups=mesh['dp'=2,'seq'=4,'tp'=4] {'dp','seq'}, dimensions={1}, use_global_device_ids=true | all-gather | bytes 4608 | tf_op jit(solution)/shard_map/all_gather | solution.py:88
  539.3 53.8 %reduce-scatter.27.cloned.1.call-done = f32[2,64,2048]{2,1,0:T(8,128)} async-done(((f32[2,256,2048]{2,1,0:T(8,128)}), f32[2,64,2048]{2,1,0:T(8,128)}) %reduce-scatter.27.cloned.1.call-update) | async-done | bytes 1048592 | tf_op jit(solution)/shard_map/reduce_scatter | solution.py:197
  598.6 46.2 %all-gather.35.cloned.1.call-done = bf16[2,256,2048]{2,1,0:T(8,128)(2,1)} async-done(((bf16[2,64,2048]{2,1,0:T(8,128)(2,1)}), bf16[2,256,2048]{2,1,0:T(8,128)(2,1)}) %all-gather.35.cloned.1.call-update) | async-done | bytes 2097168 | tf_op jit(solution)/shard_map/all_gather | solution.py:217
  674.8 75.6 %reduce-scatter.29.cloned.1.call-done = f32[2,64,2048]{2,1,0:T(8,128)} async-done(((f32[2,256,2048]{2,1,0:T(8,128)}), f32[2,64,2048]{2,1,0:T(8,128)}) %reduce-scatter.29.cloned.1.call-update) | async-done | bytes 1048592 | tf_op jit(solution)/shard_map/reduce_scatter | solution.py:228
  759.3 43.1 %all-gather.37.cloned.1.call-done = bf16[2,256,2048]{2,1,0:T(8,128)(2,1)} async-done(((bf16[2,64,2048]{2,1,0:T(8,128)(2,1)}), bf16[2,256,2048]{2,1,0:T(8,128)(2,1)}) %all-gather.37.cloned.1.call-update) | async-done | bytes 2097168 | tf_op jit(solution)/shard_map/all_gather | solution.py:237
  818.1 24.7 %while.51 = (s32[]{:T(128)}, f32[2,256,4,128]{1,3,2,0:T(8,128)}, bf16[2,512,2,1024]{1,3,2,0:T(8,128)(2,1)}, s32[2]{0:T(128)S(1)}, bf16[2,1024,4,128]{3,1,2,0:T(8...) while((s32[]{:T(128)}, f32[2,256,4,128]{1,3,2,0:T(8,128)}, ...), condition=%wide.region_21.22_spmd.clone, body=%wide.region_20.21_spmd.clone.sunk | while | flops 1358562048 | bytes 51804984 | solution.py:284
  909.6 18.7 %all-reduce.2 = (f32[2,256]{1,0:T(2,128)S(1)}, f32[2,256]{1,0:T(2,128)S(1)}, bf16[16,128]{1,0:T(8,128)(2,1)S(1)}) all-reduce(f32[2,256]{1,0:T(2,128)S(1)} %get-tuple-element.578, f32[2,256]{1,0:T(2,128)S(1)} %get-tuple-element.576, f32[16,128]{1,0:T(8,128)S(1)} %bitcast.329), channel_id=1, replica_groups=mesh['dp'=2,'seq'=4,'tp'=4] {'tp'}, use_global_device_ids=true, to_apply=%region_23.24 | all-reduce | flops 3072 | bytes 20480 | tf_op jit(solution)/shard_map/psum | solution.py:302
  958.1 52.3 %reduce-scatter.47.cloned.1.call-done = bf16[2048,256]{1,0:T(8,128)(2,1)} async-done(((bf16[2048,2048]{1,0:T(8,128)(2,1)}), bf16[2048,256]{1,0:T(8,128)(2,1)}) %reduce-scatter.47.cloned.1.call-update) | async-done | bytes 1048592 | tf_op jit(solution)/shard_map/reduce_scatter | solution.py:348
  1013.2 72.1 %reduce-scatter.43.cloned.1.call-done = bf16[256,2048]{1,0:T(8,128)(2,1)} async-done(((bf16[2048,2048]{1,0:T(8,128)(2,1)}), bf16[256,2048]{1,0:T(8,128)(2,1)}) %reduce-scatter.43.cloned.1.call-update) | async-done | bytes 1048592 | tf_op jit(solution)/shard_map/reduce_scatter | solution.py:342
  1088.0 72.2 %reduce-scatter.45.cloned.1.call-done = bf16[256,2048]{1,0:T(8,128)(2,1)} async-done(((bf16[2048,2048]{1,0:T(8,128)(2,1)}), bf16[256,2048]{1,0:T(8,128)(2,1)}) %reduce-scatter.45.cloned.1.call-update) | async-done | bytes 1048592 | tf_op jit(solution)/shard_map/reduce_scatter | solution.py:345
  1163.0 41.8 %reduce-scatter.41.cloned.1.call-done = bf16[512,256]{1,0:T(8,128)(2,1)} async-done(((bf16[512,2048]{1,0:T(8,128)(2,1)}), bf16[512,256]{1,0:T(8,128)(2,1)}) %reduce-scatter.41.cloned.1.call-update) | async-done | bytes 262160 | tf_op jit(solution)/shard_map/reduce_scatter | solution.py:339
  1206.6 33.4 %reduce-scatter.55.cloned.1.call-done = bf16[16,4]{1,0:T(8,128)(2,1)} async-done(((bf16[128,4]{1,0:T(8,128)(2,1)}), bf16[16,4]{1,0:T(8,128)(2,1)}) %reduce-scatter.55.cloned.1.call-update) | async-done | bytes 144
  1241.3 33.5 %reduce-scatter.51.cloned.1.call-done = bf16[16,4]{1,0:T(8,128)(2,1)} async-done(((bf16[128,4]{1,0:T(8,128)(2,1)}), bf16[16,4]{1,0:T(8,128)(2,1)}) %reduce-scatter.51.cloned.1.call-update) | async-done | bytes 144
  1276.2 33.7 %reduce-scatter.49.cloned.1.call-done = bf16[16,4]{1,0:T(8,128)(2,1)} async-done(((bf16[128,4]{1,0:T(8,128)(2,1)}), bf16[16,4]{1,0:T(8,128)(2,1)}) %reduce-scatter.49.cloned.1.call-update) | async-done | bytes 144
  1311.2 43.2 %reduce-scatter.37.cloned.1.call-done = bf16[256,512]{0,1:T(8,128)(2,1)} async-done(((bf16[2048,512]{0,1:T(8,128)(2,1)}), bf16[256,512]{0,1:T(8,128)(2,1)}) %reduce-scatter.37.cloned.1.call-update) | async-done | bytes 262160 | tf_op jit(solution)/shard_map/reduce_scatter | solution.py:333
  1356.3 42.9 %reduce-scatter.35.cloned.1.call-done = bf16[256,512]{0,1:T(8,128)(2,1)} async-done(((bf16[2048,512]{0,1:T(8,128)(2,1)}), bf16[256,512]{0,1:T(8,128)(2,1)}) %reduce-scatter.35.cloned.1.call-update) | async-done | bytes 262160 | tf_op jit(solution)/shard_map/reduce_scatter | solution.py:330
  1401.0 42.5 %reduce-scatter.39.cloned.1.call-done = bf16[256,512]{0,1:T(8,128)(2,1)} async-done(((bf16[2048,512]{0,1:T(8,128)(2,1)}), bf16[256,512]{0,1:T(8,128)(2,1)}) %reduce-scatter.39.cloned.1.call-update) | async-done | bytes 262160 | tf_op jit(solution)/shard_map/reduce_scatter | solution.py:336
  1445.4 44.4 %reduce-scatter.33.cloned.1.call-done = bf16[2,64,2048]{2,1,0:T(8,128)(2,1)} async-done(((bf16[2,256,2048]{2,1,0:T(8,128)(2,1)}), bf16[2,64,2048]{2,1,0:T(8,128)(2,1)}) %reduce-scatter.33.cloned.1.call-update) | async-done | bytes 524304 | tf_op jit(solution)/shard_map/reduce_scatter | solution.py:318
  (348 shorter events, 329.5 us)
Async XLA Ops:
  7.2 33.4 %all-gather.19.cloned.1.call-start = ((), (), s32[]{:S(2)}) async-start(), calls=%async_computation.18 | async-start | bytes 2359296 | tf_op jit(solution)/shard_map/all_gather | solution.py:79
  7.9 62.5 %all-gather.23.cloned.1.call-start = ((), (), s32[]{:S(2)}) async-start(), calls=%async_computation.20 | async-start | bytes 2359296 | tf_op jit(solution)/shard_map/all_gather | solution.py:78
  8.7 91.5 %all-gather.15.cloned.1.call-start = ((), (), s32[]{:S(2)}) async-start(), calls=%async_computation.16 | async-start | bytes 2359296 | tf_op jit(solution)/shard_map/all_gather | solution.py:80
  9.4 128.3 %all-gather.21.cloned.1.call-start = ((), (), s32[]{:S(2)}) async-start(), calls=%async_computation.19 | async-start | bytes 2621440 | tf_op jit(solution)/shard_map/all_gather | solution.py:134
  24.6 61.1 %copy-start.37 = (f32[128,4]{0,1:T(4,128)}, f32[128,4]{0,1:T(4,128)S(1)}, u32[]{:S(2)}) copy-start(f32[128,4]{0,1:T(4,128)S(1)} %reshape.220) | copy-start | bytes 6148
  38.5 48.7 %copy-start.27 = (f32[256,64]{0,1:T(8,128)}, f32[256,64]{0,1:T(8,128)S(1)}, u32[]{:S(2)}) copy-start(f32[256,64]{0,1:T(8,128)S(1)} %get-tuple-element.674) | copy-start | bytes 196612
  88.4 86.8 %all-gather.17.cloned.1.call-start = ((), (), s32[]{:S(2)}) async-start(), calls=%async_computation.17 | async-start | bytes 2621440 | tf_op jit(solution)/shard_map/all_gather | solution.py:135
  104.5 100.7 %all-gather.25.cloned.1.call-start = ((), (), s32[]{:S(2)}) async-start(), calls=%async_computation.21 | async-start | bytes 2359296 | tf_op jit(solution)/shard_map/all_gather | solution.py:81
  105.1 182.2 %reduce-scatter.25.cloned.1.call-start = ((), (), s32[]{:S(2)}) async-start(), calls=%async_computation.22 | async-start | bytes 5242880 | tf_op jit(solution)/shard_map/reduce_scatter | solution.py:183
  210.4 133.9 %all-gather.29.cloned.1.call-start = ((), (), s32[]{:S(2)}) async-start(), calls=%async_computation.24 | async-start | bytes 9437184 | tf_op jit(solution)/shard_map/all_gather | solution.py:82
  211.1 181.4 %all-gather.27.cloned.1.call-start = ((), (), s32[]{:S(2)}) async-start(), calls=%async_computation.23 | async-start | bytes 2621440 | tf_op jit(solution)/shard_map/all_gather | solution.py:192
  291.1 156.4 %all-gather.31.cloned.1.call-start = ((), (), s32[]{:S(2)}) async-start(), calls=%async_computation.25 | async-start | bytes 9437184 | tf_op jit(solution)/shard_map/all_gather | solution.py:83
  291.7 213.9 %all-gather.33.cloned.1.call-start = ((), (), s32[]{:S(2)}) async-start(), calls=%async_computation.26 | async-start | bytes 9437184 | tf_op jit(solution)/shard_map/all_gather | solution.py:84
  292.4 300.7 %reduce-scatter.27.cloned.1.call-start = ((), (), s32[]{:S(2)}) async-start(), calls=%async_computation.27 | async-start | bytes 5242880 | tf_op jit(solution)/shard_map/reduce_scatter | solution.py:197
  516.2 128.5 %all-gather.35.cloned.1.call-start = ((), (), s32[]{:S(2)}) async-start(), calls=%async_computation.28 | async-start | bytes 2621440 | tf_op jit(solution)/shard_map/all_gather | solution.py:217
  598.1 152.3 %reduce-scatter.29.cloned.1.call-start = ((), (), s32[]{:S(2)}) async-start(), calls=%async_computation.29 | async-start | bytes 5242880 | tf_op jit(solution)/shard_map/reduce_scatter | solution.py:228
  674.8 127.6 %all-gather.37.cloned.1.call-start = ((), (), s32[]{:S(2)}) async-start(), calls=%async_computation.30 | async-start | bytes 2621440 | tf_op jit(solution)/shard_map/all_gather | solution.py:237
  755.8 144.9 %reduce-scatter.31.cloned.1.call-start = ((), (), s32[]{:S(2)}) async-start(), calls=%async_computation.31 | async-start | bytes 5242880 | tf_op jit(solution)/shard_map/reduce_scatter | solution.py:285
  849.1 107.6 %reduce-scatter.53.cloned.1.call-start = ((), (), s32[]{:S(2)}) async-start(), calls=%async_computation.42 | async-start | bytes 36864
  861.3 149.2 %reduce-scatter.47.cloned.1.call-start = ((), (), s32[]{:S(2)}) async-start(), calls=%async_computation.39 | async-start | bytes 9437184 | tf_op jit(solution)/shard_map/reduce_scatter | solution.py:348
  869.9 215.3 %reduce-scatter.43.cloned.1.call-start = ((), (), s32[]{:S(2)}) async-start(), calls=%async_computation.37 | async-start | bytes 9437184 | tf_op jit(solution)/shard_map/reduce_scatter | solution.py:342
  879.9 280.4 %reduce-scatter.45.cloned.1.call-start = ((), (), s32[]{:S(2)}) async-start(), calls=%async_computation.38 | async-start | bytes 9437184 | tf_op jit(solution)/shard_map/reduce_scatter | solution.py:345
  888.4 316.4 %reduce-scatter.41.cloned.1.call-start = ((), (), s32[]{:S(2)}) async-start(), calls=%async_computation.36 | async-start | bytes 2359296 | tf_op jit(solution)/shard_map/reduce_scatter | solution.py:339
  892.7 347.2 %reduce-scatter.55.cloned.1.call-start = ((), (), s32[]{:S(2)}) async-start(), calls=%async_computation.43 | async-start | bytes 36864
  929.1 345.7 %reduce-scatter.51.cloned.1.call-start = ((), (), s32[]{:S(2)}) async-start(), calls=%async_computation.41 | async-start | bytes 36864
  929.9 379.9 %reduce-scatter.49.cloned.1.call-start = ((), (), s32[]{:S(2)}) async-start(), calls=%async_computation.40 | async-start | bytes 36864
  933.0 421.4 %reduce-scatter.37.cloned.1.call-start = ((), (), s32[]{:S(2)}) async-start(), calls=%async_computation.34 | async-start | bytes 2359296 | tf_op jit(solution)/shard_map/reduce_scatter | solution.py:333
  937.5 461.6 %reduce-scatter.35.cloned.1.call-start = ((), (), s32[]{:S(2)}) async-start(), calls=%async_computation.33 | async-start | bytes 2359296 | tf_op jit(solution)/shard_map/reduce_scatter | solution.py:330
  941.8 501.7 %reduce-scatter.39.cloned.1.call-start = ((), (), s32[]{:S(2)}) async-start(), calls=%async_computation.35 | async-start | bytes 2359296 | tf_op jit(solution)/shard_map/reduce_scatter | solution.py:336
  947.4 542.4 %reduce-scatter.33.cloned.1.call-start = ((), (), s32[]{:S(2)}) async-start(), calls=%async_computation.32 | async-start | bytes 2621440 | tf_op jit(solution)/shard_map/reduce_scatter | solution.py:318
  1163.0 326.8 %copy-start.7 = (bf16[2,64,2048]{2,1,0:T(8,128)(2,1)S(1)}, bf16[2,64,2048]{2,1,0:T(8,128)(2,1)}, u32[]{:S(2)}) copy-start(bf16[2,64,2048]{2,1,0:T(8,128)(2,1)} %param.33) | copy-start | bytes 1572868
  1163.0 326.8 %copy-start.12 = (f32[2,64,2048]{2,1,0:T(8,128)S(1)}, f32[2,64,2048]{2,1,0:T(8,128)}, u32[]{:S(2)}) copy-start(f32[2,64,2048]{2,1,0:T(8,128)} %reduce-scatter.29.cloned.1.call-done) | copy-start | bytes 3145732
  (52 other events, 283.0 us)
Sparse Core Ops, SparseCore 0:
  9.9 30.6 all-gather.18
  42.4 27.8 all-gather.22
  72.3 27.8 all-gather.14
  102.4 35.1 all-gather.20
  139.9 35.3 all-gather.16
  177.0 28.1 all-gather.24
  210.5 76.7 reduce-scatter.24
  289.4 54.8 all-gather.28
  346.5 45.9 all-gather.26
  394.4 53.0 all-gather.30
  449.6 55.9 all-gather.32
  516.3 76.7 reduce-scatter.26
  598.2 46.4 all-gather.34
  674.9 75.4 reduce-scatter.28
  755.9 46.4 all-gather.36
  849.3 51.4 reduce-scatter.30
  904.1 31.2 reduce-scatter.52
  939.1 71.2 reduce-scatter.46
  1013.9 71.2 reduce-scatter.42
  1088.9 71.2 reduce-scatter.44
  1163.5 41.2 reduce-scatter.40
  1208.6 31.2 reduce-scatter.54
  1243.5 31.2 reduce-scatter.50
  1278.5 31.2 reduce-scatter.48
  1313.1 41.2 reduce-scatter.36
  1357.9 41.2 reduce-scatter.34
  1402.3 41.2 reduce-scatter.38
  1445.9 43.8 reduce-scatter.32
where the time goes:
time: 1510 us; the launch traced here: 1500 us
  waiting for transfers between devices  1080 us (72%)
  matrix products  160 us (11%)
  blocking collectives  114 us (8%)
  local copies, waits for them, and re-layouts  65.4 us (4%)
  other arithmetic  51.2 us (3%)
  between operations  16.2 us (1%)
    unnamed x32, waiting for transfers between devices  105 us
    reduce_scatter x1, waiting for transfers between devices, on_device(): lax.psum_scatter(hidden_part, 'tp', scatter_dimension=1, tiled=True)  75.6 us
    reduce_scatter x1, waiting for transfers between devices, on_device(): lax.psum_scatter(grad_wup.astype(jnp.bfloat16), ('dp', 'seq'), scatter_di...  72.2 us
    reduce_scatter x1, waiting for transfers between devices, on_device(): lax.psum_scatter(grad_wgate.astype(jnp.bfloat16), ('dp', 'seq'), scatter_...  72.1 us
    reduce_scatter x1, waiting for transfers between devices, on_device(): lax.psum_scatter(project(mixed, full_down), 'tp', scatter_dimension=1, ti...  53.8 us
    reduce_scatter x1, waiting for transfers between devices, on_device(): lax.psum_scatter(project(context_low, full_out), 'tp', scatter_dimension=...  53 us
    reduce_scatter x1, waiting for transfers between devices, on_device(): lax.psum_scatter(grad_wdown.astype(jnp.bfloat16), ('dp', 'seq'), scatter_...  52.3 us
    all_gather x1, waiting for transfers between devices, on_device(): lax.all_gather(w_gate, ('dp', 'seq'), axis=0, tiled=True)  51.6 us
  transfers between devices with their start and end apart: 28, of which 27 were waited for; matrix products, arithmetic and copies ran while one was open for 11% of the time, Pallas kernels for 0%

commit v1 on v0

--- a/solution.py
+++ b/solution.py
@@ -3,6 +3,8 @@
 import jax
 import jax.numpy as jnp
 from jax import lax
+from jax.experimental import pallas as pl
+from jax.experimental.pallas import tpu as pltpu
 from jax.sharding import PartitionSpec as P
 
 NORM_EPS = 1e-06
@@ -55,7 +57,7 @@
     return inv_scale * (grad_normed - normed * (total_dot / d_model)[..., None])
 
 
-def on_device(
+def on_any_mesh(
     tokens,
     w_query,
     w_key,
@@ -397,9 +399,493 @@
     )
 
 
+VMEM_LIMIT = 48 * 1024 * 1024
+
+
+def to_neighbour(values, flip):
+    return lax.ppermute(values, "seq", [(i, i ^ flip) for i in range(4)])
+
+
+def to_core(values):
+    return lax.ppermute(values, "dp", [(0, 1), (1, 0)])
+
+
+def after(values, done):
+    return lax.optimization_barrier((values, done))[0]
+
+
+def gather_plane(shard, axis):
+    half = shard.shape[0] // 2
+    from_one = to_neighbour(shard, 1)
+    from_two = to_neighbour(shard, 2)
+    far_low = to_neighbour(from_two[:half], 1)
+    far_high = to_neighbour(from_one[half:], 2)
+    far = jnp.concatenate([far_low, far_high], axis=0)
+    mine = jnp.concatenate([shard, from_one, from_two, far], axis=axis)
+    return jnp.concatenate([mine, to_core(mine)], axis=axis)
+
+
+def scatter_plane(kept, sent, axis):
+    def blocks(values):
+        return jnp.split(values.astype(jnp.float32), 4, axis=axis)
+
+    low = jnp.bfloat16
+    mine = [a + b for a, b in zip(blocks(kept), blocks(to_core(sent)))]
+    half = mine[3].shape[0] // 2
+    far_low = to_neighbour(mine[3][:half].astype(low), 1).astype(jnp.float32)
+    far_high = to_neighbour(mine[3][half:].astype(low), 2).astype(jnp.float32)
+    by_one = jnp.concatenate([mine[1][:half], mine[1][half:] + far_high], axis=0)
+    by_two = jnp.concatenate([mine[2][:half] + far_low, mine[2][half:]], axis=0)
+    from_one = to_neighbour(by_one.astype(low), 1).astype(jnp.float32)
+    from_two = to_neighbour(by_two.astype(low), 2).astype(jnp.float32)
+    return mine[0] + from_one + from_two
+
+
+def reorder(values, order):
+    rows, width = values.shape
+    block = width // 8
+
+    def body(order_ref, in_ref, out_ref):
+        out_ref[...] = in_ref[...]
+
+    return pl.pallas_call(
+        body,
+        grid_spec=pltpu.PrefetchScalarGridSpec(
+            num_scalar_prefetch=1,
+            grid=(8,),
+            in_specs=[pl.BlockSpec((rows, block), lambda j, order_ref: (0, order_ref[j]))],
+            out_specs=pl.BlockSpec((rows, block), lambda j, order_ref: (0, j)),
+        ),
+        out_shape=jax.ShapeDtypeStruct(values.shape, values.dtype),
+        name="reorder",
+    )(order, values)
+
+
+def turned(values, cosines, sines):
+    return values * cosines + pltpu.roll(values, values.shape[-1] // 2, axis=1) * sines
+
+
+def prepare(raw, inv, gains, cosines, sines, heads, head_dim, seqs):
+    rows = raw.shape[0]
+    length = rows // seqs
+
+    def body(raw_ref, inv_ref, gain_ref, cos_ref, sin_ref, out_ref):
+        kind = pl.program_id(0)
+
+        @pl.when(kind < 2)
+        def _():
+            normed = raw_ref[...] * inv_ref[0] * gain_ref[...]
+            out_ref[0, 0] = (
+                turned(normed, cos_ref[...], sin_ref[...])
+                .astype(jnp.bfloat16)
+                .reshape(seqs, length, head_dim)
+            )
+
+        @pl.when(kind == 2)
+        def _():
+            out_ref[0, 0] = raw_ref[...].astype(jnp.bfloat16).reshape(seqs, length, head_dim)
+
+    return pl.pallas_call(
+        body,
+        grid=(3, heads),
+        in_specs=[
+            pl.BlockSpec((rows, head_dim), lambda t, h: (0, t * heads + h)),
+            pl.BlockSpec((1, rows, 1), lambda t, h: (jnp.minimum(t, 1), 0, 0)),
+            pl.BlockSpec((1, head_dim), lambda t, h: (0, jnp.minimum(t * heads + h, 2 * heads - 1))),
+            pl.BlockSpec((rows, head_dim), lambda t, h: (0, 0)),
+            pl.BlockSpec((rows, head_dim), lambda t, h: (0, 0)),
+        ],
+        out_specs=pl.BlockSpec((1, 1, seqs, length, head_dim), lambda t, h: (h, t, 0, 0, 0)),
+        out_shape=jax.ShapeDtypeStruct((heads, 3, seqs, length, head_dim), jnp.bfloat16),
+        name="prepare",
+    )(raw, inv, gains, cosines, sines)
+
+
+def scores_of(left, right):
+    return lax.dot_general(
+        left, right, (((1,), (1,)), ((), ())), preferred_element_type=jnp.float32
+    )
+
+
+def causal(scores, first):
+    rows = lax.broadcasted_iota(jnp.int32, scores.shape, 0) + first
+    columns = lax.broadcasted_iota(jnp.int32, scores.shape, 1)
+    return columns <= rows
+
+
+def attend(parts):
+    blocks, _, seqs, length, head_dim = parts.shape
+    score_scale = head_dim ** (-0.5)
+
+    def body(parts_ref, out_ref, log_ref):
+        for i in range(blocks):
+            span = (i + 1) * length
+            keys = parts_ref[: i + 1, 1, 0].reshape(span, head_dim)
+            values = parts_ref[: i + 1, 2, 0].reshape(span, head_dim)
+            scores = scores_of(parts_ref[i, 0, 0], keys) * score_scale
+            scores = jnp.where(causal(scores, i * length), scores, MASKED)
+            top = jnp.max(scores, axis=-1, keepdims=True)
+            weights = jnp.exp(scores - top)
+            total = jnp.sum(weights, axis=-1, keepdims=True)
+            probs = (weights * (1.0 / total)).astype(jnp.bfloat16)
+            out_ref[i, 0] = jnp.dot(probs, values, preferred_element_type=jnp.float32).astype(
+                jnp.bfloat16
+            )
+            log_ref[i, 0] = top + jnp.log(total)
+
+    return pl.pallas_call(
+        body,
+        grid=(seqs,),
+        in_specs=[pl.BlockSpec((blocks, 3, 1, length, head_dim), lambda m: (0, 0, m, 0, 0))],
+        out_specs=[
+            pl.BlockSpec((blocks, 1, length, head_dim), lambda m: (0, m, 0, 0)),
+            pl.BlockSpec((blocks, 1, length, 1), lambda m: (0, m, 0, 0)),
+        ],
+        out_shape=[
+            jax.ShapeDtypeStruct((blocks, seqs, length, head_dim), jnp.bfloat16),
+            jax.ShapeDtypeStruct((blocks, seqs, length, 1), jnp.float32),
+        ],
+        compiler_params=pltpu.CompilerParams(vmem_limit_bytes=VMEM_LIMIT),
+        name="attend",
+    )(parts)
+
+
+def attend_back(parts, grad_context, log_total):
+    blocks, _, seqs, length, head_dim = parts.shape
+    score_scale = head_dim ** (-0.5)
+
+    def body(parts_ref, grad_ref, log_ref, out_ref, keys_sum, values_sum):
+        keys_sum[...] = jnp.zeros_like(keys_sum)
+        values_sum[...] = jnp.zeros_like(values_sum)
+        for i in range(blocks):
+            span = (i + 1) * length
+            queries = parts_ref[i, 0, 0]
+            keys = parts_ref[: i + 1, 1, 0].reshape(span, head_dim)
+            values = parts_ref[: i + 1, 2, 0].reshape(span, head_dim)
+            grads = grad_ref[i, 0]
+            scores = scores_of(queries, keys) * score_scale
+            probs = jnp.where(
+                causal(scores, i * length), jnp.exp(scores - log_ref[i, 0]), 0.0
+            )
+            grad_probs = scores_of(grads, values)
+            delta = jnp.sum(probs * grad_probs, axis=-1, keepdims=True)
+            grad_scores = (probs * (grad_probs - delta)).astype(jnp.bfloat16)
+            out_ref[i, 0, 0] = (
+                jnp.dot(grad_scores, keys, preferred_element_type=jnp.float32) * score_scale
+            ).astype(jnp.bfloat16)
+            over_rows = (((0,), (0,)), ((), ()))
+            keys_sum[:span] += lax.dot_general(
+                grad_scores, queries, over_rows, preferred_element_type=jnp.float32
+            )
+            values_sum[:span] += lax.dot_general(
+                probs.astype(jnp.bfloat16), grads, over_rows, preferred_element_type=jnp.float32
+            )
+        out_ref[:, 1, 0] = (
+            (keys_sum[...] * score_scale).astype(jnp.bfloat16).reshape(blocks, length, head_dim)
+        )
+        out_ref[:, 2, 0] = values_sum[...].astype(jnp.bfloat16).reshape(blocks, length, head_dim)
+
+    whole = pl.BlockSpec((blocks, 3, 1, length, head_dim), lambda m: (0, 0, m, 0, 0))
+    return pl.pallas_call(
+        body,
+        grid=(seqs,),
+        in_specs=[
+            whole,
+            pl.BlockSpec((blocks, 1, length, head_dim), lambda m: (0, m, 0, 0)),
+            pl.BlockSpec((blocks, 1, length, 1), lambda m: (0, m, 0, 0)),
+        ],
+        out_specs=whole,
+        out_shape=jax.ShapeDtypeStruct(parts.shape, jnp.bfloat16),
+        scratch_shapes=[
+            pltpu.VMEM((blocks * length, head_dim), jnp.float32),
+            pltpu.VMEM((blocks * length, head_dim), jnp.float32),
+        ],
+        compiler_params=pltpu.CompilerParams(vmem_limit_bytes=VMEM_LIMIT),
+        name="attend_back",
+    )(parts, grad_context, log_total)
+
+
+def unprepare(grads, raw, inv, gains, cosines, sines, heads, head_dim):
+    rows = raw.shape[0]
+
+    def body(grad_ref, raw_ref, inv_ref, gain_ref, cos_ref, sin_ref, scaled_ref, dot_ref, sum_ref):
+        turned_back = turned(
+            grad_ref[0, 0].reshape(rows, head_dim).astype(jnp.float32), cos_ref[...], -sin_ref[...]
+        )
+        unit = raw_ref[...] * inv_ref[0]
+        along = turned_back * unit
+        sum_ref[...] = jnp.sum(along, axis=0, keepdims=True)
+        scaled_ref[...] = turned_back * gain_ref[...]
+        part = jnp.sum(along * gain_ref[...], axis=-1, keepdims=True)
+
+        @pl.when(pl.program_id(1) == 0)
+        def _():
+            dot_ref[0] = part
+
+        @pl.when(pl.program_id(1) > 0)
+        def _():
+            dot_ref[0] += part
+
+    return pl.pallas_call(
+        body,
+        grid=(2, heads),
+        in_specs=[
+            pl.BlockSpec((1, 1) + grads.shape[2:], lambda t, h: (h, t, 0, 0, 0)),
+            pl.BlockSpec((rows, head_dim), lambda t, h: (0, t * heads + h)),
+            pl.BlockSpec((1, rows, 1), lambda t, h: (t, 0, 0)),
+            pl.BlockSpec((1, head_dim), lambda t, h: (0, t * heads + h)),
+            pl.BlockSpec((rows, head_dim), lambda t, h: (0, 0)),
+            pl.BlockSpec((rows, head_dim), lambda t, h: (0, 0)),
+        ],
+        out_specs=[
+            pl.BlockSpec((rows, head_dim), lambda t, h: (0, t * heads + h)),
+            pl.BlockSpec((1, rows, 1), lambda t, h: (t, 0, 0)),
+            pl.BlockSpec((1, head_dim), lambda t, h: (0, t * heads + h)),
+        ],
+        out_shape=[
+            jax.ShapeDtypeStruct((rows, 2 * heads * head_dim), jnp.float32),
+            jax.ShapeDtypeStruct((2, rows, 1), jnp.float32),
+            jax.ShapeDtypeStruct((1, 2 * heads * head_dim), jnp.float32),
+        ],
+        name="unprepare",
+    )(grads, raw, inv, gains, cosines, sines)
+
+
+def raw_grads(grads, scaled, raw, inv, dots, heads, head_dim, d_model):
+    rows = raw.shape[0]
+
+    def body(grad_ref, scaled_ref, raw_ref, inv_ref, dot_ref, out_ref):
+        @pl.when(pl.program_id(0) < 2)
+        def _():
+            unit = raw_ref[...] * inv_ref[0]
+            out_ref[...] = (
+                inv_ref[0] * (scaled_ref[...] - unit * (dot_ref[0] * (1.0 / d_model)))
+            ).astype(jnp.bfloat16)
+
+        @pl.when(pl.program_id(0) == 2)
+        def _():
+            out_ref[...] = grad_ref[0, 0].reshape(rows, head_dim)
+
+    last = 2 * heads - 1
+    return pl.pallas_call(
+        body,
+        grid=(3, heads),
+        in_specs=[
+            pl.BlockSpec(
+                (1, 1) + grads.shape[2:], lambda t, h: (jnp.where(t == 2, h, 0), 2, 0, 0, 0)
+            ),
+            pl.BlockSpec((rows, head_dim), lambda t, h: (0, jnp.minimum(t * heads + h, last))),
+            pl.BlockSpec((rows, head_dim), lambda t, h: (0, jnp.minimum(t * heads + h, last))),
+            pl.BlockSpec((1, rows, 1), lambda t, h: (jnp.minimum(t, 1), 0, 0)),
+            pl.BlockSpec((1, rows, 1), lambda t, h: (jnp.minimum(t, 1), 0, 0)),
+        ],
+        out_specs=pl.BlockSpec((rows, head_dim), lambda t, h: (0, t * heads + h)),
+        out_shape=jax.ShapeDtypeStruct((rows, 3 * heads * head_dim), jnp.bfloat16),
+        name="raw_grads",
+    )(grads, scaled, raw, inv, dots)
+
+
+def contract(left, right, left_dim, right_dim):
+    return lax.dot_general(
+        left, right, (((left_dim,), (right_dim,)), ((), ())), preferred_element_type=jnp.float32
+    )
+
+
+def on_plane(
+    tokens,
+    w_query,
+    w_key,
+    w_value,
+    w_out,
+    w_gate,
+    w_up,
+    w_down,
+    q_gain,
+    k_gain,
+    attn_gain,
+    mlp_gain,
+    cotangent,
+):
+    low = jnp.bfloat16
+    seqs, length, d_model = tokens.shape
+    rows = seqs * length
+    tp = lax.axis_size("tp")
+    tp_rank = lax.axis_index("tp")
+    seq_rank = lax.axis_index("seq")
+    heads = q_gain.shape[0]
+    head_dim = q_gain.shape[1] * 8
+    head_span = heads * head_dim
+    own_length = length // tp
+    half = d_model // 2
+    order = (lax.axis_index("dp") * 4 + seq_rank) ^ jnp.arange(8, dtype=jnp.int32)
+
+    in_weights = gather_plane(jnp.concatenate([w_query, w_key, w_value], axis=1), 0)
+    gain_rows = jnp.concatenate([q_gain, k_gain, attn_gain, mlp_gain], axis=0)
+    all_gains = lax.all_gather(gain_rows.reshape(-1), ("dp", "seq"))
+    all_gains = (
+        jnp.transpose(all_gains.reshape((8,) + gain_rows.shape), (1, 0, 2))
+        .reshape(gain_rows.shape[0], head_dim)
+        .astype(jnp.float32)
+    )
+    qk_gain = all_gains[: 2 * heads].reshape(1, 2 * head_span)
+    feature_rows = d_model // head_dim
+
+    def features(first):
+        return jnp.take(
+            all_gains[first : first + feature_rows].reshape(8, d_model // 8), order, axis=0
+        ).reshape(d_model)
+
+    attn_gains = features(2 * heads)
+    mlp_gains = features(2 * heads + feature_rows)
+    rows_low = reorder(tokens.reshape(rows, d_model), order)
+    grad_out = (
+        reorder(cotangent.reshape(-1, d_model), order)
+        .astype(jnp.float32)
+        .reshape(seqs, own_length, d_model)
+    )
+    own_tokens = lax.dynamic_slice_in_dim(
+        rows_low.reshape(seqs, length, d_model), tp_rank * own_length, own_length, 1
+    ).astype(jnp.float32)
+
+    raw = contract(rows_low, in_weights, 1, 0)
+    squares = jnp.stack(
+        [
+            jnp.sum(jnp.square(raw[:, :head_span]), axis=-1),
+            jnp.sum(jnp.square(raw[:, head_span : 2 * head_span]), axis=-1),
+        ]
+    )
+    inv = lax.rsqrt(lax.psum(squares, "tp") / d_model + NORM_EPS)[..., None]
+    positions = seq_rank * length + jnp.arange(length, dtype=jnp.int32)
+    cosines, sines = rope_tables(positions, head_dim)
+    cosines = jnp.tile(jnp.concatenate([cosines[:, 0], cosines[:, 0]], axis=-1), (seqs, 1))
+    sines = jnp.tile(jnp.concatenate([-sines[:, 0], sines[:, 0]], axis=-1), (seqs, 1))
+    parts = prepare(raw, inv, qk_gain, cosines, sines, heads, head_dim, seqs)
+    parts = lax.all_to_all(parts, "seq", 0, 0, tiled=True)
+    context, log_total = attend(parts)
+    context = lax.all_to_all(context, "seq", 0, 0, tiled=True)
+    context_low = jnp.transpose(context, (1, 2, 0, 3)).reshape(rows, head_span)
+
+    out_weights = gather_plane(after(w_out, in_weights), 1)
+    gate_weights = gather_plane(after(w_gate, in_weights), 0)
+    up_weights = gather_plane(after(w_up, context), 0)
+    down_weights = gather_plane(after(w_down, context), 1)
+
+    def sum_rows(values):
+        return lax.psum_scatter(
+            values.astype(low).reshape(seqs, length, d_model),
+            "tp",
+            scatter_dimension=1,
+            tiled=True,
+        ).astype(jnp.float32)
+
+    def all_rows(values):
+        return lax.all_gather(values.astype(low), "tp", axis=1, tiled=True).reshape(rows, d_model)
+
+    attn_out = sum_rows(contract(context_low, out_weights, 1, 0))
+    attn_inv = lax.rsqrt(jnp.mean(attn_out * attn_out, axis=-1, keepdims=True) + NORM_EPS)
+    attn_unit = attn_out * attn_inv
+    hidden = own_tokens + attn_unit * attn_gains
+    hidden_all = all_rows(hidden)
+    gate = contract(hidden_all, gate_weights, 1, 0)
+    up = contract(hidden_all, up_weights, 1, 0)
+    gate_sig = jax.nn.sigmoid(gate)
+    mixed = (gate * gate_sig * up).astype(low)
+    mlp_out = sum_rows(contract(mixed, down_weights, 1, 0))
+    mlp_inv = lax.rsqrt(jnp.mean(mlp_out * mlp_out, axis=-1, keepdims=True) + NORM_EPS)
+    mlp_unit = mlp_out * mlp_inv
+    outputs = (hidden + mlp_unit * mlp_gains).astype(low)
+
+    grad_mgain = jnp.sum(grad_out * mlp_unit, axis=(0, 1))
+    mlp_scaled = grad_out * mlp_gains
+    grad_mlp = norm_back(
+        mlp_unit, mlp_scaled, mlp_inv, jnp.sum(mlp_scaled * mlp_unit, axis=-1), d_model
+    )
+    grad_mlp_all = all_rows(grad_mlp)
+    grad_mixed = contract(grad_mlp_all, down_weights, 1, 1)
+    grad_gate = (grad_mixed * up * gate_sig * (1.0 + gate * (1.0 - gate_sig))).astype(low)
+    grad_up = (grad_mixed * gate * gate_sig).astype(low)
+    hidden_part = contract(grad_gate, gate_weights, 1, 1) + contract(grad_up, up_weights, 1, 1)
+    hidden_sum = sum_rows(hidden_part)
+
+    def weight_grad(left, right, axis):
+        if axis == 0:
+            sent = contract(left[:, half:], right, 0, 0)
+            kept = contract(left[:, :half], right, 0, 0)
+        else:
+            sent = contract(left, right[:, half:], 0, 0)
+            kept = contract(left, right[:, :half], 0, 0)
+        return scatter_plane(kept.astype(low), sent.astype(low), axis)
+
+    sum_down = weight_grad(mixed, grad_mlp_all, 1)
+    sum_gate = weight_grad(hidden_all, grad_gate, 0)
+    sum_up = weight_grad(hidden_all, grad_up, 0)
+
+    grad_hidden = grad_out + hidden_sum
+    grad_again = jnp.sum(grad_hidden * attn_unit, axis=(0, 1))
+    attn_scaled = grad_hidden * attn_gains
+    grad_attn = norm_back(
+        attn_unit, attn_scaled, attn_inv, jnp.sum(attn_scaled * attn_unit, axis=-1), d_model
+    )
+    grad_attn_all = all_rows(grad_attn)
+    grad_context = contract(grad_attn_all, out_weights, 1, 1).astype(low)
+    grad_context = jnp.transpose(
+        grad_context.reshape(seqs, length, heads, head_dim), (2, 0, 1, 3)
+    )
+    grad_context = lax.all_to_all(grad_context, "seq", 0, 0, tiled=True)
+    sum_out = weight_grad(context_low, grad_attn_all, 1)
+    part_grads = attend_back(parts, grad_context, log_total)
+    part_grads = lax.all_to_all(part_grads, "seq", 0, 0, tiled=True)
+    scaled, dots, qk_sums = unprepare(
+        part_grads, raw, inv, qk_gain, cosines, sines, heads, head_dim
+    )
+    dots = lax.psum(dots.reshape(2, rows), "tp")[..., None]
+    grad_raw = raw_grads(part_grads, scaled, raw, inv, dots, heads, head_dim, d_model)
+    token_sum = sum_rows(contract(grad_raw, in_weights, 1, 1))
+    sum_in = weight_grad(rows_low, grad_raw, 0)
+    grad_tokens = grad_hidden + token_sum
+
+    def by_owner(values):
+        values = jnp.take(values.reshape(8, d_model // 8), order, axis=0)
+        return jnp.transpose(values.reshape(tp, heads, 8, -1), (2, 0, 1, 3))
+
+    head_sums = jnp.transpose(qk_sums.reshape(2, heads, 8, -1), (2, 0, 1, 3))[:, None]
+    is_own = (jnp.arange(tp) == tp_rank)[None, :, None, None, None]
+    payload = jnp.concatenate(
+        [
+            jnp.where(is_own, head_sums, 0.0),
+            by_owner(grad_again)[:, :, None],
+            by_owner(grad_mgain)[:, :, None],
+        ],
+        axis=2,
+    ).reshape(8 * tp, -1)
+    gain_sums = jnp.sum(
+        lax.all_to_all(payload, ("dp", "seq", "tp"), 0, 0, tiled=True), axis=0
+    ).reshape(4, heads, -1)
+
+    def in_place(values):
+        return reorder(values.reshape(-1, d_model), order).reshape(seqs, own_length, d_model)
+
+    return (
+        in_place(outputs),
+        in_place(grad_tokens),
+        sum_in[:, :head_span],
+        sum_in[:, head_span : 2 * head_span],
+        sum_in[:, 2 * head_span :],
+        sum_out,
+        sum_gate,
+        sum_up,
+        sum_down,
+        gain_sums[0],
+        gain_sums[1],
+        gain_sums[2],
+        gain_sums[3],
+    )
+
+
 def solution(mesh):
+    by_plane = mesh.shape["dp"] == 2 and mesh.shape["seq"] == 4
     return jax.shard_map(
-        on_device,
+        on_plane if by_plane else on_any_mesh,
         mesh=mesh,
         in_specs=(
             P("dp", "seq", None),

time: 1510 us -> 831 us (0.55)
  waiting for transfers between devices: 1080 us -> 263 us
  starting transfers between devices: 2.39 us -> 69.3 us
  other arithmetic: 51.2 us -> 118 us
  Pallas kernels: 0 us -> 60.5 us
  blocking collectives: 114 us -> 62.9 us
  local copies, waits for them, and re-layouts: 65.4 us -> 107 us
  matrix products: 160 us -> 124 us
    reduce_scatter x12 -> x4, waiting for transfers between devices: 600 us -> 43.9 us  [sum_rows(): lax.psum_scatter(values.astype(low).reshape(seqs, length, d_model), 'tp',...]
    all_gather x12 -> x3, waiting for transfers between devices: 379 us -> 65.7 us  [all_rows(): lax.all_gather(values.astype(low), 'tp', axis=1, tiled=True)]
    unnamed x32 -> x7, waiting for transfers between devices: 105 us -> 0.12 us
    ppermute x0 -> x50, waiting for transfers between devices: none -> 95.5 us  [the longest x40 95.5 us: to_neighbour(): return lax.ppermute(values, 'seq', [(i, i ^ flip) for i in range(4)])]
    pallas_call x0 -> x9, Pallas kernels: none -> 60.5 us  [the longest x4 23.1 us: reorder(): pl.pallas_call(body, grid_spec=pltpu.PrefetchScalarGridSpec(num_scalar_pr...]
    all_to_all x0 -> x5, waiting for transfers between devices: none -> 57.4 us  [the longest x1 31.7 us: on_plane(): grad_context = lax.all_to_all(grad_context, 'seq', 0, 0, tiled=True)]
    all_gather x4 -> x1, blocking collectives: 73.9 us -> 23 us  [on_plane(): all_gains = lax.all_gather(gain_rows.reshape(-1), ('dp', 'seq'))]
    ppermute x0 -> x50, starting transfers between devices: none -> 50.6 us  [the longest x40 49.5 us: to_neighbour(): return lax.ppermute(values, 'seq', [(i, i ^ flip) for i in range(4)])]
  transfers between devices with their start and end apart: 28 -> 62, of which waited for: 27 -> 19; matrix products, arithmetic and copies ran while one was open for 11% -> 32% of each run, Pallas kernels for 0% -> 7%
where the time goes in v1:
time: 831 us; the launch traced here: 820 us
  waiting for transfers between devices  263 us (32%)
  matrix products  124 us (15%)
  other arithmetic  118 us (14%)
  local copies, waits for them, and re-layouts  107 us (13%)
  starting transfers between devices  69.3 us (8%)
  blocking collectives  62.9 us (8%)
  Pallas kernels  60.5 us (7%)
  between operations  15.4 us (2%)
    dot_general x20, matrix products, contract(): lax.dot_general(left, right, (((left_dim,), (right_dim,)), ((), ())), pre...  124 us
    ppermute x40, waiting for transfers between devices, to_neighbour(): return lax.ppermute(values, 'seq', [(i, i ^ flip) for i in range(4)])  95.5 us
    all_gather x3, waiting for transfers between devices, all_rows(): lax.all_gather(values.astype(low), 'tp', axis=1, tiled=True)  65.7 us
    ppermute x40, starting transfers between devices, to_neighbour(): return lax.ppermute(values, 'seq', [(i, i ^ flip) for i in range(4)])  49.5 us
    unnamed x149, local copies, waits for them, and re-layouts  47.1 us
    reduce_scatter x4, waiting for transfers between devices, sum_rows(): lax.psum_scatter(values.astype(low).reshape(seqs, length, d_model), 'tp',...  43.9 us
    all_to_all x1, waiting for transfers between devices, on_plane(): grad_context = lax.all_to_all(grad_context, 'seq', 0, 0, tiled=True)  31.7 us
    psum x1, blocking collectives, on_plane(): dots = lax.psum(dots.reshape(2, rows), 'tp')[..., None]  27.9 us
  transfers between devices with their start and end apart: 62, of which 19 were waited for; matrix products, arithmetic and copies ran while one was open for 32% of the time, Pallas kernels for 7%

profile of v1, /device:TPU:0, one launch (start us, length us, event | category | flops | bytes accessed | tf_op | source)
XLA Modules:
  0.0 820.2 jit_solution(8253312456934204468)
XLA Ops:
  16.8 16.0 %collective-permute-done.1 = bf16[256,1536]{1,0:T(8,128)(2,1)S(1)} collective-permute-done((bf16[256,1536]{1,0:T(8,128)(2,1)S(1)}, bf16[256,1536]{1,0:T(8,128)(2,1)S(1)}, u32[]{:S(2)}, u32[]{:S(2)}) %collective-permute-start.1) | collective-permute-done | bytes 786464 | tf_op jit(solution)/shard_map/ppermute | solution.py:406
  48.0 23.0 %all-gather = bf16[8,1,640]{2,1,0:T(2,128)(2,1)S(1)} all-gather(bf16[1,1,640]{2,1,0:T(2,128)(2,1)S(1)} %reshape.282), channel_id=1, replica_groups=mesh['dp'=2,'seq'=4,'tp'=4] {'dp','seq'}, dimensions={0}, use_global_device_ids=true | all-gather | bytes 11520 | tf_op jit(solution)/shard_map/all_gather | solution.py:724
  72.5 6.4 reorder.4
  89.7 12.0 %psum.14 = f32[2,512]{1,0:T(2,128)S(1)} all-reduce(f32[2,512]{1,0:T(2,128)S(1)} %pad_maximum_fusion.14), channel_id=1, replica_groups=mesh['dp'=2,'seq'=4,'tp'=4] {'tp'}, use_global_device_ids=true, to_apply=%region_2.3 | all-reduce | flops 1024 | bytes 8192 | tf_op jit(solution)/shard_map/psum | solution.py:757
  105.1 8.6 %prepare.1 = bf16[4,3,2,256,128]{4,3,2,1,0:T(8,128)(2,1)} custom-call(f32[512,1536]{1,0:T(8,128)} %copy-done, f32[2,512,1]{2,1,0:T(8,128)} %copy.57.inv_ref, f32[1,1024]{1,0:T(1,128)} %reshape.217.gain_ref, f32[512,128]{1,0:T(8,128)} %bitcast.88, f32[512,128]{1,0:T(8,128)} %bitcast.90), custom_call_target="tpu_custom_call" | custom-call | tf_op jit(solution)/shard_map/prepare/pallas_call | solution.py:488
  121.7 15.0 %collective-permute-done.7 = bf16[256,256]{1,0:T(8,128)(2,1)S(1)} collective-permute-done((bf16[256,256]{1,0:T(8,128)(2,1)S(1)}, bf16[256,256]{1,0:T(8,128)(2,1)S(1)}, u32[]{:S(2)}, u32[]{:S(2)}) %collective-permute-start.7) | collective-permute-done | bytes 131104 | tf_op jit(solution)/shard_map/ppermute | solution.py:406
  158.5 13.0 %all-to-all-done.1 = bf16[4,2,256,128]{3,2,1,0:T(8,128)(2,1)S(1)} async-done(((bf16[4,2,256,128]{3,2,1,0:T(8,128)(2,1)}), bf16[4,2,256,128]{3,2,1,0:T(8,128)(2,1)S(1)}, u32[]{:S(2)}, u32[]{:S(2)}) %all-to-all-start.1) | async-done | bytes 524320 | tf_op jit(solution)/shard_map/all_to_all | solution.py:765
  201.6 19.8 %collective-permute-done.21 = bf16[2048,256]{1,0:T(8,128)(2,1)S(1)} collective-permute-done((bf16[2048,256]{1,0:T(8,128)(2,1)S(1)}, bf16[2048,256]{1,0:T(8,128)(2,1)S(1)}, u32[]{:S(2)}, u32[]{:S(2)}) %collective-permute-start.21) | collective-permute-done | bytes 1048608 | tf_op jit(solution)/shard_map/ppermute | solution.py:406
  223.6 20.3 %collective-permute-done.16 = bf16[256,2048]{1,0:T(8,128)(2,1)S(1)} collective-permute-done((bf16[256,2048]{1,0:T(8,128)(2,1)S(1)}, bf16[256,2048]{1,0:T(8,128)(2,1)S(1)}, u32[]{:S(2)}, u32[]{:S(2)}) %collective-permute-start.16) | collective-permute-done | bytes 1048608 | tf_op jit(solution)/shard_map/ppermute | solution.py:406
  255.1 15.2 %maximum_maximum_fusion = bf16[2048,1024]{1,0:T(8,128)(2,1)} fusion(bf16[1024,256]{1,0:T(8,128)(2,1)S(1)} %collective-permute-done.23, bf16[1024,256]{1,0:T(8,128)(2,1)S(1)} %collective-permute-done.22, bf16[2048,256]{1,0:T(8,128)(2,1)S(1)} %collective-permute-done.21, bf16[2048,256]{1,0:T(8,128)(2,1)S(1)} %collective-permute-done.20, ...), kind=kLoop, calls=%fused_computation.4 | loop fusion | flops 20971520 | bytes 8388608 | tf_op jit(solution)/shard_map/concatenate | solution.py:424
  300.3 20.7 %all-gather.5.cloned.1.call-done = bf16[2,256,2048]{2,1,0:T(8,128)(2,1)} async-done(((bf16[2,64,2048]{2,1,0:T(8,128)(2,1)}), bf16[2,256,2048]{2,1,0:T(8,128)(2,1)}) %all-gather.5.cloned.1.call-update) | async-done | bytes 2097168 | tf_op jit(solution)/shard_map/all_gather | solution.py:782
  321.0 8.5 %fusion.78 = f32[512,2048]{1,0:T(8,128)S(1)} fusion(bf16[512,2048]{1,0:T(8,128)(2,1)} %bitcast.124, bf16[2048,2048]{1,0:T(8,128)(2,1)} %constant_dynamic-update-slice_fusion.28), kind=kOutput, calls=%fused_computation.241 | convolution fusion | flops 4294967296 | bytes 14680064 | tf_op jit(solution)/shard_map/dot_general | solution.py:689
  329.5 11.6 %multiply_convert_fusion.2 = (bf16[512,2048]{1,0:T(8,128)(2,1)S(1)}, f32[512,2048]{1,0:T(8,128)}) fusion(f32[512,2048]{1,0:T(8,128)S(1)} %fusion.78, bf16[512,2048]{1,0:T(8,128)(2,1)S(1)} %bitcast.126, bf16[2048,2048]{1,0:T(8,128)(2,1)} %constant_dynamic-update-slice_fusion.39), kind=kOutput, calls=%fused_computation.11 | convolution fusion | flops 4301258752 | bytes 20971520 | tf_op jit(solution)/shard_map/dot_general | solution.py:689
  341.2 9.8 %convolution_convert_fusion.6 = bf16[512,2048]{1,0:T(8,128)(2,1)} fusion(bf16[512,2048]{1,0:T(8,128)(2,1)S(1)} %get-tuple-element.120, bf16[2048,2048]{1,0:T(8,128)(2,1)} %constant_dynamic-update-slice_fusion.45), kind=kOutput, calls=%fused_computation.20 | convolution fusion | flops 4296015872 | bytes 12582912 | tf_op jit(solution)/shard_map/dot_general | solution.py:689
  356.5 37.3 %reduce-scatter.7.cloned.1.call-done = bf16[2,64,2048]{2,1,0:T(8,128)(2,1)} async-done(((bf16[2,256,2048]{2,1,0:T(8,128)(2,1)}), bf16[2,64,2048]{2,1,0:T(8,128)(2,1)}) %reduce-scatter.7.cloned.1.call-update) | async-done | bytes 524304 | tf_op jit(solution)/shard_map/reduce_scatter | solution.py:774
  399.7 45.0 %all-gather.7.cloned.1.call-done = bf16[2,256,2048]{2,1,0:T(8,128)(2,1)} async-done(((bf16[2,64,2048]{2,1,0:T(8,128)(2,1)}), bf16[2,256,2048]{2,1,0:T(8,128)(2,1)}) %all-gather.7.cloned.1.call-update) | async-done | bytes 2097168 | tf_op jit(solution)/shard_map/all_gather | solution.py:782
  444.7 11.9 %multiply_convert_fusion.1 = (bf16[512,2048]{1,0:T(8,128)(2,1)S(1)}, bf16[512,2048]{1,0:T(8,128)(2,1)S(1)}) fusion(f32[512,2048]{1,0:T(8,128)} %copy-done.56, f32[512,2048]{1,0:T(8,128)} %get-tuple-element.121, bf16[512,2048]{1,0:T(8,128)(2,1)} %bitcast.130, bf16[2048,2048]{1,0:T(8,128)(2,1)} %constant_dynamic-update-slice_fusion.45), kind=kOutput, calls=%fused_computation.10 | convolution fusion | flops 4308598784 | bytes 23068672 | tf_op jit(solution)/shard_map/dot_general | solution.py:689
  456.6 8.5 %fusion.79 = f32[512,2048]{1,0:T(8,128)S(1)} fusion(bf16[512,2048]{1,0:T(8,128)(2,1)S(1)} %get-tuple-element.51, bf16[2048,2048]{1,0:T(8,128)(2,1)} %constant_dynamic-update-slice_fusion.39), kind=kOutput, calls=%fused_computation.242 | convolution fusion | flops 4294967296 | bytes 14680064 | tf_op jit(solution)/shard_map/dot_general | solution.py:689
  465.1 9.2 %add_convert_fusion = bf16[512,2048]{1,0:T(8,128)(2,1)} fusion(f32[512,2048]{1,0:T(8,128)S(1)} %fusion.79, bf16[512,2048]{1,0:T(8,128)(2,1)S(1)} %get-tuple-element.50, bf16[2048,2048]{1,0:T(8,128)(2,1)} %constant_dynamic-update-slice_fusion.28), kind=kOutput, calls=%fused_computation.8 | convolution fusion | flops 4297064448 | bytes 16777216 | tf_op jit(solution)/shard_map/dot_general | solution.py:689
  474.5 6.2 convolution_convert_fusion
  481.3 6.5 convolution_convert_fusion.1
  504.2 6.2 convert_convert_fusion.2
  510.4 6.7 reduce-scatter.9.cloned.1.call-done
  526.6 9.1 %slice_add_fusion.2 = (f32[2048,256]{1,0:T(8,128)}, f32[2048,256]{1,0:T(8,128)}, bf16[2048,256]{1,0:T(8,128)(2,1)S(1)}) fusion(f32[2048,1024]{1,0:T(8,128)S(1)} %convert_element_type.265, f32[2048,1024]{1,0:T(8,128)} %convert_convert_fusion), kind=kLoop, calls=%fused_computation.25 | loop fusion | flops 2097152 | bytes 17825792 | tf_op jit(solution)/shard_map/add | solution.py:433
  543.2 8.6 %slice_add_fusion.6 = (f32[256,2048]{1,0:T(8,128)}, f32[256,2048]{1,0:T(8,128)}, bf16[256,2048]{1,0:T(8,128)(2,1)}) fusion(f32[1024,2048]{1,0:T(8,128)S(1)} %convert_element_type.257, f32[1024,2048]{1,0:T(8,128)} %convert_convert_fusion.1), kind=kLoop, calls=%fused_computation.32 | loop fusion | flops 2097152 | bytes 17825792 | tf_op jit(solution)/shard_map/add | solution.py:433
  617.9 31.7 %all-to-all-done.2.grad_ref = bf16[4,2,256,128]{3,2,1,0:T(8,128)(2,1)S(1)} async-done(((bf16[4,2,256,128]{3,2,1,0:T(8,128)(2,1)}), bf16[4,2,256,128]{3,2,1,0:T(8,128)(2,1)S(1)}, u32[]{:S(2)}, u32[]{:S(2)}) %all-to-all-start.2) | async-done | bytes 524320 | tf_op jit(solution)/shard_map/all_to_all | solution.py:834
  649.6 6.9 attend_back.1
  673.4 12.7 %all-to-all-done.3.grad_ref = bf16[4,3,2,256,128]{4,3,2,1,0:T(8,128)(2,1)S(1)} async-done(((bf16[4,3,2,256,128]{4,3,2,1,0:T(8,128)(2,1)}), bf16[4,3,2,256,128]{4,3,2,1,0:T(8,128)(2,1)S(1)}, u32[]{:S(2)}, u32[]{:S(2)}) %all-to-all-start.3) | async-done | bytes 1572896 | tf_op jit(solution)/shard_map/all_to_all | solution.py:837
  687.2 7.4 unprepare.1
  694.6 27.9 %psum.15.dot_ref = f32[2,512,1]{2,1,0:T(8,128)} all-reduce(f32[2,512,1]{2,1,0:T(8,128)} %get-tuple-element.30), channel_id=1, replica_groups=mesh['dp'=2,'seq'=4,'tp'=4] {'tp'}, use_global_device_ids=true, to_apply=%region_10.12 | all-reduce | flops 1024 | bytes 8192 | tf_op jit(solution)/shard_map/psum | solution.py:841
  722.5 9.1 %raw_grads.1 = bf16[512,1536]{1,0:T(8,128)(2,1)} custom-call(bf16[4,3,2,256,128]{4,3,2,1,0:T(8,128)(2,1)} %copy-done.7, f32[512,1024]{1,0:T(8,128)} %get-tuple-element.29.scaled_ref, f32[512,1536]{1,0:T(8,128)} %copy-done, f32[2,512,1]{2,1,0:T(8,128)} %copy.57.inv_ref, f32[2,512,1]{2,1,0:T(8,128)} %psum.15.dot_ref), custom_call_target="tpu_custom_call" | custom-call | tf_op jit(solution)/shard_map/raw_grads/pallas_call | solution.py:670
  800.5 5.9 reorder.7
  (419 shorter events, 348.2 us)
Async XLA Ops:
  47.9 32.4 %collective-permute-start.4 = (bf16[1024,1536]{1,0:T(8,128)(2,1)}, bf16[1024,1536]{1,0:T(8,128)(2,1)S(1)}, u32[]{:S(2)}, u32[]{:S(2)}) collective-permute-start(bf16[1024,1536]{1,0:T(8,128)(2,1)} %get-tuple-element.92), channel_id=1, source_target_pairs={{0,16},{16,0},{1,17},{17,1},{2,18},{18,2},{3,19},{19,3},{4,20},{20... | collective-permute-start | bytes 9437192 | tf_op jit(solution)/shard_map/ppermute | solution.py:410
  82.1 35.1 %collective-permute-start.6 = (bf16[512,256]{1,0:T(8,128)(2,1)}, bf16[512,256]{1,0:T(8,128)(2,1)S(1)}, u32[]{:S(2)}, u32[]{:S(2)}) collective-permute-start(bf16[512,256]{1,0:T(8,128)(2,1)} %param.19), channel_id=1, source_target_pairs={{0,8},{4,12},{8,0},{12,4},{1,9},{5,13},{9,1},{13,5},{2,10},{6,14},... | collective-permute-start | bytes 786440 | tf_op jit(solution)/shard_map/ppermute | solution.py:406
  83.7 35.6 %collective-permute-start.5 = (bf16[512,256]{1,0:T(8,128)(2,1)}, bf16[512,256]{1,0:T(8,128)(2,1)}, u32[]{:S(2)}, u32[]{:S(2)}) collective-permute-start(bf16[512,256]{1,0:T(8,128)(2,1)} %param.19), channel_id=1, source_target_pairs={{0,4},{4,0},{8,12},{12,8},{1,5},{5,1},{9,13},{13,9},{2,6},{6,2},{1... | collective-permute-start | bytes 786440 | tf_op jit(solution)/shard_map/ppermute | solution.py:406
  139.0 44.0 %collective-permute-start.10 = (bf16[256,2048]{1,0:T(8,128)(2,1)}, bf16[256,2048]{1,0:T(8,128)(2,1)}, u32[]{:S(2)}, u32[]{:S(2)}) collective-permute-start(bf16[256,2048]{1,0:T(8,128)(2,1)} %param.20), channel_id=1, source_target_pairs={{0,4},{4,0},{8,12},{12,8},{1,5},{5,1},{9,13},{13,9},{2,6},{6,2},{1... | collective-permute-start | bytes 3145736 | tf_op jit(solution)/shard_map/ppermute | solution.py:406
  140.4 38.3 %collective-permute-start.11 = (bf16[256,2048]{1,0:T(8,128)(2,1)}, bf16[256,2048]{1,0:T(8,128)(2,1)}, u32[]{:S(2)}, u32[]{:S(2)}) collective-permute-start(bf16[256,2048]{1,0:T(8,128)(2,1)} %param.20), channel_id=1, source_target_pairs={{0,8},{4,12},{8,0},{12,4},{1,9},{5,13},{9,1},{13,5},{2,10},{6,14},... | collective-permute-start | bytes 3145736 | tf_op jit(solution)/shard_map/ppermute | solution.py:406
  153.2 121.1 %reduce-scatter.5.cloned.1.call-start = ((), (), s32[]{:S(2)}) async-start(), calls=%async_computation.9 | async-start | bytes 2621440 | tf_op jit(solution)/shard_map/reduce_scatter | solution.py:774
  178.2 142.8 %all-gather.5.cloned.1.call-start = ((), (), s32[]{:S(2)}) async-start(), calls=%async_computation.10 | async-start | bytes 2621440 | tf_op jit(solution)/shard_map/all_gather | solution.py:782
  187.8 33.6 %collective-permute-start.21 = (bf16[2048,256]{1,0:T(8,128)(2,1)S(1)}, bf16[2048,256]{1,0:T(8,128)(2,1)S(1)}, u32[]{:S(2)}, u32[]{:S(2)}) collective-permute-start(bf16[2048,256]{1,0:T(8,128)(2,1)S(1)} %copy-done.22), channel_id=1, source_target_pairs={{0,8},{4,12},{8,0},{12,4},{1,9},{5,13},{9,1},{13,5},{2,10},{6,14},... | collective-permute-start | bytes 3145736 | tf_op jit(solution)/shard_map/ppermute | solution.py:406
  188.5 34.3 %collective-permute-start.20 = (bf16[2048,256]{1,0:T(8,128)(2,1)S(1)}, bf16[2048,256]{1,0:T(8,128)(2,1)S(1)}, u32[]{:S(2)}, u32[]{:S(2)}) collective-permute-start(bf16[2048,256]{1,0:T(8,128)(2,1)S(1)} %copy-done.22), channel_id=1, source_target_pairs={{0,4},{4,0},{8,12},{12,8},{1,5},{5,1},{9,13},{13,9},{2,6},{6,2},{1... | collective-permute-start | bytes 3145736 | tf_op jit(solution)/shard_map/ppermute | solution.py:406
  189.8 55.5 %collective-permute-start.15 = (bf16[256,2048]{1,0:T(8,128)(2,1)S(1)}, bf16[256,2048]{1,0:T(8,128)(2,1)S(1)}, u32[]{:S(2)}, u32[]{:S(2)}) collective-permute-start(bf16[256,2048]{1,0:T(8,128)(2,1)S(1)} %copy-done.32), channel_id=1, source_target_pairs={{0,4},{4,0},{8,12},{12,8},{1,5},{5,1},{9,13},{13,9},{2,6},{6,2},{1... | collective-permute-start | bytes 3145736 | tf_op jit(solution)/shard_map/ppermute | solution.py:406
  194.7 49.2 %collective-permute-start.16 = (bf16[256,2048]{1,0:T(8,128)(2,1)S(1)}, bf16[256,2048]{1,0:T(8,128)(2,1)S(1)}, u32[]{:S(2)}, u32[]{:S(2)}) collective-permute-start(bf16[256,2048]{1,0:T(8,128)(2,1)S(1)} %copy-done.32), channel_id=1, source_target_pairs={{0,8},{4,12},{8,0},{12,4},{1,9},{5,13},{9,1},{13,5},{2,10},{6,14},... | collective-permute-start | bytes 3145736 | tf_op jit(solution)/shard_map/ppermute | solution.py:406
  199.8 86.1 %collective-permute-start.14 = (bf16[1024,2048]{1,0:T(8,128)(2,1)}, bf16[1024,2048]{1,0:T(8,128)(2,1)}, u32[]{:S(2)}, u32[]{:S(2)}) collective-permute-start(bf16[1024,2048]{1,0:T(8,128)(2,1)} %get-tuple-element.84), channel_id=1, source_target_pairs={{0,16},{16,0},{1,17},{17,1},{2,18},{18,2},{3,19},{19,3},{4,20},{20... | collective-permute-start | bytes 12582920 | tf_op jit(solution)/shard_map/ppermute | solution.py:410
  277.8 116.0 %reduce-scatter.7.cloned.1.call-start = ((), (), s32[]{:S(2)}) async-start(), calls=%async_computation.11 | async-start | bytes 2621440 | tf_op jit(solution)/shard_map/reduce_scatter | solution.py:774
  351.0 93.6 %all-gather.7.cloned.1.call-start = ((), (), s32[]{:S(2)}) async-start(), calls=%async_computation.12 | async-start | bytes 2621440 | tf_op jit(solution)/shard_map/all_gather | solution.py:782
  399.2 117.8 %reduce-scatter.9.cloned.1.call-start = ((), (), s32[]{:S(2)}) async-start(), calls=%async_computation.13 | async-start | bytes 2621440 | tf_op jit(solution)/shard_map/reduce_scatter | solution.py:774
  474.3 127.9 %all-gather.9.cloned.1.call-start = ((), (), s32[]{:S(2)}) async-start(), calls=%async_computation.14 | async-start | bytes 2621440 | tf_op jit(solution)/shard_map/all_gather | solution.py:782
  480.7 42.7 %collective-permute-start.45 = (bf16[2048,1024]{1,0:T(8,128)(2,1)}, bf16[2048,1024]{1,0:T(8,128)(2,1)}, u32[]{:S(2)}, u32[]{:S(2)}) collective-permute-start(bf16[2048,1024]{1,0:T(8,128)(2,1)} %convolution_convert_fusion), channel_id=1, source_target_pairs={{0,16},{16,0},{1,17},{17,1},{2,18},{18,2},{3,19},{19,3},{4,20},{20... | collective-permute-start | bytes 12582920 | tf_op jit(solution)/shard_map/ppermute | solution.py:410
  487.9 51.9 %collective-permute-start.40 = (bf16[1024,2048]{1,0:T(8,128)(2,1)}, bf16[1024,2048]{1,0:T(8,128)(2,1)}, u32[]{:S(2)}, u32[]{:S(2)}) collective-permute-start(bf16[1024,2048]{1,0:T(8,128)(2,1)} %convolution_convert_fusion.1), channel_id=1, source_target_pairs={{0,16},{16,0},{1,17},{17,1},{2,18},{18,2},{3,19},{19,3},{4,20},{20... | collective-permute-start | bytes 12582920 | tf_op jit(solution)/shard_map/ppermute | solution.py:410
  492.8 61.9 %collective-permute-start.35 = (bf16[1024,2048]{1,0:T(8,128)(2,1)}, bf16[1024,2048]{1,0:T(8,128)(2,1)}, u32[]{:S(2)}, u32[]{:S(2)}) collective-permute-start(bf16[1024,2048]{1,0:T(8,128)(2,1)} %convolution_convert_fusion.2), channel_id=1, source_target_pairs={{0,16},{16,0},{1,17},{17,1},{2,18},{18,2},{3,19},{19,3},{4,20},{20... | collective-permute-start | bytes 12582920 | tf_op jit(solution)/shard_map/ppermute | solution.py:410
  536.8 47.1 %collective-permute-start.46 = (bf16[1024,256]{1,0:T(8,128)(2,1)}, bf16[1024,256]{1,0:T(8,128)(2,1)}, u32[]{:S(2)}, u32[]{:S(2)}) collective-permute-start(bf16[1024,256]{1,0:T(8,128)(2,1)} %get-tuple-element.58), channel_id=1, source_target_pairs={{0,8},{4,12},{8,0},{12,4},{1,9},{5,13},{9,1},{13,5},{2,10},{6,14},... | collective-permute-start | bytes 1572872 | tf_op jit(solution)/shard_map/ppermute | solution.py:406
  538.3 50.9 %collective-permute-start.48 = (bf16[1024,256]{1,0:T(8,128)(2,1)}, bf16[1024,256]{1,0:T(8,128)(2,1)}, u32[]{:S(2)}, u32[]{:S(2)}) collective-permute-start(bf16[1024,256]{1,0:T(8,128)(2,1)} %get-tuple-element.59), channel_id=1, source_target_pairs={{0,4},{4,0},{8,12},{12,8},{1,5},{5,1},{9,13},{13,9},{2,6},{6,2},{1... | collective-permute-start | bytes 1572872 | tf_op jit(solution)/shard_map/ppermute | solution.py:406
  554.1 40.8 %collective-permute-start.43 = (bf16[128,2048]{1,0:T(8,128)(2,1)}, bf16[128,2048]{1,0:T(8,128)(2,1)}, u32[]{:S(2)}, u32[]{:S(2)}) collective-permute-start(bf16[128,2048]{1,0:T(8,128)(2,1)} %get-tuple-element.61), channel_id=1, source_target_pairs={{0,4},{4,0},{8,12},{12,8},{1,5},{5,1},{9,13},{13,9},{2,6},{6,2},{1... | collective-permute-start | bytes 1572872 | tf_op jit(solution)/shard_map/ppermute | solution.py:406
  589.1 71.0 %collective-permute-start.47 = (bf16[2048,256]{1,0:T(8,128)(2,1)}, bf16[2048,256]{1,0:T(8,128)(2,1)}, u32[]{:S(2)}, u32[]{:S(2)}) collective-permute-start(bf16[2048,256]{1,0:T(8,128)(2,1)} %pad_maximum_fusion.4), channel_id=1, source_target_pairs={{0,4},{4,0},{8,12},{12,8},{1,5},{5,1},{9,13},{13,9},{2,6},{6,2},{1... | collective-permute-start | bytes 3145736 | tf_op jit(solution)/shard_map/ppermute | solution.py:406
  592.1 70.1 %collective-permute-start.49 = (bf16[2048,256]{1,0:T(8,128)(2,1)}, bf16[2048,256]{1,0:T(8,128)(2,1)}, u32[]{:S(2)}, u32[]{:S(2)}) collective-permute-start(bf16[2048,256]{1,0:T(8,128)(2,1)} %pad_maximum_fusion.5), channel_id=1, source_target_pairs={{0,8},{4,12},{8,0},{12,4},{1,9},{5,13},{9,1},{13,5},{2,10},{6,14},... | collective-permute-start | bytes 3145736 | tf_op jit(solution)/shard_map/ppermute | solution.py:406
  594.9 73.7 %collective-permute-start.42 = (bf16[256,2048]{1,0:T(8,128)(2,1)}, bf16[256,2048]{1,0:T(8,128)(2,1)}, u32[]{:S(2)}, u32[]{:S(2)}) collective-permute-start(bf16[256,2048]{1,0:T(8,128)(2,1)} %pad_maximum_fusion.2), channel_id=1, source_target_pairs={{0,4},{4,0},{8,12},{12,8},{1,5},{5,1},{9,13},{13,9},{2,6},{6,2},{1... | collective-permute-start | bytes 3145736 | tf_op jit(solution)/shard_map/ppermute | solution.py:406
  598.5 70.1 %collective-permute-start.44 = (bf16[256,2048]{1,0:T(8,128)(2,1)}, bf16[256,2048]{1,0:T(8,128)(2,1)}, u32[]{:S(2)}, u32[]{:S(2)}) collective-permute-start(bf16[256,2048]{1,0:T(8,128)(2,1)} %pad_maximum_fusion.3), channel_id=1, source_target_pairs={{0,8},{4,12},{8,0},{12,4},{1,9},{5,13},{9,1},{13,5},{2,10},{6,14},... | collective-permute-start | bytes 3145736 | tf_op jit(solution)/shard_map/ppermute | solution.py:406
  608.6 41.0 %all-to-all-start.2 = ((bf16[4,2,256,128]{3,2,1,0:T(8,128)(2,1)}), bf16[4,2,256,128]{3,2,1,0:T(8,128)(2,1)S(1)}, u32[]{:S(2)}, u32[]{:S(2)}) async-start(bf16[4,2,256,128]{3,2,1,0:T(8,128)(2,1)} %bitcast.101), calls=%async_computation.5 | async-start | bytes 1048576 | tf_op jit(solution)/shard_map/all_to_all | solution.py:834
  612.3 129.1 %collective-permute-start.37 = (bf16[256,2048]{1,0:T(8,128)(2,1)}, bf16[256,2048]{1,0:T(8,128)(2,1)}, u32[]{:S(2)}, u32[]{:S(2)}) collective-permute-start(bf16[256,2048]{1,0:T(8,128)(2,1)} %pad_maximum_fusion), channel_id=1, source_target_pairs={{0,4},{4,0},{8,12},{12,8},{1,5},{5,1},{9,13},{13,9},{2,6},{6,2},{1... | collective-permute-start | bytes 3145736 | tf_op jit(solution)/shard_map/ppermute | solution.py:406
  660.1 138.1 %reduce-scatter.11.cloned.1.call-start = ((), (), s32[]{:S(2)}) async-start(), calls=%async_computation.15 | async-start | bytes 2621440 | tf_op jit(solution)/shard_map/reduce_scatter | solution.py:774
  660.1 81.2 %collective-permute-start.39 = (bf16[256,2048]{1,0:T(8,128)(2,1)}, bf16[256,2048]{1,0:T(8,128)(2,1)}, u32[]{:S(2)}, u32[]{:S(2)}) collective-permute-start(bf16[256,2048]{1,0:T(8,128)(2,1)} %pad_maximum_fusion.1), channel_id=1, source_target_pairs={{0,8},{4,12},{8,0},{12,4},{1,9},{5,13},{9,1},{13,5},{2,10},{6,14},... | collective-permute-start | bytes 3145736 | tf_op jit(solution)/shard_map/ppermute | solution.py:406
  668.6 68.9 %collective-permute-start.30 = (bf16[512,1024]{1,0:T(8,128)(2,1)}, bf16[512,1024]{1,0:T(8,128)(2,1)}, u32[]{:S(2)}, u32[]{:S(2)}) collective-permute-start(bf16[512,1024]{1,0:T(8,128)(2,1)} %convolution_convert_fusion.8), channel_id=1, source_target_pairs={{0,16},{16,0},{1,17},{17,1},{2,18},{18,2},{3,19},{19,3},{4,20},{20... | collective-permute-start | bytes 3145736 | tf_op jit(solution)/shard_map/ppermute | solution.py:410
  749.2 43.4 %collective-permute-start.32 = (bf16[512,256]{1,0:T(8,128)(2,1)}, bf16[512,256]{1,0:T(8,128)(2,1)}, u32[]{:S(2)}, u32[]{:S(2)}) collective-permute-start(bf16[512,256]{1,0:T(8,128)(2,1)} %pad_maximum_fusion.8), channel_id=1, source_target_pairs={{0,4},{4,0},{8,12},{12,8},{1,5},{5,1},{9,13},{13,9},{2,6},{6,2},{1... | collective-permute-start | bytes 786440 | tf_op jit(solution)/shard_map/ppermute | solution.py:406
  (91 other events, 1198.0 us)
Sparse Core Ops, SparseCore 0:
  178.3 41.1 reduce-scatter.4
  277.9 43.0 all-gather.4
  351.2 42.5 reduce-scatter.6
  399.3 45.2 all-gather.6
  474.4 42.5 reduce-scatter.8
  523.5 45.2 all-gather.8
  754.3 42.5 reduce-scatter.10

commit v2 on v0

--- a/solution.py
+++ b/solution.py
@@ -3,6 +3,8 @@
 import jax
 import jax.numpy as jnp
 from jax import lax
+from jax.experimental import pallas as pl
+from jax.experimental.pallas import tpu as pltpu
 from jax.sharding import PartitionSpec as P
 
 NORM_EPS = 1e-06
@@ -55,7 +57,7 @@
     return inv_scale * (grad_normed - normed * (total_dot / d_model)[..., None])
 
 
-def on_device(
+def on_any_mesh(
     tokens,
     w_query,
     w_key,
@@ -397,9 +399,924 @@
     )
 
 
+LOW = jnp.bfloat16
+VMEM_LIMIT = 50 * 1024 * 1024
+PARAMS = pltpu.CompilerParams(vmem_limit_bytes=VMEM_LIMIT)
+
+
+def to_neighbour(values, flip):
+    return lax.ppermute(values, "seq", [(i, i ^ flip) for i in range(4)])
+
+
+def to_core(values):
+    return lax.ppermute(values, "dp", [(0, 1), (1, 0)])
+
+
+def after(values, done):
+    return lax.optimization_barrier((values, done))[0]
+
+
+def first_step(shard):
+    return to_neighbour(shard, 1), to_neighbour(shard, 2)
+
+
+def gather_plane(shard, firsts, meanwhile=()):
+    half = shard.shape[0] // 2
+    (from_one, from_two), meanwhile = lax.optimization_barrier((firsts, meanwhile))
+    far_low = to_neighbour(from_two[:half], 1)
+    far_high = to_neighbour(from_one[half:], 2)
+    mine = [shard, from_one, from_two, far_low, far_high]
+    return mine + [to_core(piece) for piece in mine], meanwhile
+
+
+def place_piece(out_ref, order_ref, k, piece, axis):
+    block = piece.shape[axis]
+    if axis == 0 and k % 5 > 2:
+        block *= 2
+    first = piece.shape[0] if k % 5 == 4 else 0
+    start = order_ref[(k // 5) * 4 + min(k % 5, 3)] * block
+    if axis == 0:
+        out_ref[pl.ds(pl.multiple_of(start + first, piece.shape[0]), piece.shape[0])] = piece
+    else:
+        out_ref[first : first + piece.shape[0], pl.ds(pl.multiple_of(start, block), block)] = piece
+
+
+def assemble_columns(pieces, order):
+    height, block = pieces[0].shape
+
+    def body(order_ref, *refs):
+        for k in range(10):
+            place_piece(refs[10], order_ref, k, refs[k][...], 1)
+
+    return pl.pallas_call(
+        body,
+        in_specs=[pl.BlockSpec(memory_space=pltpu.SMEM)]
+        + [pl.BlockSpec(memory_space=pltpu.VMEM)] * 10,
+        out_specs=pl.BlockSpec(memory_space=pltpu.VMEM),
+        out_shape=jax.ShapeDtypeStruct((height, 8 * block), pieces[0].dtype),
+        compiler_params=PARAMS,
+        name="assemble_columns",
+    )(order, *pieces)
+
+
+def project_in(rows_low, pieces, order):
+    rows, width = rows_low.shape
+    columns = pieces[0].shape[1]
+    tile = columns // 3
+
+    def body(order_ref, rows_ref, *refs):
+        for k in range(10):
+            place_piece(refs[11], order_ref, k, refs[k][...], 0)
+        refs[10][...] = jnp.dot(rows_ref[...], refs[11][...], preferred_element_type=jnp.float32)
+
+    return pl.pallas_call(
+        body,
+        grid_spec=pltpu.PrefetchScalarGridSpec(
+            num_scalar_prefetch=1,
+            grid=(3,),
+            in_specs=[pl.BlockSpec((rows, width), lambda j, o: (0, 0))]
+            + [pl.BlockSpec((piece.shape[0], tile), lambda j, o: (0, j)) for piece in pieces],
+            out_specs=[
+                pl.BlockSpec((rows, tile), lambda j, o: (0, j)),
+                pl.BlockSpec((width, tile), lambda j, o: (0, j)),
+            ],
+        ),
+        out_shape=[
+            jax.ShapeDtypeStruct((rows, columns), jnp.float32),
+            jax.ShapeDtypeStruct((width, columns), LOW),
+        ],
+        compiler_params=PARAMS,
+        name="project_in",
+    )(order, rows_low, *pieces)
+
+
+def grad_blocks(lefts, rights, groups, order, blocks, received=None):
+    rows, d_model = lefts[0].shape
+    block = d_model // 8
+    half = block // 2
+    count = len(blocks)
+    width = sum(rights[right].shape[1] for _, right in groups[0])
+    fresh = received is None
+
+    def body(order_ref, *refs):
+        left_refs, right_refs = refs[: len(lefts)], refs[len(lefts) : len(lefts) + len(rights)]
+        rest = refs[len(lefts) + len(rights) :]
+        for k, pairs in enumerate(groups):
+
+            @pl.when(pl.program_id(1) == k)
+            def _(pairs=pairs):
+                first = 0
+                for left, right in pairs:
+                    total = contract(left_refs[left][...], right_refs[right][...], 0, 0)
+                    columns = slice(first, first + total.shape[1])
+                    first += total.shape[1]
+                    if fresh:
+                        rest[0][:, columns] = total.astype(LOW)
+                        continue
+                    total = (total + rest[0][:, columns].astype(jnp.float32)).astype(LOW)
+                    for b in range(count):
+
+                        @pl.when(pl.program_id(0) == b)
+                        def _(total=total, columns=columns, b=b):
+                            rest[1 + 2 * b][:, columns] = total[:half]
+                            rest[2 + 2 * b][:, columns] = total[half:]
+
+    def chosen(b, j, k):
+        return jnp.where(j == b, k, jnp.where(j < b, 0, len(groups) - 1))
+
+    def pick(j):
+        value = blocks[0]
+        for i, entry in enumerate(blocks[1:]):
+            value = jnp.where(j > i, entry, value)
+        return value
+
+    in_specs = [pl.BlockSpec((rows, block), lambda j, k, o: (0, o[pick(j)])) for _ in lefts]
+    in_specs += [pl.BlockSpec(right.shape, lambda j, k, o: (0, 0)) for right in rights]
+    if fresh:
+        out_specs = [pl.BlockSpec((block, width), lambda j, k, o: (j, k))]
+        out_shape = [jax.ShapeDtypeStruct((count * block, len(groups) * width), LOW)]
+    else:
+        in_specs.append(pl.BlockSpec((block, width), lambda j, k, o: (pick(j), k)))
+        out_specs = [
+            pl.BlockSpec((half, width), lambda j, k, o, b=b: (0, chosen(b, j, k)))
+            for b in range(count)
+            for _ in range(2)
+        ]
+        out_shape = [jax.ShapeDtypeStruct((half, len(groups) * width), LOW)] * (2 * count)
+    return pl.pallas_call(
+        body,
+        grid_spec=pltpu.PrefetchScalarGridSpec(
+            num_scalar_prefetch=1, grid=(count, len(groups)), in_specs=in_specs, out_specs=out_specs
+        ),
+        out_shape=out_shape,
+        compiler_params=PARAMS,
+        name="grad_blocks",
+    )(order, *lefts, *rights, *(() if fresh else (received,)))
+
+
+def add_low(mine, got):
+    return (mine.astype(jnp.float32) + got.astype(jnp.float32)).astype(LOW)
+
+
+def sum_in_core(lefts, rights, groups, order):
+    (sent,) = grad_blocks(lefts, rights, groups, order, (4, 5, 6, 7))
+    received = to_core(sent)
+    far = grad_blocks(lefts, rights, groups, order, (3,), received)
+    near = grad_blocks(lefts, rights, groups, order, (1, 2, 0), received)
+    return far, near
+
+
+def send_first(far, near):
+    one_low, _, _, two_high, _, _ = near
+    return [to_neighbour(far[0], 1), to_neighbour(far[1], 2)], [
+        to_neighbour(one_low, 1),
+        to_neighbour(two_high, 2),
+    ]
+
+
+def send_second(far, near):
+    return [
+        to_neighbour(add_low(near[1], far[1]), 1),
+        to_neighbour(add_low(near[2], far[0]), 2),
+    ]
+
+
+def halves_total(near, first, second):
+    def total(*values):
+        low, one, two = (value.astype(jnp.float32) for value in values)
+        return low + one + two
+
+    return total(near[4], first[0], second[1]), total(near[5], second[0], first[1])
+
+
+def gather_line(own):
+    up, down = own, own
+    ups, downs = [], []
+    for t in range(1, 4):
+        up = lax.ppermute(up, "tp", [(i, i + 1) for i in range(t - 1, 3)])
+        down = lax.ppermute(down, "tp", [(i, i - 1) for i in range(1, 5 - t)])
+        ups.append(up)
+        downs.append(down)
+    return [own] + ups + downs
+
+
+def scatter_line(slots, meanwhile=((), ())):
+    meanwhile = list(meanwhile)
+    def added(mine, got):
+        return (mine.astype(jnp.float32) + got.astype(jnp.float32)).astype(LOW)
+
+    up, down = slots[1], slots[3]
+    for t in range(1, 4):
+        up = lax.ppermute(up, "tp", [(i, i + 1) for i in range(t)])
+        down = lax.ppermute(down, "tp", [(i, i - 1) for i in range(4 - t, 4)])
+        if t < 3:
+            up, down, meanwhile[t - 1] = lax.optimization_barrier((up, down, meanwhile[t - 1]))
+            up = added(slots[t + 1], up)
+            down = added(slots[3 - t], down)
+    total = slots[0].astype(jnp.float32) + up.astype(jnp.float32) + down.astype(jnp.float32)
+    return total, meanwhile
+
+
+def sum_line(values):
+    flat = lax.optimization_barrier(values.reshape(-1, 128))
+    return lax.optimization_barrier(lax.psum(flat, "tp"))
+
+
+def contract(left, right, left_dim, right_dim):
+    return lax.dot_general(
+        left, right, (((left_dim,), (right_dim,)), ((), ())), preferred_element_type=jnp.float32
+    )
+
+
+def turned(values, cosines, sines):
+    return values * cosines + pltpu.roll(values, values.shape[-1] // 2, axis=1) * sines
+
+
+def inverse_norm(squares, d_model):
+    return lax.rsqrt(squares * (1.0 / d_model) + NORM_EPS)
+
+
+def prepare(raw, squares, gains, cosines, sines, heads, head_dim, d_model):
+    seqs, length, _ = raw.shape
+    own = length // 4
+    rows = seqs * own
+    span = heads * head_dim
+
+    def body(raw_ref, square_ref, gain_ref, cos_ref, sin_ref, out_ref):
+        cosine = jnp.concatenate([cos_ref[...]] * seqs, axis=0)
+        sine = jnp.concatenate([sin_ref[...]] * seqs, axis=0)
+        for t in range(2):
+            inv = inverse_norm(square_ref[t].reshape(rows, 1), d_model)
+            for h in range(heads):
+                columns = slice(t * span + h * head_dim, t * span + (h + 1) * head_dim)
+                normed = raw_ref[:, :, columns].reshape(rows, head_dim) * inv * gain_ref[:, columns]
+                out_ref[h, t] = (
+                    turned(normed, cosine, sine).astype(LOW).reshape(seqs, own, head_dim)
+                )
+        for h in range(heads):
+            columns = slice(2 * span + h * head_dim, 2 * span + (h + 1) * head_dim)
+            out_ref[h, 2] = raw_ref[:, :, columns].astype(LOW)
+
+    return pl.pallas_call(
+        body,
+        grid=(4,),
+        in_specs=[
+            pl.BlockSpec((seqs, own, 3 * span), lambda t: (0, t, 0)),
+            pl.BlockSpec((2, seqs, own, 1), lambda t: (0, 0, t, 0)),
+            pl.BlockSpec((1, 2 * span), lambda t: (0, 0)),
+            pl.BlockSpec((own, head_dim), lambda t: (t, 0)),
+            pl.BlockSpec((own, head_dim), lambda t: (t, 0)),
+        ],
+        out_specs=pl.BlockSpec((heads, 3, seqs, own, head_dim), lambda t: (0, 0, 0, t, 0)),
+        out_shape=jax.ShapeDtypeStruct((heads, 3, seqs, length, head_dim), LOW),
+        compiler_params=PARAMS,
+        name="prepare",
+    )(raw, squares, gains, cosines, sines)
+
+
+def scores_of(left, right):
+    return lax.dot_general(
+        left, right, (((1,), (1,)), ((), ())), preferred_element_type=jnp.float32
+    )
+
+
+def causal(scores, first):
+    rows = lax.broadcasted_iota(jnp.int32, scores.shape, 0) + first
+    columns = lax.broadcasted_iota(jnp.int32, scores.shape, 1)
+    return columns <= rows
+
+
+def attend(parts):
+    blocks, _, seqs, length, head_dim = parts.shape
+    score_scale = head_dim ** (-0.5)
+
+    def body(parts_ref, out_ref, log_ref):
+        for i in range(blocks):
+            span = (i + 1) * length
+            keys = parts_ref[: i + 1, 1, 0].reshape(span, head_dim)
+            values = parts_ref[: i + 1, 2, 0].reshape(span, head_dim)
+            scores = scores_of(parts_ref[i, 0, 0], keys) * score_scale
+            scores = jnp.where(causal(scores, i * length), scores, MASKED)
+            top = jnp.max(scores, axis=-1, keepdims=True)
+            weights = jnp.exp(scores - top)
+            total = jnp.sum(weights, axis=-1, keepdims=True)
+            probs = (weights * (1.0 / total)).astype(LOW)
+            out_ref[i, 0] = jnp.dot(probs, values, preferred_element_type=jnp.float32).astype(LOW)
+            log_ref[i, 0] = top + jnp.log(total)
+
+    return pl.pallas_call(
+        body,
+        grid=(seqs,),
+        in_specs=[pl.BlockSpec((blocks, 3, 1, length, head_dim), lambda m: (0, 0, m, 0, 0))],
+        out_specs=[
+            pl.BlockSpec((blocks, 1, length, head_dim), lambda m: (0, m, 0, 0)),
+            pl.BlockSpec((blocks, 1, length, 1), lambda m: (0, m, 0, 0)),
+        ],
+        out_shape=[
+            jax.ShapeDtypeStruct((blocks, seqs, length, head_dim), LOW),
+            jax.ShapeDtypeStruct((blocks, seqs, length, 1), jnp.float32),
+        ],
+        compiler_params=PARAMS,
+        name="attend",
+    )(parts)
+
+
+def attend_back(parts, grad_context, log_total):
+    blocks, _, seqs, length, head_dim = parts.shape
+    score_scale = head_dim ** (-0.5)
+
+    def body(parts_ref, grad_ref, log_ref, out_ref, keys_sum, values_sum):
+        keys_sum[...] = jnp.zeros_like(keys_sum)
+        values_sum[...] = jnp.zeros_like(values_sum)
+        for i in range(blocks):
+            span = (i + 1) * length
+            queries = parts_ref[i, 0, 0]
+            keys = parts_ref[: i + 1, 1, 0].reshape(span, head_dim)
+            values = parts_ref[: i + 1, 2, 0].reshape(span, head_dim)
+            grads = grad_ref[i, 0]
+            scores = scores_of(queries, keys) * score_scale
+            probs = jnp.where(causal(scores, i * length), jnp.exp(scores - log_ref[i, 0]), 0.0)
+            grad_probs = scores_of(grads, values)
+            delta = jnp.sum(probs * grad_probs, axis=-1, keepdims=True)
+            grad_scores = (probs * (grad_probs - delta)).astype(LOW)
+            out_ref[i, 0, 0] = (
+                jnp.dot(grad_scores, keys, preferred_element_type=jnp.float32) * score_scale
+            ).astype(LOW)
+            keys_sum[:span] += contract(grad_scores, queries, 0, 0)
+            values_sum[:span] += contract(probs.astype(LOW), grads, 0, 0)
+        out_ref[:, 1, 0] = (
+            (keys_sum[...] * score_scale).astype(LOW).reshape(blocks, length, head_dim)
+        )
+        out_ref[:, 2, 0] = values_sum[...].astype(LOW).reshape(blocks, length, head_dim)
+
+    whole = pl.BlockSpec((blocks, 3, 1, length, head_dim), lambda m: (0, 0, m, 0, 0))
+    return pl.pallas_call(
+        body,
+        grid=(seqs,),
+        in_specs=[
+            whole,
+            pl.BlockSpec((blocks, 1, length, head_dim), lambda m: (0, m, 0, 0)),
+            pl.BlockSpec((blocks, 1, length, 1), lambda m: (0, m, 0, 0)),
+        ],
+        out_specs=whole,
+        out_shape=jax.ShapeDtypeStruct(parts.shape, LOW),
+        scratch_shapes=[
+            pltpu.VMEM((blocks * length, head_dim), jnp.float32),
+            pltpu.VMEM((blocks * length, head_dim), jnp.float32),
+        ],
+        compiler_params=PARAMS,
+        name="attend_back",
+    )(parts, grad_context, log_total)
+
+
+def project_out(context, weights, slots):
+    heads, seqs, length, head_dim = context.shape
+    span, width = weights.shape
+    own = length // 4
+    own_rows = seqs * own
+    tile = width // 2
+
+    def body(slots_ref, context_ref, weight_ref, rows_ref, *outs):
+        @pl.when(pl.program_id(0) == 0)
+        def _():
+            for t in range(4):
+                place = pl.ds(pl.multiple_of(slots_ref[t] * own, own), own)
+                for h in range(heads):
+                    rows_ref[
+                        t * own_rows : (t + 1) * own_rows, h * head_dim : (h + 1) * head_dim
+                    ] = context_ref[h, :, place].reshape(own_rows, head_dim)
+
+        product = jnp.dot(rows_ref[...], weight_ref[...], preferred_element_type=jnp.float32)
+        for t in range(4):
+            outs[t][...] = product[t * own_rows : (t + 1) * own_rows].astype(LOW)
+
+    return pl.pallas_call(
+        body,
+        grid_spec=pltpu.PrefetchScalarGridSpec(
+            num_scalar_prefetch=1,
+            grid=(2,),
+            in_specs=[
+                pl.BlockSpec(context.shape, lambda j, s: (0, 0, 0, 0)),
+                pl.BlockSpec((span, tile), lambda j, s: (0, j)),
+            ],
+            out_specs=[pl.BlockSpec((4 * own_rows, span), lambda j, s: (0, 0))]
+            + [pl.BlockSpec((own_rows, tile), lambda j, s: (0, j))] * 4,
+        ),
+        out_shape=[jax.ShapeDtypeStruct((4 * own_rows, span), LOW)]
+        + [jax.ShapeDtypeStruct((own_rows, width), LOW)] * 4,
+        compiler_params=PARAMS,
+        name="project_out",
+    )(slots, context, weights)
+
+
+def project_out_back(pieces, weights, slots, heads, seqs):
+    own_rows, width = pieces[0].shape
+    span = weights.shape[0]
+    head_dim = span // heads
+    own = own_rows // seqs
+    rows = 4 * own_rows
+
+    def body(slots_ref, *refs):
+        ins, weight_ref, out_ref, rows_ref = refs[:7], refs[7], refs[8], refs[9]
+        fill_slots(rows_ref, ins)
+        product = scores_of(rows_ref[...], weight_ref[...]).astype(LOW)
+        for t in range(4):
+            place = pl.ds(pl.multiple_of(slots_ref[t] * own, own), own)
+            for h in range(heads):
+                out_ref[h, :, place] = product[
+                    t * own_rows : (t + 1) * own_rows, h * head_dim : (h + 1) * head_dim
+                ].reshape(seqs, own, head_dim)
+
+    scalars = pl.BlockSpec(memory_space=pltpu.SMEM)
+    whole = pl.BlockSpec(memory_space=pltpu.VMEM)
+    return pl.pallas_call(
+        body,
+        in_specs=[scalars] + [whole] * 8,
+        out_specs=[whole] * 2,
+        out_shape=[
+            jax.ShapeDtypeStruct((heads, seqs, 4 * own, head_dim), LOW),
+            jax.ShapeDtypeStruct((rows, width), LOW),
+        ],
+        compiler_params=PARAMS,
+        name="project_out_back",
+    )(slots, *pieces, weights)
+
+
+def unprepare(grads, raw, squares, gains, cosines, sines, d_model):
+    heads, _, seqs, length, head_dim = grads.shape
+    own = length // 4
+    rows = seqs * own
+    span = heads * head_dim
+
+    def body(
+        grad_ref, raw_ref, square_ref, gain_ref, cos_ref, sin_ref, scaled_ref, dot_ref, sum_ref
+    ):
+        cosine = jnp.concatenate([cos_ref[...]] * seqs, axis=0)
+        sine = -jnp.concatenate([sin_ref[...]] * seqs, axis=0)
+
+        @pl.when(pl.program_id(0) == 0)
+        def _():
+            sum_ref[...] = jnp.zeros_like(sum_ref)
+
+        for t in range(2):
+            inv = inverse_norm(square_ref[t].reshape(rows, 1), d_model)
+            total = jnp.zeros((rows, head_dim), jnp.float32)
+            for h in range(heads):
+                columns = slice(t * span + h * head_dim, t * span + (h + 1) * head_dim)
+                back = turned(
+                    grad_ref[h, t].reshape(rows, head_dim).astype(jnp.float32), cosine, sine
+                )
+                along = back * (raw_ref[:, :, columns].reshape(rows, head_dim) * inv)
+                sum_ref[:, columns] += jnp.sum(along, axis=0, keepdims=True)
+                scaled_ref[:, :, columns] = (back * gain_ref[:, columns]).reshape(
+                    seqs, own, head_dim
+                )
+                total += along * gain_ref[:, columns]
+            dot_ref[t] = jnp.sum(total, axis=-1, keepdims=True).reshape(seqs, own, 1)
+
+    return pl.pallas_call(
+        body,
+        grid=(4,),
+        in_specs=[
+            pl.BlockSpec((heads, 3, seqs, own, head_dim), lambda t: (0, 0, 0, t, 0)),
+            pl.BlockSpec((seqs, own, 3 * span), lambda t: (0, t, 0)),
+            pl.BlockSpec((2, seqs, own, 1), lambda t: (0, 0, t, 0)),
+            pl.BlockSpec((1, 2 * span), lambda t: (0, 0)),
+            pl.BlockSpec((own, head_dim), lambda t: (t, 0)),
+            pl.BlockSpec((own, head_dim), lambda t: (t, 0)),
+        ],
+        out_specs=[
+            pl.BlockSpec((seqs, own, 2 * span), lambda t: (0, t, 0)),
+            pl.BlockSpec((2, seqs, own, 1), lambda t: (0, 0, t, 0)),
+            pl.BlockSpec((1, 2 * span), lambda t: (0, 0)),
+        ],
+        out_shape=[
+            jax.ShapeDtypeStruct((seqs, length, 2 * span), jnp.float32),
+            jax.ShapeDtypeStruct((2, seqs, length, 1), jnp.float32),
+            jax.ShapeDtypeStruct((1, 2 * span), jnp.float32),
+        ],
+        compiler_params=PARAMS,
+        name="unprepare",
+    )(grads, raw, squares, gains, cosines, sines)
+
+
+def project_in_back(grads, scaled, raw, squares, dots, weights, slots):
+    heads, _, seqs, length, head_dim = grads.shape
+    own = length // 4
+    own_rows = seqs * own
+    rows = seqs * length
+    span = heads * head_dim
+    d_model = weights.shape[0]
+    tile = d_model // 4
+
+    def body(
+        slots_ref, grad_ref, scaled_ref, raw_ref, square_ref, dot_ref, weight_ref, rows_ref, *refs
+    ):
+        outs, product = refs[:4], refs[4]
+
+        @pl.when(pl.program_id(0) == 0)
+        def _():
+            for k in range(2):
+                columns = slice(k * span, (k + 1) * span)
+                inv = inverse_norm(square_ref[k].reshape(rows, 1), d_model)
+                mean = dot_ref[k].reshape(rows, 1) * (1.0 / d_model)
+                unit = raw_ref[:, :, columns].reshape(rows, span) * inv
+                rows_ref[:, columns] = (
+                    inv * (scaled_ref[:, :, columns].reshape(rows, span) - unit * mean)
+                ).astype(LOW)
+            for h in range(heads):
+                columns = slice(2 * span + h * head_dim, 2 * span + (h + 1) * head_dim)
+                rows_ref[:, columns] = grad_ref[h, 0].reshape(rows, head_dim)
+
+        product[...] = scores_of(rows_ref[...], weight_ref[...]).reshape(seqs, length, tile)
+        for t in range(4):
+            place = pl.ds(pl.multiple_of(slots_ref[t] * own, own), own)
+            outs[t][...] = product[:, place].reshape(own_rows, tile).astype(LOW)
+
+    flat = pl.BlockSpec((2, seqs, length, 1), lambda j, s: (0, 0, 0, 0))
+    return pl.pallas_call(
+        body,
+        grid_spec=pltpu.PrefetchScalarGridSpec(
+            num_scalar_prefetch=1,
+            grid=(4,),
+            in_specs=[
+                pl.BlockSpec((heads, 1, seqs, length, head_dim), lambda j, s: (0, 2, 0, 0, 0)),
+                pl.BlockSpec((seqs, length, 2 * span), lambda j, s: (0, 0, 0)),
+                pl.BlockSpec((seqs, length, 2 * span), lambda j, s: (0, 0, 0)),
+                flat,
+                flat,
+                pl.BlockSpec((tile, 3 * span), lambda j, s: (j, 0)),
+            ],
+            out_specs=[pl.BlockSpec((rows, 3 * span), lambda j, s: (0, 0))]
+            + [pl.BlockSpec((own_rows, tile), lambda j, s: (0, j))] * 4,
+            scratch_shapes=[pltpu.VMEM((seqs, length, tile), jnp.float32)],
+        ),
+        out_shape=[jax.ShapeDtypeStruct((rows, 3 * span), LOW)]
+        + [jax.ShapeDtypeStruct((own_rows, d_model), LOW)] * 4,
+        compiler_params=PARAMS,
+        name="project_in_back",
+    )(slots, grads, scaled, raw, squares, dots, weights)
+
+
+def fill_slots(rows_ref, refs):
+    own = refs[0].shape[0]
+    rows_ref[:own] = refs[0][...]
+    for t in range(1, 4):
+        rows_ref[t * own : (t + 1) * own] = refs[t][...] + refs[7 - t][...]
+
+
+def weight_tiles(width, tile, tiles):
+    return [pl.BlockSpec((width, tile), lambda j, k=k: (0, k * tiles + j)) for k in range(3)]
+
+
+def feed_forward(pieces, weights):
+    own, width = pieces[0].shape
+    hidden_units = weights.shape[1] // 3
+    tile = 512
+    tiles = hidden_units // tile
+    rows = 4 * own
+
+    def body(*refs):
+        ins, (gate_w, up_w, down_w) = refs[:7], refs[7:10]
+        rows_ref, gate_ref, up_ref, mixed_ref = refs[10:14]
+        outs, total = refs[14:18], refs[18]
+
+        @pl.when(pl.program_id(0) == 0)
+        def _():
+            fill_slots(rows_ref, ins)
+
+        gate = jnp.dot(rows_ref[...], gate_w[...], preferred_element_type=jnp.float32)
+        up = jnp.dot(rows_ref[...], up_w[...], preferred_element_type=jnp.float32)
+        mixed = (gate * jax.nn.sigmoid(gate) * up).astype(LOW)
+        gate_ref[...] = gate.astype(LOW)
+        up_ref[...] = up.astype(LOW)
+        mixed_ref[...] = mixed
+        part = scores_of(mixed, down_w[...])
+
+        @pl.when(pl.program_id(0) == 0)
+        def _():
+            total[...] = part
+
+        @pl.when((pl.program_id(0) > 0) & (pl.program_id(0) < tiles - 1))
+        def _():
+            total[...] += part
+
+        @pl.when(pl.program_id(0) == tiles - 1)
+        def _():
+            for t in range(4):
+                mine = slice(t * own, (t + 1) * own)
+                outs[t][...] = (total[mine] + part[mine]).astype(LOW)
+
+    fixed = pl.BlockSpec((own, width), lambda j: (0, 0))
+    by_tile = pl.BlockSpec((rows, tile), lambda j: (0, j))
+    return pl.pallas_call(
+        body,
+        grid=(tiles,),
+        in_specs=[fixed] * 7 + weight_tiles(width, tile, tiles),
+        out_specs=[pl.BlockSpec((rows, width), lambda j: (0, 0))] + [by_tile] * 3 + [fixed] * 4,
+        out_shape=[jax.ShapeDtypeStruct((rows, width), LOW)]
+        + [jax.ShapeDtypeStruct((rows, hidden_units), LOW)] * 3
+        + [jax.ShapeDtypeStruct((own, width), LOW)] * 4,
+        scratch_shapes=[pltpu.VMEM((rows, width), jnp.float32)],
+        compiler_params=PARAMS,
+        name="feed_forward",
+    )(*pieces, weights, weights, weights)
+
+
+def feed_forward_back(rows_low, gate, up, weights):
+    rows, width = rows_low.shape
+    own = rows // 4
+    hidden_units = gate.shape[1]
+    tile = 512
+    tiles = hidden_units // tile
+
+    def body(rows_ref, gate_ref, up_ref, gate_w, up_w, down_w, grad_gate_ref, grad_up_ref, *refs):
+        outs, total = refs[:4], refs[4]
+        grad_mixed = jnp.dot(rows_ref[...], down_w[...], preferred_element_type=jnp.float32)
+        gate = gate_ref[...].astype(jnp.float32)
+        up = up_ref[...].astype(jnp.float32)
+        sig = jax.nn.sigmoid(gate)
+        grad_gate = (grad_mixed * up * sig * (1.0 + gate * (1.0 - sig))).astype(LOW)
+        grad_up = (grad_mixed * gate * sig).astype(LOW)
+        grad_gate_ref[...] = grad_gate
+        grad_up_ref[...] = grad_up
+        part = scores_of(grad_gate, gate_w[...]) + scores_of(grad_up, up_w[...])
+
+        @pl.when(pl.program_id(0) == 0)
+        def _():
+            total[...] = part
+
+        @pl.when((pl.program_id(0) > 0) & (pl.program_id(0) < tiles - 1))
+        def _():
+            total[...] += part
+
+        @pl.when(pl.program_id(0) == tiles - 1)
+        def _():
+            for t in range(4):
+                mine = slice(t * own, (t + 1) * own)
+                outs[t][...] = (total[mine] + part[mine]).astype(LOW)
+
+    fixed = pl.BlockSpec((own, width), lambda j: (0, 0))
+    by_tile = pl.BlockSpec((rows, tile), lambda j: (0, j))
+    return pl.pallas_call(
+        body,
+        grid=(tiles,),
+        in_specs=[pl.BlockSpec((rows, width), lambda j: (0, 0))]
+        + [by_tile] * 2
+        + weight_tiles(width, tile, tiles),
+        out_specs=[by_tile] * 2 + [fixed] * 4,
+        out_shape=[jax.ShapeDtypeStruct((rows, hidden_units), LOW)] * 2
+        + [jax.ShapeDtypeStruct((own, width), LOW)] * 4,
+        scratch_shapes=[pltpu.VMEM((rows, width), jnp.float32)],
+        compiler_params=PARAMS,
+        name="feed_forward_back",
+    )(rows_low, gate, up, weights, weights, weights)
+
+
+def down_grad(pieces, mixed):
+    own, width = pieces[0].shape
+    rows, columns = mixed.shape
+    tile = 512
+
+    def body(*refs):
+        rows_ref, out_ref = refs[8], refs[9]
+
+        @pl.when(pl.program_id(0) == 0)
+        def _():
+            fill_slots(rows_ref, refs[:7])
+
+        place = pl.ds(pl.multiple_of(pl.program_id(0) * tile, tile), tile)
+        out_ref[...] = contract(rows_ref[:, place], refs[7][...], 0, 0).astype(LOW)
+
+    return pl.pallas_call(
+        body,
+        grid=(width // tile,),
+        in_specs=[pl.BlockSpec((own, width), lambda j: (0, 0))] * 7
+        + [pl.BlockSpec((rows, columns), lambda j: (0, 0))],
+        out_specs=[
+            pl.BlockSpec((rows, width), lambda j: (0, 0)),
+            pl.BlockSpec((tile, columns), lambda j: (j, 0)),
+        ],
+        out_shape=[
+            jax.ShapeDtypeStruct((rows, width), LOW),
+            jax.ShapeDtypeStruct((width, columns), LOW),
+        ],
+        compiler_params=PARAMS,
+        name="down_grad",
+    )(*pieces, mixed)
+
+
+def weight_grad(left, right, all_columns, place, others=None):
+    rows, width = left.shape
+    columns = right.shape[1]
+    tile = 512
+
+    def body(left_ref, right_ref, *refs):
+        refs[-1][...] = contract(left_ref[...], right_ref[...], 0, 0).astype(LOW)
+
+    given = () if others is None else (others,)
+    return pl.pallas_call(
+        body,
+        grid=(width // tile,),
+        in_specs=[
+            pl.BlockSpec((rows, tile), lambda j: (0, j)),
+            pl.BlockSpec((rows, columns), lambda j: (0, 0)),
+        ]
+        + [pl.BlockSpec(memory_space=pl.ANY)] * len(given),
+        out_specs=pl.BlockSpec((tile, columns), lambda j: (j, place)),
+        out_shape=jax.ShapeDtypeStruct((width, all_columns), LOW),
+        input_output_aliases={2: 0} if given else {},
+        compiler_params=PARAMS,
+        name="weight_grad",
+    )(left, right, *given)
+
+
+def on_plane(
+    tokens,
+    w_query,
+    w_key,
+    w_value,
+    w_out,
+    w_gate,
+    w_up,
+    w_down,
+    q_gain,
+    k_gain,
+    attn_gain,
+    mlp_gain,
+    cotangent,
+):
+    seqs, length, d_model = tokens.shape
+    rows = seqs * length
+    tp_rank = lax.axis_index("tp")
+    seq_rank = lax.axis_index("seq")
+    heads = q_gain.shape[0]
+    head_dim = q_gain.shape[1] * 8
+    head_span = heads * head_dim
+    own_length = length // 4
+    own_rows = seqs * own_length
+    order = (lax.axis_index("dp") * 4 + seq_rank) ^ jnp.arange(8, dtype=jnp.int32)
+    slots = (tp_rank + 4 - jnp.arange(4, dtype=jnp.int32)) % 4
+
+    gain_rows = jnp.concatenate([q_gain, k_gain, attn_gain, mlp_gain], axis=0)
+    all_gains = lax.all_to_all(
+        jnp.broadcast_to(gain_rows.reshape(1, -1), (8, gain_rows.size)), ("dp", "seq"), 0, 0, tiled=True
+    )
+    packed = jnp.concatenate([w_gate, w_up, w_down.T], axis=1)
+    in_shard = jnp.concatenate([w_query, w_key, w_value], axis=1)
+    in_pieces, (all_gains, packed) = gather_plane(
+        in_shard, first_step(in_shard), (all_gains, packed)
+    )
+    all_gains = (
+        jnp.transpose(all_gains.reshape((8,) + gain_rows.shape), (1, 0, 2))
+        .reshape(gain_rows.shape[0], head_dim)
+        .astype(jnp.float32)
+    )
+    qk_gain = all_gains[: 2 * heads].reshape(1, 2 * head_span)
+    feature_rows = d_model // head_dim
+    attn_gains = all_gains[2 * heads : 2 * heads + feature_rows].reshape(d_model)
+    mlp_gains = all_gains[2 * heads + feature_rows :].reshape(d_model)
+    positions = seq_rank * length + jnp.arange(length, dtype=jnp.int32)
+    cosines, sines = rope_tables(positions, head_dim)
+    cosines = jnp.concatenate([cosines[:, 0], cosines[:, 0]], axis=-1)
+    sines = jnp.concatenate([-sines[:, 0], sines[:, 0]], axis=-1)
+    own_tokens = (
+        lax.dynamic_slice_in_dim(tokens, tp_rank * own_length, own_length, 1)
+        .astype(jnp.float32)
+        .reshape(own_rows, d_model)
+    )
+    grad_out = cotangent.astype(jnp.float32).reshape(own_rows, d_model)
+
+    raw, in_weights = project_in(tokens.reshape(rows, d_model), in_pieces, order)
+    out_firsts = first_step(after(w_out, in_pieces[3:5]))
+    weights = lax.all_gather(after(packed, in_pieces[3:5]), ("dp", "seq"), axis=0, tiled=True)
+
+    squares = jnp.stack(
+        [
+            jnp.sum(jnp.square(raw[:, :head_span]), axis=-1),
+            jnp.sum(jnp.square(raw[:, head_span : 2 * head_span]), axis=-1),
+        ]
+    )
+    squares, out_firsts = lax.optimization_barrier((sum_line(squares), out_firsts))
+    squares = squares.reshape(2, seqs, length, 1)
+    out_pieces, _ = gather_plane(w_out, out_firsts)
+    raw = raw.reshape(seqs, length, 3 * head_span)
+    parts = prepare(raw, squares, qk_gain, cosines, sines, heads, head_dim, d_model)
+    parts = lax.all_to_all(parts, "seq", 0, 0, tiled=True)
+    parts, out_pieces = lax.optimization_barrier((parts, out_pieces))
+    out_weights = assemble_columns(out_pieces, order)
+    context, log_total = attend(parts)
+    context = lax.all_to_all(context, "seq", 0, 0, tiled=True)
+    context_rows, *attn_slots = project_out(context, out_weights, slots)
+    attn_out, _ = scatter_line(attn_slots)
+    attn_inv = lax.rsqrt(jnp.mean(attn_out * attn_out, axis=-1, keepdims=True) + NORM_EPS)
+    attn_unit = attn_out * attn_inv
+    hidden = own_tokens + attn_unit * attn_gains
+    hidden_rows, gate, up, mixed, *mlp_slots = feed_forward(
+        gather_line(hidden.astype(LOW)), weights
+    )
+    mlp_out, _ = scatter_line(mlp_slots)
+    mlp_inv = lax.rsqrt(jnp.mean(mlp_out * mlp_out, axis=-1, keepdims=True) + NORM_EPS)
+    mlp_unit = mlp_out * mlp_inv
+    outputs = (hidden + mlp_unit * mlp_gains).astype(LOW)
+
+    grad_mgain = jnp.sum(grad_out * mlp_unit, axis=0)
+    mlp_scaled = grad_out * mlp_gains
+    grad_mlp = norm_back(
+        mlp_unit, mlp_scaled, mlp_inv, jnp.sum(mlp_scaled * mlp_unit, axis=-1), d_model
+    )
+    grad_mlp_rows, down_part = down_grad(gather_line(grad_mlp.astype(LOW)), mixed)
+    grad_gate, grad_up, *hidden_slots = feed_forward_back(grad_mlp_rows, gate, up, weights)
+    units = mixed.shape[1]
+    gate_part = weight_grad(hidden_rows, grad_gate, 2 * units, 0)
+    hidden_sum, (gate_part, _) = scatter_line(hidden_slots, (gate_part, ()))
+    gate_up_part = weight_grad(hidden_rows, grad_up, 2 * units, 1, gate_part)
+    hidden_sum, gate_up_part = lax.optimization_barrier((hidden_sum, gate_up_part))
+
+    def sum_plane(part):
+        return lax.optimization_barrier(
+            lax.psum_scatter(part, ("dp", "seq"), scatter_dimension=0, tiled=True)
+        )
+
+    down_sum = sum_plane(down_part)
+    gate_up_sum = sum_plane(gate_up_part)
+    ff_sums = (
+        gate_up_sum[:, :units].astype(jnp.float32),
+        gate_up_sum[:, units:].astype(jnp.float32),
+        down_sum.T.astype(jnp.float32),
+    )
+
+    def joined(halves, first, last):
+        return jnp.concatenate([half[:, first:last] for half in halves], axis=0)
+
+    grad_hidden = grad_out + hidden_sum
+    grad_again = jnp.sum(grad_hidden * attn_unit, axis=0)
+    attn_scaled = grad_hidden * attn_gains
+    grad_attn = norm_back(
+        attn_unit, attn_scaled, attn_inv, jnp.sum(attn_scaled * attn_unit, axis=-1), d_model
+    ).astype(LOW)
+    grad_context, grad_attn_rows = project_out_back(
+        gather_line(grad_attn), out_weights, slots, heads, seqs
+    )
+    grad_context = lax.all_to_all(grad_context, "seq", 0, 0, tiled=True)
+    part_grads = attend_back(parts, grad_context, log_total)
+    part_grads = lax.all_to_all(part_grads, "seq", 0, 0, tiled=True)
+    scaled, dots, qk_sums = unprepare(part_grads, raw, squares, qk_gain, cosines, sines, d_model)
+    dots = sum_line(dots.reshape(2, rows)).reshape(2, seqs, length, 1)
+    grad_raw, *token_slots = project_in_back(
+        part_grads, scaled, raw, squares, dots, in_weights, slots
+    )
+    in_far, in_near = sum_in_core(
+        (tokens.reshape(rows, d_model), grad_attn_rows),
+        (grad_raw, context_rows),
+        (((0, 0), (1, 1)),),
+        order,
+    )
+    token_sum, (in_far, in_near) = scatter_line(token_slots, (in_far, in_near))
+    in_far, in_first = send_first(in_far, in_near)
+    in_second = send_second(in_far, in_near)
+    in_second, ff_sums = lax.optimization_barrier((in_second, ff_sums))
+    in_halves = halves_total(in_near, in_first, in_second)
+    grad_tokens = grad_hidden + token_sum
+
+    def by_owner(values):
+        return jnp.transpose(values.reshape(4, feature_rows // 4, 8, -1), (2, 0, 1, 3))
+
+    head_sums = jnp.transpose(qk_sums.reshape(2, heads, 8, -1), (2, 0, 1, 3))[:, None]
+    is_own = (jnp.arange(4) == tp_rank)[None, :, None, None, None]
+    payload = jnp.concatenate(
+        [
+            jnp.where(is_own, head_sums, 0.0),
+            by_owner(grad_again)[:, :, None],
+            by_owner(grad_mgain)[:, :, None],
+        ],
+        axis=2,
+    ).reshape(32, -1)
+    payload = after(payload, in_near)
+    gain_sums = jnp.sum(
+        lax.all_to_all(payload, ("dp", "seq", "tp"), 0, 0, tiled=True), axis=0
+    ).reshape(4, heads, -1)
+    return (
+        outputs.reshape(seqs, own_length, d_model),
+        grad_tokens.reshape(seqs, own_length, d_model),
+        joined(in_halves, 0, head_span),
+        joined(in_halves, head_span, 2 * head_span),
+        joined(in_halves, 2 * head_span, 3 * head_span),
+        joined(in_halves, 3 * head_span, 4 * head_span).T,
+        ff_sums[0],
+        ff_sums[1],
+        ff_sums[2],
+        gain_sums[0],
+        gain_sums[1],
+        gain_sums[2],
+        gain_sums[3],
+    )
+
+
 def solution(mesh):
+    by_plane = (mesh.shape["dp"], mesh.shape["seq"], mesh.shape["tp"]) == (2, 4, 4)
     return jax.shard_map(
-        on_device,
+        on_plane if by_plane else on_any_mesh,
         mesh=mesh,
         in_specs=(
             P("dp", "seq", None),

time: 1510 us -> 672 us (0.45)
  waiting for transfers between devices: 1080 us -> 207 us
  matrix products: 160 us -> 0 us
  starting transfers between devices: 2.39 us -> 141 us
  Pallas kernels: 0 us -> 138 us
  blocking collectives: 114 us -> 69.5 us
  local copies, waits for them, and re-layouts: 65.4 us -> 39.7 us
    reduce_scatter x12 -> x2, waiting for transfers between devices: 600 us -> 0.01 us  [sum_plane(): lax.psum_scatter(part, ('dp', 'seq'), scatter_dimension=0, tiled=True)]
    all_gather x12 -> x1, waiting for transfers between devices: 379 us -> 0.01 us  [on_plane(): lax.all_gather(after(packed, in_pieces[3:5]), ('dp', 'seq'), axis=0, tile...]
    ppermute x0 -> x67, waiting for transfers between devices: none -> 194 us  [the longest x9 75.9 us: gather_line(): down = lax.ppermute(down, 'tp', [(i, i - 1) for i in range(1, 5 - t)])]
    dot_general x39 -> x0, matrix products: 160 us -> none  [the longest x7 50.1 us: project(): return jnp.dot(left, right, preferred_element_type=jnp.float32)]
    pallas_call x0 -> x17, Pallas kernels: none -> 138 us  [the longest x1 23.8 us: feed_forward_back(): pl.pallas_call(body, grid=(tiles,), in_specs=[pl.BlockSpec((rows, width),...]
    ppermute x0 -> x67, starting transfers between devices: none -> 125 us  [the longest x12 61 us: scatter_line(): up = lax.ppermute(up, 'tp', [(i, i + 1) for i in range(t)])]
    unnamed x32 -> x3, waiting for transfers between devices: 105 us -> 0.05 us
    all_gather x4 -> x0, blocking collectives: 73.9 us -> none  [the longest x1 23 us: on_device(): lax.all_gather(attn_gain, ('dp', 'seq'), axis=1, tiled=True)]
  transfers between devices with their start and end apart: 28 -> 74, of which waited for: 27 -> 32; matrix products, arithmetic and copies ran while one was open for 11% -> 8% of each run, Pallas kernels for 0% -> 16%
where the time goes in v2:
time: 672 us; the launch traced here: 661 us
  waiting for transfers between devices  207 us (31%)
  starting transfers between devices  141 us (21%)
  Pallas kernels  138 us (21%)
  blocking collectives  69.5 us (10%)
  other arithmetic  51.6 us (8%)
  local copies, waits for them, and re-layouts  39.7 us (6%)
  between operations  15.3 us (2%)
    ppermute x9, waiting for transfers between devices, gather_line(): down = lax.ppermute(down, 'tp', [(i, i - 1) for i in range(1, 5 - t)])  75.9 us
    ppermute x12, starting transfers between devices, scatter_line(): up = lax.ppermute(up, 'tp', [(i, i + 1) for i in range(t)])  61 us
    ppermute x12, waiting for transfers between devices, scatter_line(): up = lax.ppermute(up, 'tp', [(i, i + 1) for i in range(t)])  51.6 us
    ppermute x14, waiting for transfers between devices, to_neighbour(): return lax.ppermute(values, 'seq', [(i, i ^ flip) for i in range(4)])  36.9 us
    all_to_all x1, blocking collectives, on_plane(): part_grads = lax.all_to_all(part_grads, 'seq', 0, 0, tiled=True)  31.6 us
    unnamed x98, local copies, waits for them, and re-layouts  29.8 us
    pallas_call x1, Pallas kernels, feed_forward_back(): pl.pallas_call(body, grid=(tiles,), in_specs=[pl.BlockSpec((rows, width),...  23.8 us
    pallas_call x1, Pallas kernels, feed_forward(): pl.pallas_call(body, grid=(tiles,), in_specs=[fixed] * 7 + weight_tiles(w...  21.4 us
  transfers between devices with their start and end apart: 74, of which 32 were waited for; matrix products, arithmetic and copies ran while one was open for 8% of the time, Pallas kernels for 16%

profile of v2, /device:TPU:0, one launch (start us, length us, event | category | flops | bytes accessed | tf_op | source)
XLA Modules:
  0.0 661.5 jit_solution(3685263433656655108)
XLA Ops:
  35.2 9.0 %collective-permute-done.2.refs_3_ = bf16[128,1536]{1,0:T(8,128)(2,1)S(1)} collective-permute-done((bf16[128,1536]{1,0:T(8,128)(2,1)S(1)}, bf16[128,1536]{1,0:T(8,128)(2,1)S(1)}, u32[]{:S(2)}, u32[]{:S(2)}) %collective-permute-start.2) | collective-permute-done | bytes 393248 | tf_op jit(solution)/shard_map/ppermute | solution.py:408
  51.2 9.9 %project_in.1 = (f32[512,1536]{1,0:T(8,128)}, bf16[2048,1536]{1,0:T(8,128)(2,1)}) custom-call(s32[8]{0:T(128)S(1)} %iota_xor_fusion.order_ref, bf16[512,2048]{1,0:T(8,128)(2,1)} %bitcast.43, bf16[256,1536]{1,0:T(8,128)(2,1)S(1)} %constant_dynamic-update-slice_fusion.refs_0_, bf16[256,1536]{1,0:T(8,128)(2,1)S(1)} %collective-permute-done.refs_1_, ...), custom_call_target="tpu_custom_call" | custom-call | tf_op jit(solution)/shard_map/project_in/pallas_call | solution.py:472
  62.9 12.0 %psum.14 = f32[8,128]{1,0:T(8,128)S(1)} all-reduce(f32[8,128]{1,0:T(8,128)S(1)} %reshape.181), channel_id=1, replica_groups=mesh['dp'=2,'seq'=4,'tp'=4] {'tp'}, use_global_device_ids=true, to_apply=%region_2.3 | all-reduce | flops 1024 | bytes 8192 | tf_op jit(solution)/shard_map/psum | solution.py:622
  87.6 24.8 %collective-permute-done.11.refs_3_ = bf16[256,256]{1,0:T(8,128)(2,1)S(1)} collective-permute-done((bf16[256,256]{1,0:T(8,128)(2,1)S(1)}, bf16[256,256]{1,0:T(8,128)(2,1)S(1)}, u32[]{:S(2)}, u32[]{:S(2)}) %collective-permute-start.11) | collective-permute-done | bytes 131104 | tf_op jit(solution)/shard_map/ppermute | solution.py:408
  135.2 6.6 all-to-all-done.2.context_ref
  149.3 10.3 %collective-permute-done.18 = bf16[128,2048]{1,0:T(8,128)(2,1)S(1)} collective-permute-done((bf16[128,2048]{1,0:T(8,128)(2,1)S(1)}, bf16[128,2048]{1,0:T(8,128)(2,1)S(1)}, u32[]{:S(2)}, u32[]{:S(2)}) %collective-permute-start.18) | collective-permute-done | bytes 524320 | tf_op jit(solution)/shard_map/ppermute | solution.py:610
  165.2 9.4 %collective-permute-done.20 = bf16[128,2048]{1,0:T(8,128)(2,1)S(1)} collective-permute-done((bf16[128,2048]{1,0:T(8,128)(2,1)S(1)}, bf16[128,2048]{1,0:T(8,128)(2,1)S(1)}, u32[]{:S(2)}, u32[]{:S(2)}) %collective-permute-start.20) | collective-permute-done | bytes 524320 | tf_op jit(solution)/shard_map/ppermute | solution.py:610
  176.9 9.8 %collective-permute-start.22 = (bf16[128,2048]{1,0:T(8,128)(2,1)}, bf16[128,2048]{1,0:T(8,128)(2,1)}, u32[]{:S(2)}, u32[]{:S(2)}) collective-permute-start(bf16[128,2048]{1,0:T(8,128)(2,1)} %add_convert_fusion.10), channel_id=1, source_target_pairs={{0,1},{1,2},{2,3},{4,5},{5,6},{6,7},{8,9},{9,10},{10,11},{12,13},{... | collective-permute-start | bytes 1572872 | tf_op jit(solution)/shard_map/ppermute | solution.py:610
  203.0 7.1 %collective-permute-done.24.refs_1_ = bf16[128,2048]{1,0:T(8,128)(2,1)S(1)} collective-permute-done((bf16[128,2048]{1,0:T(8,128)(2,1)S(1)}, bf16[128,2048]{1,0:T(8,128)(2,1)S(1)}, u32[]{:S(2)}, u32[]{:S(2)}) %collective-permute-start.24) | collective-permute-done | bytes 524320 | tf_op jit(solution)/shard_map/ppermute | solution.py:596
  216.2 10.1 %collective-permute-done.28.refs_5_ = bf16[128,2048]{1,0:T(8,128)(2,1)S(1)} collective-permute-done((bf16[128,2048]{1,0:T(8,128)(2,1)S(1)}, bf16[128,2048]{1,0:T(8,128)(2,1)S(1)}, u32[]{:S(2)}, u32[]{:S(2)}) %collective-permute-start.28) | collective-permute-done | bytes 524320 | tf_op jit(solution)/shard_map/ppermute | solution.py:597
  228.6 8.9 %collective-permute-done.29.refs_6_ = bf16[128,2048]{1,0:T(8,128)(2,1)} collective-permute-done((bf16[128,2048]{1,0:T(8,128)(2,1)S(1)}, bf16[128,2048]{1,0:T(8,128)(2,1)}, u32[]{:S(2)}, u32[]{:S(2)}) %collective-permute-start.29) | collective-permute-done | bytes 524320 | tf_op jit(solution)/shard_map/ppermute | solution.py:597
  237.5 21.4 %feed_forward.1 = (bf16[512,2048]{1,0:T(8,128)(2,1)}, bf16[512,2048]{1,0:T(8,128)(2,1)}, bf16[512,2048]{1,0:T(8,128)(2,1)}, bf16[512,2048]{1,0:T(8,128)(2,1)}, b...) custom-call(bf16[128,2048]{1,0:T(8,128)(2,1)S(1)} %fusion.14.refs_0_, ...), custom_call_target="tpu_custom_call" | custom-call | tf_op jit(solution)/shard_map/feed_forward/pallas_call | solution.py:1012
  261.0 8.1 %collective-permute-done.30 = bf16[128,2048]{1,0:T(8,128)(2,1)S(1)} collective-permute-done((bf16[128,2048]{1,0:T(8,128)(2,1)S(1)}, bf16[128,2048]{1,0:T(8,128)(2,1)S(1)}, u32[]{:S(2)}, u32[]{:S(2)}) %collective-permute-start.30) | collective-permute-done | bytes 524320 | tf_op jit(solution)/shard_map/ppermute | solution.py:610
  283.6 12.5 %collective-permute-start.34 = (bf16[128,2048]{1,0:T(8,128)(2,1)}, bf16[128,2048]{1,0:T(8,128)(2,1)}, u32[]{:S(2)}, u32[]{:S(2)}) collective-permute-start(bf16[128,2048]{1,0:T(8,128)(2,1)} %add_convert_fusion.8), channel_id=1, source_target_pairs={{0,1},{1,2},{2,3},{4,5},{5,6},{6,7},{8,9},{9,10},{10,11},{12,13},{... | collective-permute-start | bytes 1572872 | tf_op jit(solution)/shard_map/ppermute | solution.py:610
  325.0 6.8 %collective-permute-done.39.refs_4_ = bf16[128,2048]{1,0:T(8,128)(2,1)S(1)} collective-permute-done((bf16[128,2048]{1,0:T(8,128)(2,1)S(1)}, bf16[128,2048]{1,0:T(8,128)(2,1)S(1)}, u32[]{:S(2)}, u32[]{:S(2)}) %collective-permute-start.39) | collective-permute-done | bytes 524320 | tf_op jit(solution)/shard_map/ppermute | solution.py:597
  333.8 9.1 %collective-permute-done.40.refs_5_ = bf16[128,2048]{1,0:T(8,128)(2,1)S(1)} collective-permute-done((bf16[128,2048]{1,0:T(8,128)(2,1)S(1)}, bf16[128,2048]{1,0:T(8,128)(2,1)S(1)}, u32[]{:S(2)}, u32[]{:S(2)}) %collective-permute-start.40) | collective-permute-done | bytes 524320 | tf_op jit(solution)/shard_map/ppermute | solution.py:597
  344.2 9.8 %collective-permute-done.41.refs_6_ = bf16[128,2048]{1,0:T(8,128)(2,1)S(1)} collective-permute-done((bf16[128,2048]{1,0:T(8,128)(2,1)S(1)}, bf16[128,2048]{1,0:T(8,128)(2,1)S(1)}, u32[]{:S(2)}, u32[]{:S(2)}) %collective-permute-start.41) | collective-permute-done | bytes 524320 | tf_op jit(solution)/shard_map/ppermute | solution.py:597
  353.9 8.4 %down_grad.1 = (bf16[512,2048]{1,0:T(8,128)(2,1)}, bf16[2048,2048]{1,0:T(8,128)(2,1)}) custom-call(bf16[128,2048]{1,0:T(8,128)(2,1)S(1)} %get-tuple-element.284.refs_0_, bf16[128,2048]{1,0:T(8,128)(2,1)S(1)} %collective-permute-done.36.refs_1_, bf16[128,2048]{1,0:T(8,128)(2,1)S(1)} %collective-permute-done.37.refs_2_, ...), custom_call_target="tpu_custom_call" | custom-call | tf_op jit(solution)/shard_map/down_grad/pallas_call | solution.py:1091
  362.6 23.8 %feed_forward_back.1 = (bf16[512,2048]{1,0:T(8,128)(2,1)}, bf16[512,2048]{1,0:T(8,128)(2,1)}, bf16[128,2048]{1,0:T(8,128)(2,1)S(1)}, bf16[128,2048]{1,0:T(8,128)...) custom-call(bf16[512,2048]{1,0:T(8,128)(2,1)} %get-tuple-element.152.rows_ref, ...), custom_call_target="tpu_custom_call" | custom-call | tf_op jit(solution)/shard_map/feed_forward_back/pallas_call | solution.py:1061
  388.4 8.4 %weight_grad.2.refs_0_ = bf16[2048,4096]{1,0:T(8,128)(2,1)} custom-call(bf16[512,2048]{1,0:T(8,128)(2,1)S(1)} %copy-done.3, bf16[512,2048]{1,0:T(8,128)(2,1)} %get-tuple-element.160.right_ref), custom_call_target="tpu_custom_call" | custom-call | tf_op jit(solution)/shard_map/weight_grad/pallas_call | solution.py:1118
  408.9 7.7 %collective-permute-start.46 = (bf16[128,2048]{1,0:T(8,128)(2,1)}, bf16[128,2048]{1,0:T(8,128)(2,1)}, u32[]{:S(2)}, u32[]{:S(2)}) collective-permute-start(bf16[128,2048]{1,0:T(8,128)(2,1)} %add_convert_fusion.5), channel_id=1, source_target_pairs={{0,1},{1,2},{2,3},{4,5},{5,6},{6,7},{8,9},{9,10},{10,11},{12,13},{... | collective-permute-start | bytes 1572872 | tf_op jit(solution)/shard_map/ppermute | solution.py:610
  416.6 8.4 %weight_grad.3 = bf16[2048,4096]{1,0:T(8,128)(2,1)} custom-call(bf16[512,2048]{1,0:T(8,128)(2,1)S(1)} %copy-done.3, bf16[512,2048]{1,0:T(8,128)(2,1)} %get-tuple-element.165.right_ref, bf16[2048,4096]{1,0:T(8,128)(2,1)} %weight_grad.2.refs_0_), custom_call_target="tpu_custom_call", output_to_operand_aliasing={{}: (2, {})} | custom-call | tf_op jit(solution)/shard_map/weight_grad/pallas_call | solution.py:1118
  442.3 9.0 %collective-permute-done.51.refs_4_ = bf16[128,2048]{1,0:T(8,128)(2,1)S(1)} collective-permute-done((bf16[128,2048]{1,0:T(8,128)(2,1)S(1)}, bf16[128,2048]{1,0:T(8,128)(2,1)S(1)}, u32[]{:S(2)}, u32[]{:S(2)}) %collective-permute-start.51) | collective-permute-done | bytes 524320 | tf_op jit(solution)/shard_map/ppermute | solution.py:597
  453.4 9.1 %collective-permute-done.52.refs_5_ = bf16[128,2048]{1,0:T(8,128)(2,1)S(1)} collective-permute-done((bf16[128,2048]{1,0:T(8,128)(2,1)S(1)}, bf16[128,2048]{1,0:T(8,128)(2,1)S(1)}, u32[]{:S(2)}, u32[]{:S(2)}) %collective-permute-start.52) | collective-permute-done | bytes 524320 | tf_op jit(solution)/shard_map/ppermute | solution.py:597
  463.7 9.8 %collective-permute-done.53.refs_6_ = bf16[128,2048]{1,0:T(8,128)(2,1)S(1)} collective-permute-done((bf16[128,2048]{1,0:T(8,128)(2,1)S(1)}, bf16[128,2048]{1,0:T(8,128)(2,1)S(1)}, u32[]{:S(2)}, u32[]{:S(2)}) %collective-permute-start.53) | collective-permute-done | bytes 524320 | tf_op jit(solution)/shard_map/ppermute | solution.py:597
  478.5 17.6 %all_to_all.38.grad_ref = bf16[4,2,256,128]{3,2,1,0:T(8,128)(2,1)S(1)} all-to-all(bf16[4,2,256,128]{3,2,1,0:T(8,128)(2,1)S(1)} %get-tuple-element.168), channel_id=1, replica_groups=mesh['dp'=2,'seq'=4,'tp'=4] {'seq'}, dimensions={0} | all-to-all | bytes 1048576 | tf_op jit(solution)/shard_map/all_to_all | solution.py:1261
  496.1 7.0 %attend_back.1 = bf16[4,3,2,256,128]{4,3,2,1,0:T(8,128)(2,1)S(1)} custom-call(bf16[4,3,2,256,128]{4,3,2,1,0:T(8,128)(2,1)} %copy-done, bf16[4,2,256,128]{3,2,1,0:T(8,128)(2,1)S(1)} %all_to_all.38.grad_ref, f32[4,2,256,1]{3,2,1,0:T(8,128)S(1)} %copy-done.6), custom_call_target="tpu_custom_call" | custom-call | tf_op jit(solution)/shard_map/attend_back/pallas_call | solution.py:753
  503.1 31.6 %all_to_all.39.grad_ref = bf16[4,3,2,256,128]{4,3,2,1,0:T(8,128)(2,1)S(1)} all-to-all(bf16[4,3,2,256,128]{4,3,2,1,0:T(8,128)(2,1)S(1)} %attend_back.1), channel_id=1, replica_groups=mesh['dp'=2,'seq'=4,'tp'=4] {'seq'}, dimensions={0} | all-to-all | bytes 3145728 | tf_op jit(solution)/shard_map/all_to_all | solution.py:1263
  540.3 8.4 %psum.15 = f32[8,128]{1,0:T(8,128)S(1)} all-reduce(f32[8,128]{1,0:T(8,128)S(1)} %reshape_reshape.3), channel_id=1, replica_groups=mesh['dp'=2,'seq'=4,'tp'=4] {'tp'}, use_global_device_ids=true, to_apply=%region_7.8 | all-reduce | flops 1024 | bytes 8192 | tf_op jit(solution)/shard_map/psum | solution.py:622
  549.0 9.7 %project_in_back.1 = (bf16[512,1536]{1,0:T(8,128)(2,1)}, bf16[128,2048]{1,0:T(8,128)(2,1)S(1)}, bf16[128,2048]{1,0:T(8,128)(2,1)S(1)}, bf16[128,2048]{1,0:T(8,128)(2,1)S(1)}, bf16[128,2048]{1,0:T(8,128)(2,1)S(1)}) custom-call(s32[4]{0:T(128)S(1)} %and_select_fusion.slots_ref, bf16[4,3,2,256,128]{4,3,2,1,0:T(8,128)(2,1)} %copy-done.1, ...), custom_call_target="tpu_custom_call" | custom-call | tf_op jit(solution)/shard_map/project_in_back/pallas_call | solution.py:937
  561.0 6.3 grad_blocks.3
  594.6 7.0 %grad_blocks.5 = (bf16[128,2048]{1,0:T(8,128)(2,1)}, bf16[128,2048]{1,0:T(8,128)(2,1)S(1)}, bf16[128,2048]{1,0:T(8,128)(2,1)S(1)}, bf16[128,2048]{1,0:T(8,128)(2...) custom-call(s32[8]{0:T(128)S(1)} %iota_xor_fusion.order_ref, bf16[512,2048]{1,0:T(8,128)(2,1)} %bitcast.46, ...), custom_call_target="tpu_custom_call" | custom-call | tf_op jit(solution)/shard_map/grad_blocks/pallas_call | solution.py:546
  (328 shorter events, 288.8 us)
Async XLA Ops:
  10.1 22.9 %collective-permute-start = (bf16[256,1536]{1,0:T(8,128)(2,1)S(1)}, bf16[256,1536]{1,0:T(8,128)(2,1)S(1)}, u32[]{:S(2)}, u32[]{:S(2)}) collective-permute-start(bf16[256,1536]{1,0:T(8,128)(2,1)S(1)} %constant_dynamic-update-slice_fusion.refs_0_), channel_id=1, source_target_pairs={{0,4},{4,0},{8,12},{12,8},{1,5},{5,1},{9,13},{13,9},{2,6},{6,2},{1... | collective-permute-start | bytes 2359304 | tf_op jit(solution)/shard_map/ppermute | solution.py:408
  13.1 19.9 %collective-permute-start.1 = (bf16[256,1536]{1,0:T(8,128)(2,1)S(1)}, bf16[256,1536]{1,0:T(8,128)(2,1)S(1)}, u32[]{:S(2)}, u32[]{:S(2)}) collective-permute-start(bf16[256,1536]{1,0:T(8,128)(2,1)S(1)} %constant_dynamic-update-slice_fusion.refs_0_), channel_id=1, source_target_pairs={{0,8},{4,12},{8,0},{12,4},{1,9},{5,13},{9,1},{13,5},{2,10},{6,14},... | collective-permute-start | bytes 2359304 | tf_op jit(solution)/shard_map/ppermute | solution.py:408
  17.4 14.9 %all-to-all-start = ((bf16[8,2,320]{2,1,0:T(2,128)(2,1)}), bf16[8,2,320]{2,1,0:T(2,128)(2,1)S(1)}, u32[]{:S(2)}, u32[]{:S(2)}) async-start(bf16[8,2,320]{2,1,0:T(2,128)(2,1)} %reshape.210), calls=%async_computation | async-start | bytes 24576 | tf_op jit(solution)/shard_map/all_to_all | solution.py:1162
  20.7 216.8 %all-gather.2.cloned.1.call-start = ((), (), s32[]{:S(2)}) async-start(), calls=%async_computation.8 | async-start | bytes 28311552 | tf_op jit(solution)/shard_map/all_gather | solution.py:1192
  48.8 26.0 %collective-permute-start.9 = (bf16[512,256]{1,0:T(8,128)(2,1)}, bf16[512,256]{1,0:T(8,128)(2,1)S(1)}, u32[]{:S(2)}, u32[]{:S(2)}) collective-permute-start(bf16[512,256]{1,0:T(8,128)(2,1)} %refs_0_), channel_id=1, source_target_pairs={{0,4},{4,0},{8,12},{12,8},{1,5},{5,1},{9,13},{13,9},{2,6},{6,2},{1... | collective-permute-start | bytes 786440 | tf_op jit(solution)/shard_map/ppermute | solution.py:408
  49.7 25.1 %collective-permute-start.10 = (bf16[512,256]{1,0:T(8,128)(2,1)}, bf16[512,256]{1,0:T(8,128)(2,1)S(1)}, u32[]{:S(2)}, u32[]{:S(2)}) collective-permute-start(bf16[512,256]{1,0:T(8,128)(2,1)} %refs_0_), channel_id=1, source_target_pairs={{0,8},{4,12},{8,0},{12,4},{1,9},{5,13},{9,1},{13,5},{2,10},{6,14},... | collective-permute-start | bytes 786440 | tf_op jit(solution)/shard_map/ppermute | solution.py:408
  79.9 37.1 %all-to-all-start.1 = ((bf16[4,3,2,256,128]{4,3,2,1,0:T(8,128)(2,1)}), bf16[4,3,2,256,128]{4,3,2,1,0:T(8,128)(2,1)S(1)}, u32[]{:S(2)}, u32[]{:S(2)}) async-start(bf16[4,3,2,256,128]{4,3,2,1,0:T(8,128)(2,1)} %copy-done.4), calls=%async_computation.1 | async-start | bytes 3145728 | tf_op jit(solution)/shard_map/all_to_all | solution.py:1205
  83.5 30.1 %collective-permute-start.13 = (bf16[512,256]{1,0:T(8,128)(2,1)}, bf16[512,256]{1,0:T(8,128)(2,1)S(1)}, u32[]{:S(2)}, u32[]{:S(2)}) collective-permute-start(bf16[512,256]{1,0:T(8,128)(2,1)} %refs_0_), channel_id=1, source_target_pairs={{0,16},{16,0},{1,17},{17,1},{2,18},{18,2},{3,19},{19,3},{4,20},{20... | collective-permute-start | bytes 786440 | tf_op jit(solution)/shard_map/ppermute | solution.py:412
  83.6 30.7 %collective-permute-start.14 = (bf16[512,256]{1,0:T(8,128)(2,1)S(1)}, bf16[512,256]{1,0:T(8,128)(2,1)S(1)}, u32[]{:S(2)}, u32[]{:S(2)}) collective-permute-start(bf16[512,256]{1,0:T(8,128)(2,1)S(1)} %collective-permute-done.9.refs_1_), channel_id=1, source_target_pairs={{0,16},{16,0},{1,17},{17,1},{2,18},{18,2},{3,19},{19,3},{4,20},{20... | collective-permute-start | bytes 786440 | tf_op jit(solution)/shard_map/ppermute | solution.py:412
  84.1 28.2 %collective-permute-start.11 = (bf16[256,256]{1,0:T(8,128)(2,1)S(1)}, bf16[256,256]{1,0:T(8,128)(2,1)S(1)}, u32[]{:S(2)}, u32[]{:S(2)}) collective-permute-start(bf16[256,256]{1,0:T(8,128)(2,1)S(1)} %slice.113), channel_id=1, source_target_pairs={{0,4},{4,0},{8,12},{12,8},{1,5},{5,1},{9,13},{13,9},{2,6},{6,2},{1... | collective-permute-start | bytes 393224 | tf_op jit(solution)/shard_map/ppermute | solution.py:408
  86.1 28.8 %collective-permute-start.15 = (bf16[512,256]{1,0:T(8,128)(2,1)S(1)}, bf16[512,256]{1,0:T(8,128)(2,1)S(1)}, u32[]{:S(2)}, u32[]{:S(2)}) collective-permute-start(bf16[512,256]{1,0:T(8,128)(2,1)S(1)} %collective-permute-done.10.refs_2_), channel_id=1, source_target_pairs={{0,16},{16,0},{1,17},{17,1},{2,18},{18,2},{3,19},{19,3},{4,20},{20... | collective-permute-start | bytes 786440 | tf_op jit(solution)/shard_map/ppermute | solution.py:412
  86.1 26.7 %collective-permute-start.12 = (bf16[256,256]{1,0:T(8,128)(2,1)S(1)}, bf16[256,256]{1,0:T(8,128)(2,1)S(1)}, u32[]{:S(2)}, u32[]{:S(2)}) collective-permute-start(bf16[256,256]{1,0:T(8,128)(2,1)S(1)} %slice.114), channel_id=1, source_target_pairs={{0,8},{4,12},{8,0},{12,4},{1,9},{5,13},{9,1},{13,5},{2,10},{6,14},... | collective-permute-start | bytes 393224 | tf_op jit(solution)/shard_map/ppermute | solution.py:408
  123.5 18.2 %all-to-all-start.2 = ((bf16[4,2,256,128]{3,2,1,0:T(8,128)(2,1)}), bf16[4,2,256,128]{3,2,1,0:T(8,128)(2,1)S(1)}, u32[]{:S(2)}, u32[]{:S(2)}) async-start(bf16[4,2,256,128]{3,2,1,0:T(8,128)(2,1)} %copy-done.8), calls=%async_computation.2 | async-start | bytes 1048576 | tf_op jit(solution)/shard_map/all_to_all | solution.py:1209
  127.0 507.3 %reduce-scatter.5.cloned.1.call-start = ((), (), s32[]{:S(2)}) async-start(), calls=%async_computation.10 | async-start | bytes 9437184 | tf_op jit(solution)/shard_map/reduce_scatter | solution.py:1238
  174.7 18.4 %collective-permute-start.23 = (bf16[128,2048]{1,0:T(8,128)(2,1)S(1)}, bf16[128,2048]{1,0:T(8,128)(2,1)}, u32[]{:S(2)}, u32[]{:S(2)}) collective-permute-start(bf16[128,2048]{1,0:T(8,128)(2,1)S(1)} %add_convert_fusion.9), channel_id=1, source_target_pairs={{1,0},{2,1},{3,2},{5,4},{6,5},{7,6},{9,8},{10,9},{11,10},{13,12},{... | collective-permute-start | bytes 1572872 | tf_op jit(solution)/shard_map/ppermute | solution.py:611
  176.9 18.5 %collective-permute-start.22 = (bf16[128,2048]{1,0:T(8,128)(2,1)}, bf16[128,2048]{1,0:T(8,128)(2,1)}, u32[]{:S(2)}, u32[]{:S(2)}) collective-permute-start(bf16[128,2048]{1,0:T(8,128)(2,1)} %add_convert_fusion.10), channel_id=1, source_target_pairs={{0,1},{1,2},{2,3},{4,5},{5,6},{6,7},{8,9},{9,10},{10,11},{12,13},{... | collective-permute-start | bytes 1572872 | tf_op jit(solution)/shard_map/ppermute | solution.py:610
  281.4 18.4 %collective-permute-start.35 = (bf16[128,2048]{1,0:T(8,128)(2,1)}, bf16[128,2048]{1,0:T(8,128)(2,1)}, u32[]{:S(2)}, u32[]{:S(2)}) collective-permute-start(bf16[128,2048]{1,0:T(8,128)(2,1)} %add_convert_fusion.7), channel_id=1, source_target_pairs={{1,0},{2,1},{3,2},{5,4},{6,5},{7,6},{9,8},{10,9},{11,10},{13,12},{... | collective-permute-start | bytes 1572872 | tf_op jit(solution)/shard_map/ppermute | solution.py:611
  283.6 22.1 %collective-permute-start.34 = (bf16[128,2048]{1,0:T(8,128)(2,1)}, bf16[128,2048]{1,0:T(8,128)(2,1)}, u32[]{:S(2)}, u32[]{:S(2)}) collective-permute-start(bf16[128,2048]{1,0:T(8,128)(2,1)} %add_convert_fusion.8), channel_id=1, source_target_pairs={{0,1},{1,2},{2,3},{4,5},{5,6},{6,7},{8,9},{9,10},{10,11},{12,13},{... | collective-permute-start | bytes 1572872 | tf_op jit(solution)/shard_map/ppermute | solution.py:610
  362.3 274.7 %reduce-scatter.3.cloned.1.call-start = ((), (), s32[]{:S(2)}) async-start(), calls=%async_computation.9 | async-start | bytes 18874368 | tf_op jit(solution)/shard_map/reduce_scatter | solution.py:1238
  406.7 18.8 %collective-permute-start.47 = (bf16[128,2048]{1,0:T(8,128)(2,1)}, bf16[128,2048]{1,0:T(8,128)(2,1)}, u32[]{:S(2)}, u32[]{:S(2)}) collective-permute-start(bf16[128,2048]{1,0:T(8,128)(2,1)} %add_convert_fusion.4), channel_id=1, source_target_pairs={{1,0},{2,1},{3,2},{5,4},{6,5},{7,6},{9,8},{10,9},{11,10},{13,12},{... | collective-permute-start | bytes 1572872 | tf_op jit(solution)/shard_map/ppermute | solution.py:611
  408.9 16.6 %collective-permute-start.46 = (bf16[128,2048]{1,0:T(8,128)(2,1)}, bf16[128,2048]{1,0:T(8,128)(2,1)}, u32[]{:S(2)}, u32[]{:S(2)}) collective-permute-start(bf16[128,2048]{1,0:T(8,128)(2,1)} %add_convert_fusion.5), channel_id=1, source_target_pairs={{0,1},{1,2},{2,3},{4,5},{5,6},{6,7},{8,9},{9,10},{10,11},{12,13},{... | collective-permute-start | bytes 1572872 | tf_op jit(solution)/shard_map/ppermute | solution.py:610
  435.0 16.4 %collective-permute-start.51 = (bf16[128,2048]{1,0:T(8,128)(2,1)S(1)}, bf16[128,2048]{1,0:T(8,128)(2,1)S(1)}, u32[]{:S(2)}, u32[]{:S(2)}) collective-permute-start(bf16[128,2048]{1,0:T(8,128)(2,1)S(1)} %multiply_convert_fusion.refs_0_), channel_id=1, source_target_pairs={{1,0},{2,1},{3,2},{5,4},{6,5},{7,6},{9,8},{10,9},{11,10},{13,12},{... | collective-permute-start | bytes 1572872 | tf_op jit(solution)/shard_map/ppermute | solution.py:597
  567.2 15.9 %collective-permute-start.54 = (bf16[128,2048]{1,0:T(8,128)(2,1)S(1)}, bf16[128,2048]{1,0:T(8,128)(2,1)S(1)}, u32[]{:S(2)}, u32[]{:S(2)}) collective-permute-start(bf16[128,2048]{1,0:T(8,128)(2,1)S(1)} %get-tuple-element.176), channel_id=1, source_target_pairs={{0,1},{4,5},{8,9},{12,13},{16,17},{20,21},{24,25},{28,29}} | collective-permute-start | bytes 1572872 | tf_op jit(solution)/shard_map/ppermute | solution.py:610
  584.4 17.2 %collective-permute-start.57 = (bf16[128,2048]{1,0:T(8,128)(2,1)}, bf16[128,2048]{1,0:T(8,128)(2,1)}, u32[]{:S(2)}, u32[]{:S(2)}) collective-permute-start(bf16[128,2048]{1,0:T(8,128)(2,1)} %get-tuple-element.295), channel_id=1, source_target_pairs={{0,1},{1,2},{4,5},{5,6},{8,9},{9,10},{12,13},{13,14},{16,17},{17,1... | collective-permute-start | bytes 1572872 | tf_op jit(solution)/shard_map/ppermute | solution.py:610
  593.0 23.0 %collective-permute-start.62 = (bf16[128,2048]{1,0:T(8,128)(2,1)}, bf16[128,2048]{1,0:T(8,128)(2,1)}, u32[]{:S(2)}, u32[]{:S(2)}) collective-permute-start(bf16[128,2048]{1,0:T(8,128)(2,1)} %get-tuple-element.195), channel_id=1, source_target_pairs={{0,8},{4,12},{8,0},{12,4},{1,9},{5,13},{9,1},{13,5},{2,10},{6,14},... | collective-permute-start | bytes 1572872 | tf_op jit(solution)/shard_map/ppermute | solution.py:408
  594.5 28.4 %collective-permute-start.64 = (bf16[128,2048]{1,0:T(8,128)(2,1)}, bf16[128,2048]{1,0:T(8,128)(2,1)}, u32[]{:S(2)}, u32[]{:S(2)}) collective-permute-start(bf16[128,2048]{1,0:T(8,128)(2,1)} %get-tuple-element.197), channel_id=1, source_target_pairs={{0,4},{4,0},{8,12},{12,8},{1,5},{5,1},{9,13},{13,9},{2,6},{6,2},{1... | collective-permute-start | bytes 1572872 | tf_op jit(solution)/shard_map/ppermute | solution.py:408
  603.8 25.3 %collective-permute-start.60 = (bf16[128,2048]{1,0:T(8,128)(2,1)}, bf16[128,2048]{1,0:T(8,128)(2,1)}, u32[]{:S(2)}, u32[]{:S(2)}) collective-permute-start(bf16[128,2048]{1,0:T(8,128)(2,1)} %add_convert_fusion.2), channel_id=1, source_target_pairs={{1,0},{2,1},{3,2},{5,4},{6,5},{7,6},{9,8},{10,9},{11,10},{13,12},{... | collective-permute-start | bytes 1572872 | tf_op jit(solution)/shard_map/ppermute | solution.py:611
  607.2 35.6 %collective-permute-start.66 = (bf16[128,2048]{1,0:T(8,128)(2,1)}, bf16[128,2048]{1,0:T(8,128)(2,1)}, u32[]{:S(2)}, u32[]{:S(2)}) collective-permute-start(bf16[128,2048]{1,0:T(8,128)(2,1)} %get-tuple-element.203), channel_id=1, source_target_pairs={{0,8},{4,12},{8,0},{12,4},{1,9},{5,13},{9,1},{13,5},{2,10},{6,14},... | collective-permute-start | bytes 1572872 | tf_op jit(solution)/shard_map/ppermute | solution.py:408
  609.1 35.9 %collective-permute-start.61 = (bf16[128,2048]{1,0:T(8,128)(2,1)}, bf16[128,2048]{1,0:T(8,128)(2,1)}, u32[]{:S(2)}, u32[]{:S(2)}) collective-permute-start(bf16[128,2048]{1,0:T(8,128)(2,1)} %get-tuple-element.193), channel_id=1, source_target_pairs={{0,4},{4,0},{8,12},{12,8},{1,5},{5,1},{9,13},{13,9},{2,6},{6,2},{1... | collective-permute-start | bytes 1572872 | tf_op jit(solution)/shard_map/ppermute | solution.py:408
  610.3 16.0 %all-to-all-start.5 = ((f32[32,1,256]{2,1,0:T(1,128)}), f32[32,1,256]{2,1,0:T(1,128)S(1)}, u32[]{:S(2)}, u32[]{:S(2)}) async-start(f32[32,1,256]{2,1,0:T(1,128)} %all_to_all.30), calls=%async_computation.7 | async-start | bytes 65536 | tf_op jit(solution)/shard_map/all_to_all | solution.py:1297
  616.0 15.5 %collective-permute-start.59 = (bf16[128,2048]{1,0:T(8,128)(2,1)}, bf16[128,2048]{1,0:T(8,128)(2,1)}, u32[]{:S(2)}, u32[]{:S(2)}) collective-permute-start(bf16[128,2048]{1,0:T(8,128)(2,1)} %add_convert_fusion.3), channel_id=1, source_target_pairs={{0,1},{1,2},{2,3},{4,5},{5,6},{6,7},{8,9},{9,10},{10,11},{12,13},{... | collective-permute-start | bytes 1572872 | tf_op jit(solution)/shard_map/ppermute | solution.py:610
  622.9 18.3 %collective-permute-start.63 = (bf16[128,2048]{1,0:T(8,128)(2,1)}, bf16[128,2048]{1,0:T(8,128)(2,1)S(1)}, u32[]{:S(2)}, u32[]{:S(2)}) collective-permute-start(bf16[128,2048]{1,0:T(8,128)(2,1)} %add_convert_fusion.1), channel_id=1, source_target_pairs={{0,4},{4,0},{8,12},{12,8},{1,5},{5,1},{9,13},{13,9},{2,6},{6,2},{1... | collective-permute-start | bytes 1572872 | tf_op jit(solution)/shard_map/ppermute | solution.py:408
  (87 other events, 787.0 us)
Sparse Core Ops, SparseCore 0:
  45.4 150.8 all-gather.1
  362.4 68.8 reduce-scatter.4
  435.3 133.7 reduce-scatter.2

commit v3 on v2

--- a/solution.py
+++ b/solution.py
@@ -423,10 +423,10 @@
 def gather_plane(shard, firsts, meanwhile=()):
     half = shard.shape[0] // 2
     (from_one, from_two), meanwhile = lax.optimization_barrier((firsts, meanwhile))
-    far_low = to_neighbour(from_two[:half], 1)
-    far_high = to_neighbour(from_one[half:], 2)
-    mine = [shard, from_one, from_two, far_low, far_high]
-    return mine + [to_core(piece) for piece in mine], meanwhile
+    far = [to_neighbour(from_two[:half], 1), to_neighbour(from_one[half:], 2)]
+    near = [shard, from_one, from_two]
+    far, other = lax.optimization_barrier((far, [to_core(piece) for piece in near]))
+    return near + far + other + [to_core(piece) for piece in far], meanwhile
 
 
 def place_piece(out_ref, order_ref, k, piece, axis):
@@ -490,39 +490,52 @@
     )(order, rows_low, *pieces)
 
 
-def grad_blocks(lefts, rights, groups, order, blocks, received=None):
+def grad_blocks(lefts, rights, extra, order, blocks, received=None, far=None):
     rows, d_model = lefts[0].shape
     block = d_model // 8
     half = block // 2
     count = len(blocks)
-    width = sum(rights[right].shape[1] for _, right in groups[0])
+    width = sum(right.shape[1] for right in rights) + extra.shape[1]
     fresh = received is None
 
     def body(order_ref, *refs):
         left_refs, right_refs = refs[: len(lefts)], refs[len(lefts) : len(lefts) + len(rights)]
-        rest = refs[len(lefts) + len(rights) :]
-        for k, pairs in enumerate(groups):
-
-            @pl.when(pl.program_id(1) == k)
-            def _(pairs=pairs):
-                first = 0
-                for left, right in pairs:
-                    total = contract(left_refs[left][...], right_refs[right][...], 0, 0)
-                    columns = slice(first, first + total.shape[1])
-                    first += total.shape[1]
-                    if fresh:
-                        rest[0][:, columns] = total.astype(LOW)
-                        continue
-                    total = (total + rest[0][:, columns].astype(jnp.float32)).astype(LOW)
-                    for b in range(count):
-
-                        @pl.when(pl.program_id(0) == b)
-                        def _(total=total, columns=columns, b=b):
-                            rest[1 + 2 * b][:, columns] = total[:half]
-                            rest[2 + 2 * b][:, columns] = total[half:]
-
-    def chosen(b, j, k):
-        return jnp.where(j == b, k, jnp.where(j < b, 0, len(groups) - 1))
+        extra_ref, rest = refs[len(lefts) + len(rights)], refs[len(lefts) + len(rights) + 1 :]
+        first = 0
+        for k in range(len(lefts) + 1):
+            if k < len(lefts):
+                total = contract(left_refs[k][...], right_refs[k][...], 0, 0)
+            else:
+                total = extra_ref[...]
+            columns = slice(first, first + total.shape[1])
+            first += total.shape[1]
+            if fresh:
+                rest[0][:, columns] = total.astype(LOW)
+                continue
+            total = total + rest[0][:, columns].astype(jnp.float32)
+            if far is None:
+                rest[1][:, columns] = total[:half].astype(LOW)
+                rest[2][:, columns] = total[half:].astype(LOW)
+                continue
+            low, high, outs = rest[1], rest[2], rest[3:]
+
+            @pl.when(pl.program_id(0) == 0)
+            def _(total=total, columns=columns):
+                outs[0][:half, columns] = total[:half].astype(LOW)
+                outs[0][half:, columns] = (
+                    total[half:] + high[:, columns].astype(jnp.float32)
+                ).astype(LOW)
+
+            @pl.when(pl.program_id(0) == 1)
+            def _(total=total, columns=columns):
+                outs[1][:half, columns] = (
+                    total[:half] + low[:, columns].astype(jnp.float32)
+                ).astype(LOW)
+                outs[1][half:, columns] = total[half:].astype(LOW)
+
+            @pl.when(pl.program_id(0) == 2)
+            def _(total=total, columns=columns):
+                outs[2][:, columns] = total.astype(LOW)
 
     def pick(j):
         value = blocks[0]
@@ -530,63 +543,44 @@
             value = jnp.where(j > i, entry, value)
         return value
 
-    in_specs = [pl.BlockSpec((rows, block), lambda j, k, o: (0, o[pick(j)])) for _ in lefts]
-    in_specs += [pl.BlockSpec(right.shape, lambda j, k, o: (0, 0)) for right in rights]
+    def fixed(height):
+        return pl.BlockSpec((height, width), lambda j, o: (0, 0))
+
+    in_specs = [pl.BlockSpec((rows, block), lambda j, o: (0, o[pick(j)])) for _ in lefts]
+    in_specs += [pl.BlockSpec(right.shape, lambda j, o: (0, 0)) for right in rights]
+    in_specs.append(pl.BlockSpec((block, extra.shape[1]), lambda j, o: (o[pick(j)], 0)))
+    more = ()
     if fresh:
-        out_specs = [pl.BlockSpec((block, width), lambda j, k, o: (j, k))]
-        out_shape = [jax.ShapeDtypeStruct((count * block, len(groups) * width), LOW)]
+        out_specs = [pl.BlockSpec((block, width), lambda j, o: (j, 0))]
+        out_shape = [jax.ShapeDtypeStruct((count * block, width), LOW)]
     else:
-        in_specs.append(pl.BlockSpec((block, width), lambda j, k, o: (pick(j), k)))
-        out_specs = [
-            pl.BlockSpec((half, width), lambda j, k, o, b=b: (0, chosen(b, j, k)))
-            for b in range(count)
-            for _ in range(2)
-        ]
-        out_shape = [jax.ShapeDtypeStruct((half, len(groups) * width), LOW)] * (2 * count)
+        in_specs.append(pl.BlockSpec((block, width), lambda j, o: (pick(j), 0)))
+        more = (received,)
+        if far is None:
+            out_specs = [fixed(half)] * 2
+            out_shape = [jax.ShapeDtypeStruct((half, width), LOW)] * 2
+        else:
+            more += tuple(far)
+            in_specs += [fixed(half)] * 2
+            out_specs = [fixed(block)] * 3
+            out_shape = [jax.ShapeDtypeStruct((block, width), LOW)] * 3
     return pl.pallas_call(
         body,
         grid_spec=pltpu.PrefetchScalarGridSpec(
-            num_scalar_prefetch=1, grid=(count, len(groups)), in_specs=in_specs, out_specs=out_specs
+            num_scalar_prefetch=1, grid=(count,), in_specs=in_specs, out_specs=out_specs
         ),
         out_shape=out_shape,
         compiler_params=PARAMS,
         name="grad_blocks",
-    )(order, *lefts, *rights, *(() if fresh else (received,)))
-
-
-def add_low(mine, got):
-    return (mine.astype(jnp.float32) + got.astype(jnp.float32)).astype(LOW)
-
-
-def sum_in_core(lefts, rights, groups, order):
-    (sent,) = grad_blocks(lefts, rights, groups, order, (4, 5, 6, 7))
+    )(order, *lefts, *rights, extra, *more)
+
+
+def sum_in_plane(*parts):
+    (sent,) = grad_blocks(*parts, (4, 5, 6, 7))
     received = to_core(sent)
-    far = grad_blocks(lefts, rights, groups, order, (3,), received)
-    near = grad_blocks(lefts, rights, groups, order, (1, 2, 0), received)
-    return far, near
-
-
-def send_first(far, near):
-    one_low, _, _, two_high, _, _ = near
-    return [to_neighbour(far[0], 1), to_neighbour(far[1], 2)], [
-        to_neighbour(one_low, 1),
-        to_neighbour(two_high, 2),
-    ]
-
-
-def send_second(far, near):
-    return [
-        to_neighbour(add_low(near[1], far[1]), 1),
-        to_neighbour(add_low(near[2], far[0]), 2),
-    ]
-
-
-def halves_total(near, first, second):
-    def total(*values):
-        low, one, two = (value.astype(jnp.float32) for value in values)
-        return low + one + two
-
-    return total(near[4], first[0], second[1]), total(near[5], second[0], first[1])
+    sent = grad_blocks(*parts, (3,), received)
+    far = [to_neighbour(sent[0], 1), to_neighbour(sent[1], 2)]
+    return sent, grad_blocks(*parts, (1, 2, 0), received, far)
 
 
 def gather_line(own):
@@ -613,8 +607,7 @@
             up, down, meanwhile[t - 1] = lax.optimization_barrier((up, down, meanwhile[t - 1]))
             up = added(slots[t + 1], up)
             down = added(slots[3 - t], down)
-    total = slots[0].astype(jnp.float32) + up.astype(jnp.float32) + down.astype(jnp.float32)
-    return total, meanwhile
+    return (slots[0], up, down), meanwhile
 
 
 def sum_line(values):
@@ -733,7 +726,7 @@
             queries = parts_ref[i, 0, 0]
             keys = parts_ref[: i + 1, 1, 0].reshape(span, head_dim)
             values = parts_ref[: i + 1, 2, 0].reshape(span, head_dim)
-            grads = grad_ref[i, 0]
+            grads = grad_ref[i, :, 0].reshape(length, head_dim)
             scores = scores_of(queries, keys) * score_scale
             probs = jnp.where(causal(scores, i * length), jnp.exp(scores - log_ref[i, 0]), 0.0)
             grad_probs = scores_of(grads, values)
@@ -755,7 +748,7 @@
         grid=(seqs,),
         in_specs=[
             whole,
-            pl.BlockSpec((blocks, 1, length, head_dim), lambda m: (0, m, 0, 0)),
+            pl.BlockSpec((blocks, 4, 1, length // 4, head_dim), lambda m: (0, 0, m, 0, 0)),
             pl.BlockSpec((blocks, 1, length, 1), lambda m: (0, m, 0, 0)),
         ],
         out_specs=whole,
@@ -809,37 +802,44 @@
     )(slots, context, weights)
 
 
-def project_out_back(pieces, weights, slots, heads, seqs):
-    own_rows, width = pieces[0].shape
-    span = weights.shape[0]
-    head_dim = span // heads
-    own = own_rows // seqs
-    rows = 4 * own_rows
-
-    def body(slots_ref, *refs):
-        ins, weight_ref, out_ref, rows_ref = refs[:7], refs[7], refs[8], refs[9]
-        fill_slots(rows_ref, ins)
-        product = scores_of(rows_ref[...], weight_ref[...]).astype(LOW)
-        for t in range(4):
-            place = pl.ds(pl.multiple_of(slots_ref[t] * own, own), own)
-            for h in range(heads):
-                out_ref[h, :, place] = product[
-                    t * own_rows : (t + 1) * own_rows, h * head_dim : (h + 1) * head_dim
-                ].reshape(seqs, own, head_dim)
-
-    scalars = pl.BlockSpec(memory_space=pltpu.SMEM)
-    whole = pl.BlockSpec(memory_space=pltpu.VMEM)
-    return pl.pallas_call(
-        body,
-        in_specs=[scalars] + [whole] * 8,
-        out_specs=[whole] * 2,
-        out_shape=[
-            jax.ShapeDtypeStruct((heads, seqs, 4 * own, head_dim), LOW),
-            jax.ShapeDtypeStruct((rows, width), LOW),
-        ],
+def project_out_back(grads, weights, heads, head_dim, seqs):
+    rows, width = grads.shape
+    own = rows // seqs
+    span = heads * head_dim
+
+    def body(grad_ref, weight_ref, out_ref):
+        product = jnp.dot(grad_ref[...], weight_ref[...], preferred_element_type=jnp.float32)
+        for h in range(heads):
+            out_ref[h, 0] = (
+                product[:, h * head_dim : (h + 1) * head_dim].astype(LOW).reshape(seqs, own, head_dim)
+            )
+
+    return pl.pallas_call(
+        body,
+        grid=(4,),
+        in_specs=[
+            pl.BlockSpec((rows, width), lambda j: (0, 0)),
+            pl.BlockSpec((width, span), lambda j: (0, j)),
+        ],
+        out_specs=pl.BlockSpec((heads, 1, seqs, own, head_dim), lambda j: (0, j, 0, 0, 0)),
+        out_shape=jax.ShapeDtypeStruct((heads, 4, seqs, own, head_dim), LOW),
         compiler_params=PARAMS,
         name="project_out_back",
-    )(slots, *pieces, weights)
+    )(grads, weights)
+
+
+def rows_of(pieces):
+    own, width = pieces[0].shape
+
+    def body(*refs):
+        fill_slots(refs[7], refs[:7])
+
+    return pl.pallas_call(
+        body,
+        out_shape=jax.ShapeDtypeStruct((4 * own, width), LOW),
+        compiler_params=PARAMS,
+        name="rows_of",
+    )(*pieces)
 
 
 def unprepare(grads, raw, squares, gains, cosines, sines, d_model):
@@ -960,9 +960,156 @@
 
 def fill_slots(rows_ref, refs):
     own = refs[0].shape[0]
-    rows_ref[:own] = refs[0][...]
-    for t in range(1, 4):
-        rows_ref[t * own : (t + 1) * own] = refs[t][...] + refs[7 - t][...]
+    seqs = len(refs) // 7
+    for m in range(seqs):
+        mine = refs[7 * m : 7 * m + 7]
+        rows_ref[m * own : (m + 1) * own] = mine[0][...]
+        for t in range(1, 4):
+            first = (t * seqs + m) * own
+            rows_ref[first : first + own] = mine[t][...] + mine[7 - t][...]
+
+
+def attn_norm(parts, tokens, gains):
+    rows, width = tokens.shape
+
+    def body(own_ref, up_ref, down_ref, token_ref, gain_ref, hidden_ref, low_ref, unit_ref, inv_ref):
+        total = (
+            own_ref[...].astype(jnp.float32)
+            + up_ref[...].astype(jnp.float32)
+            + down_ref[...].astype(jnp.float32)
+        )
+        inv = lax.rsqrt(jnp.mean(total * total, axis=-1, keepdims=True) + NORM_EPS)
+        unit = total * inv
+        hidden = token_ref[...].astype(jnp.float32) + unit * gain_ref[...]
+        hidden_ref[...] = hidden
+        low_ref[...] = hidden.astype(LOW)
+        unit_ref[...] = unit
+        inv_ref[...] = inv
+
+    full = jax.ShapeDtypeStruct((rows, width), jnp.float32)
+    return pl.pallas_call(
+        body,
+        out_shape=[
+            full,
+            jax.ShapeDtypeStruct((rows, width), LOW),
+            full,
+            jax.ShapeDtypeStruct((rows, 1), jnp.float32),
+        ],
+        compiler_params=PARAMS,
+        name="attn_norm",
+    )(*parts, tokens, gains)
+
+
+def mlp_norm(parts, hidden, cotangent, gains):
+    rows, width = hidden.shape
+
+    def body(own_ref, up_ref, down_ref, hidden_ref, grad_ref, gain_ref, out_ref, back_ref, sum_ref):
+        total = (
+            own_ref[...].astype(jnp.float32)
+            + up_ref[...].astype(jnp.float32)
+            + down_ref[...].astype(jnp.float32)
+        )
+        inv = lax.rsqrt(jnp.mean(total * total, axis=-1, keepdims=True) + NORM_EPS)
+        unit = total * inv
+        out_ref[...] = (hidden_ref[...] + unit * gain_ref[...]).astype(LOW)
+        grad = grad_ref[...].astype(jnp.float32)
+        sum_ref[...] = jnp.sum(grad * unit, axis=0, keepdims=True)
+        scaled = grad * gain_ref[...]
+        mean = jnp.mean(scaled * unit, axis=-1, keepdims=True)
+        back_ref[...] = (inv * (scaled - unit * mean)).astype(LOW)
+
+    return pl.pallas_call(
+        body,
+        out_shape=[jax.ShapeDtypeStruct((rows, width), LOW)] * 2
+        + [jax.ShapeDtypeStruct((1, width), jnp.float32)],
+        compiler_params=PARAMS,
+        name="mlp_norm",
+    )(*parts, hidden, cotangent, gains)
+
+
+def attn_norm_back(parts, cotangent, unit, inv, gains):
+    rows, width = unit.shape
+
+    def body(
+        own_ref, up_ref, down_ref, grad_ref, unit_ref, inv_ref, gain_ref, hidden_ref, back_ref, sum_ref
+    ):
+        grad = (
+            grad_ref[...].astype(jnp.float32)
+            + own_ref[...].astype(jnp.float32)
+            + up_ref[...].astype(jnp.float32)
+            + down_ref[...].astype(jnp.float32)
+        )
+        hidden_ref[...] = grad
+        unit = unit_ref[...]
+        sum_ref[...] = jnp.sum(grad * unit, axis=0, keepdims=True)
+        scaled = grad * gain_ref[...]
+        mean = jnp.mean(scaled * unit, axis=-1, keepdims=True)
+        back_ref[...] = (inv_ref[...] * (scaled - unit * mean)).astype(LOW)
+
+    return pl.pallas_call(
+        body,
+        out_shape=[
+            jax.ShapeDtypeStruct((rows, width), jnp.float32),
+            jax.ShapeDtypeStruct((rows, width), LOW),
+            jax.ShapeDtypeStruct((1, width), jnp.float32),
+        ],
+        compiler_params=PARAMS,
+        name="attn_norm_back",
+    )(*parts, cotangent, unit, inv, gains)
+
+
+def ff_totals(gate_up, down):
+    height, units = down.shape
+    steps = 4
+
+    def body(gate_ref, up_ref, down_ref, gate_out, up_out, down_out):
+        gate_out[...] = gate_ref[...].astype(jnp.float32)
+        up_out[...] = up_ref[...].astype(jnp.float32)
+        down_out[...] = down_ref[...].astype(jnp.float32).T
+
+    tile = units // steps
+    return pl.pallas_call(
+        body,
+        grid=(steps,),
+        in_specs=[
+            pl.BlockSpec((height, tile), lambda j: (0, j)),
+            pl.BlockSpec((height, tile), lambda j: (0, steps + j)),
+            pl.BlockSpec((height, tile), lambda j: (0, j)),
+        ],
+        out_specs=[pl.BlockSpec((height, tile), lambda j: (0, j))] * 2
+        + [pl.BlockSpec((tile, height), lambda j: (j, 0))],
+        out_shape=[jax.ShapeDtypeStruct((height, units), jnp.float32)] * 2
+        + [jax.ShapeDtypeStruct((units, height), jnp.float32)],
+        compiler_params=PARAMS,
+        name="ff_totals",
+    )(gate_up, gate_up, down)
+
+
+def plane_totals(sums, span):
+    height, width = sums[0].shape
+    more = width - 4 * span
+
+    def body(*refs):
+        outs = refs[3:]
+        for k in range(5):
+            columns = slice(k * span, min((k + 1) * span, width))
+            total = (
+                refs[0][:, columns].astype(jnp.float32)
+                + refs[1][:, columns].astype(jnp.float32)
+                + refs[2][:, columns].astype(jnp.float32)
+            )
+            outs[k][...] = total.T if k == 3 else total
+
+    return pl.pallas_call(
+        body,
+        out_shape=[jax.ShapeDtypeStruct((height, span), jnp.float32)] * 3
+        + [
+            jax.ShapeDtypeStruct((span, height), jnp.float32),
+            jax.ShapeDtypeStruct((height, more), jnp.float32),
+        ],
+        compiler_params=PARAMS,
+        name="plane_totals",
+    )(*sums)
 
 
 def weight_tiles(width, tile, tiles):
@@ -970,16 +1117,18 @@
 
 
 def feed_forward(pieces, weights):
+    count = len(pieces)
     own, width = pieces[0].shape
     hidden_units = weights.shape[1] // 3
     tile = 512
     tiles = hidden_units // tile
-    rows = 4 * own
+    parts = 4 * count // 7
+    rows = parts * own
 
     def body(*refs):
-        ins, (gate_w, up_w, down_w) = refs[:7], refs[7:10]
-        rows_ref, gate_ref, up_ref, mixed_ref = refs[10:14]
-        outs, total = refs[14:18], refs[18]
+        ins, (gate_w, up_w, down_w) = refs[:count], refs[count : count + 3]
+        rows_ref, gate_ref, up_ref, mixed_ref, *outs = refs[count + 3 : -1]
+        total = refs[-1]
 
         @pl.when(pl.program_id(0) == 0)
         def _():
@@ -1003,7 +1152,7 @@
 
         @pl.when(pl.program_id(0) == tiles - 1)
         def _():
-            for t in range(4):
+            for t in range(parts):
                 mine = slice(t * own, (t + 1) * own)
                 outs[t][...] = (total[mine] + part[mine]).astype(LOW)
 
@@ -1012,26 +1161,26 @@
     return pl.pallas_call(
         body,
         grid=(tiles,),
-        in_specs=[fixed] * 7 + weight_tiles(width, tile, tiles),
-        out_specs=[pl.BlockSpec((rows, width), lambda j: (0, 0))] + [by_tile] * 3 + [fixed] * 4,
+        in_specs=[fixed] * count + weight_tiles(width, tile, tiles),
+        out_specs=[pl.BlockSpec((rows, width), lambda j: (0, 0))] + [by_tile] * 3 + [fixed] * parts,
         out_shape=[jax.ShapeDtypeStruct((rows, width), LOW)]
         + [jax.ShapeDtypeStruct((rows, hidden_units), LOW)] * 3
-        + [jax.ShapeDtypeStruct((own, width), LOW)] * 4,
+        + [jax.ShapeDtypeStruct((own, width), LOW)] * parts,
         scratch_shapes=[pltpu.VMEM((rows, width), jnp.float32)],
         compiler_params=PARAMS,
         name="feed_forward",
     )(*pieces, weights, weights, weights)
 
 
-def feed_forward_back(rows_low, gate, up, weights):
+def feed_forward_back(rows_low, gate, up, weights, parts):
     rows, width = rows_low.shape
-    own = rows // 4
+    own = rows // parts
     hidden_units = gate.shape[1]
     tile = 512
     tiles = hidden_units // tile
 
     def body(rows_ref, gate_ref, up_ref, gate_w, up_w, down_w, grad_gate_ref, grad_up_ref, *refs):
-        outs, total = refs[:4], refs[4]
+        outs, total = refs[:parts], refs[parts]
         grad_mixed = jnp.dot(rows_ref[...], down_w[...], preferred_element_type=jnp.float32)
         gate = gate_ref[...].astype(jnp.float32)
         up = up_ref[...].astype(jnp.float32)
@@ -1052,7 +1201,7 @@
 
         @pl.when(pl.program_id(0) == tiles - 1)
         def _():
-            for t in range(4):
+            for t in range(parts):
                 mine = slice(t * own, (t + 1) * own)
                 outs[t][...] = (total[mine] + part[mine]).astype(LOW)
 
@@ -1064,9 +1213,9 @@
         in_specs=[pl.BlockSpec((rows, width), lambda j: (0, 0))]
         + [by_tile] * 2
         + weight_tiles(width, tile, tiles),
-        out_specs=[by_tile] * 2 + [fixed] * 4,
+        out_specs=[by_tile] * 2 + [fixed] * parts,
         out_shape=[jax.ShapeDtypeStruct((rows, hidden_units), LOW)] * 2
-        + [jax.ShapeDtypeStruct((own, width), LOW)] * 4,
+        + [jax.ShapeDtypeStruct((own, width), LOW)] * parts,
         scratch_shapes=[pltpu.VMEM((rows, width), jnp.float32)],
         compiler_params=PARAMS,
         name="feed_forward_back",
@@ -1074,24 +1223,25 @@
 
 
 def down_grad(pieces, mixed):
+    count = len(pieces)
     own, width = pieces[0].shape
     rows, columns = mixed.shape
     tile = 512
 
     def body(*refs):
-        rows_ref, out_ref = refs[8], refs[9]
+        rows_ref, out_ref = refs[count + 1], refs[count + 2]
 
         @pl.when(pl.program_id(0) == 0)
         def _():
-            fill_slots(rows_ref, refs[:7])
+            fill_slots(rows_ref, refs[:count])
 
         place = pl.ds(pl.multiple_of(pl.program_id(0) * tile, tile), tile)
-        out_ref[...] = contract(rows_ref[:, place], refs[7][...], 0, 0).astype(LOW)
+        out_ref[...] = contract(rows_ref[:, place], refs[count][...], 0, 0).astype(LOW)
 
     return pl.pallas_call(
         body,
         grid=(width // tile,),
-        in_specs=[pl.BlockSpec((own, width), lambda j: (0, 0))] * 7
+        in_specs=[pl.BlockSpec((own, width), lambda j: (0, 0))] * count
         + [pl.BlockSpec((rows, columns), lambda j: (0, 0))],
         out_specs=[
             pl.BlockSpec((rows, width), lambda j: (0, 0)),
@@ -1174,22 +1324,21 @@
     )
     qk_gain = all_gains[: 2 * heads].reshape(1, 2 * head_span)
     feature_rows = d_model // head_dim
-    attn_gains = all_gains[2 * heads : 2 * heads + feature_rows].reshape(d_model)
-    mlp_gains = all_gains[2 * heads + feature_rows :].reshape(d_model)
+    attn_gains = all_gains[2 * heads : 2 * heads + feature_rows].reshape(1, d_model)
+    mlp_gains = all_gains[2 * heads + feature_rows :].reshape(1, d_model)
     positions = seq_rank * length + jnp.arange(length, dtype=jnp.int32)
     cosines, sines = rope_tables(positions, head_dim)
     cosines = jnp.concatenate([cosines[:, 0], cosines[:, 0]], axis=-1)
     sines = jnp.concatenate([-sines[:, 0], sines[:, 0]], axis=-1)
-    own_tokens = (
-        lax.dynamic_slice_in_dim(tokens, tp_rank * own_length, own_length, 1)
-        .astype(jnp.float32)
-        .reshape(own_rows, d_model)
-    )
-    grad_out = cotangent.astype(jnp.float32).reshape(own_rows, d_model)
+    own_tokens = lax.dynamic_slice_in_dim(tokens, tp_rank * own_length, own_length, 1).reshape(
+        own_rows, d_model
+    )
+    grad_out = cotangent.reshape(own_rows, d_model)
+    out_rows = lax.all_gather(w_out, "tp", axis=0, tiled=True)
 
     raw, in_weights = project_in(tokens.reshape(rows, d_model), in_pieces, order)
     out_firsts = first_step(after(w_out, in_pieces[3:5]))
-    weights = lax.all_gather(after(packed, in_pieces[3:5]), ("dp", "seq"), axis=0, tiled=True)
+    weights = lax.all_gather(after(packed, (in_pieces[3:5], out_rows)), ("dp", "seq"), axis=0, tiled=True)
 
     squares = jnp.stack(
         [
@@ -1202,36 +1351,29 @@
     out_pieces, _ = gather_plane(w_out, out_firsts)
     raw = raw.reshape(seqs, length, 3 * head_span)
     parts = prepare(raw, squares, qk_gain, cosines, sines, heads, head_dim, d_model)
+    parts, out_pieces[3:5] = lax.optimization_barrier((parts, out_pieces[3:5]))
     parts = lax.all_to_all(parts, "seq", 0, 0, tiled=True)
     parts, out_pieces = lax.optimization_barrier((parts, out_pieces))
     out_weights = assemble_columns(out_pieces, order)
     context, log_total = attend(parts)
     context = lax.all_to_all(context, "seq", 0, 0, tiled=True)
     context_rows, *attn_slots = project_out(context, out_weights, slots)
-    attn_out, _ = scatter_line(attn_slots)
-    attn_inv = lax.rsqrt(jnp.mean(attn_out * attn_out, axis=-1, keepdims=True) + NORM_EPS)
-    attn_unit = attn_out * attn_inv
-    hidden = own_tokens + attn_unit * attn_gains
-    hidden_rows, gate, up, mixed, *mlp_slots = feed_forward(
-        gather_line(hidden.astype(LOW)), weights
-    )
-    mlp_out, _ = scatter_line(mlp_slots)
-    mlp_inv = lax.rsqrt(jnp.mean(mlp_out * mlp_out, axis=-1, keepdims=True) + NORM_EPS)
-    mlp_unit = mlp_out * mlp_inv
-    outputs = (hidden + mlp_unit * mlp_gains).astype(LOW)
-
-    grad_mgain = jnp.sum(grad_out * mlp_unit, axis=0)
-    mlp_scaled = grad_out * mlp_gains
-    grad_mlp = norm_back(
-        mlp_unit, mlp_scaled, mlp_inv, jnp.sum(mlp_scaled * mlp_unit, axis=-1), d_model
-    )
-    grad_mlp_rows, down_part = down_grad(gather_line(grad_mlp.astype(LOW)), mixed)
-    grad_gate, grad_up, *hidden_slots = feed_forward_back(grad_mlp_rows, gate, up, weights)
+    hidden, hidden_low, attn_unit, attn_inv = attn_norm(
+        scatter_line(attn_slots)[0], own_tokens, attn_gains
+    )
+    out_columns = after(out_rows, hidden_low).T
+    out_columns = lax.all_gather(out_columns, ("dp", "seq"), axis=0, tiled=True)
+    hidden_rows, gate, up, mixed, *mlp_slots = feed_forward(gather_line(hidden_low), weights)
+    outputs, grad_mlp, grad_mgain = mlp_norm(
+        scatter_line(mlp_slots)[0], hidden, grad_out, mlp_gains
+    )
+    grad_mlp, out_columns = lax.optimization_barrier((grad_mlp, out_columns))
+    grad_mlp_rows, down_part = down_grad(gather_line(grad_mlp), mixed)
+    grad_gate, grad_up, *hidden_slots = feed_forward_back(grad_mlp_rows, gate, up, weights, 4)
     units = mixed.shape[1]
     gate_part = weight_grad(hidden_rows, grad_gate, 2 * units, 0)
-    hidden_sum, (gate_part, _) = scatter_line(hidden_slots, (gate_part, ()))
     gate_up_part = weight_grad(hidden_rows, grad_up, 2 * units, 1, gate_part)
-    hidden_sum, gate_up_part = lax.optimization_barrier((hidden_sum, gate_up_part))
+    hidden_sum, (gate_part, gate_up_part) = scatter_line(hidden_slots, (gate_part, gate_up_part))
 
     def sum_plane(part):
         return lax.optimization_barrier(
@@ -1240,69 +1382,59 @@
 
     down_sum = sum_plane(down_part)
     gate_up_sum = sum_plane(gate_up_part)
-    ff_sums = (
-        gate_up_sum[:, :units].astype(jnp.float32),
-        gate_up_sum[:, units:].astype(jnp.float32),
-        down_sum.T.astype(jnp.float32),
-    )
-
-    def joined(halves, first, last):
-        return jnp.concatenate([half[:, first:last] for half in halves], axis=0)
-
-    grad_hidden = grad_out + hidden_sum
-    grad_again = jnp.sum(grad_hidden * attn_unit, axis=0)
-    attn_scaled = grad_hidden * attn_gains
-    grad_attn = norm_back(
-        attn_unit, attn_scaled, attn_inv, jnp.sum(attn_scaled * attn_unit, axis=-1), d_model
-    ).astype(LOW)
-    grad_context, grad_attn_rows = project_out_back(
-        gather_line(grad_attn), out_weights, slots, heads, seqs
-    )
-    grad_context = lax.all_to_all(grad_context, "seq", 0, 0, tiled=True)
+    ff_sums = ff_totals(gate_up_sum, down_sum)
+
+    grad_hidden, grad_attn, grad_again = attn_norm_back(
+        hidden_sum, grad_out, attn_unit, attn_inv, attn_gains
+    )
+    grad_context = project_out_back(grad_attn, out_columns, heads, head_dim, seqs)
+    grad_context = lax.all_to_all(
+        grad_context.reshape((16,) + grad_context.shape[2:]), ("seq", "tp"), 0, 0, tiled=True
+    ).reshape(grad_context.shape)
     part_grads = attend_back(parts, grad_context, log_total)
     part_grads = lax.all_to_all(part_grads, "seq", 0, 0, tiled=True)
+    grad_attn_rows = rows_of(gather_line(grad_attn))
+    own_gains = lax.all_to_all(
+        jnp.concatenate([grad_again.reshape(4, 4, -1), grad_mgain.reshape(4, 4, -1)], axis=1),
+        "tp",
+        0,
+        0,
+        tiled=True,
+    )
+    part_grads, grad_attn_rows, own_gains = lax.optimization_barrier(
+        (part_grads, grad_attn_rows, own_gains)
+    )
+    own_gains = jnp.sum(own_gains, axis=0)
     scaled, dots, qk_sums = unprepare(part_grads, raw, squares, qk_gain, cosines, sines, d_model)
     dots = sum_line(dots.reshape(2, rows)).reshape(2, seqs, length, 1)
     grad_raw, *token_slots = project_in_back(
         part_grads, scaled, raw, squares, dots, in_weights, slots
     )
-    in_far, in_near = sum_in_core(
+    gain_parts = jnp.concatenate([qk_sums.reshape(2, heads, 8, -1), own_gains.reshape(2, heads, 8, -1)])
+    gain_parts = jnp.transpose(gain_parts, (2, 0, 1, 3)).reshape(8, -1, 128)
+    gain_rows_used = gain_parts.shape[1]
+    gain_parts = jnp.pad(
+        gain_parts, ((0, 0), (0, d_model // 8 - gain_rows_used), (0, 0))
+    ).reshape(d_model, 128)
+    far_sent, near = sum_in_plane(
         (tokens.reshape(rows, d_model), grad_attn_rows),
         (grad_raw, context_rows),
-        (((0, 0), (1, 1)),),
+        gain_parts,
         order,
     )
-    token_sum, (in_far, in_near) = scatter_line(token_slots, (in_far, in_near))
-    in_far, in_first = send_first(in_far, in_near)
-    in_second = send_second(in_far, in_near)
-    in_second, ff_sums = lax.optimization_barrier((in_second, ff_sums))
-    in_halves = halves_total(in_near, in_first, in_second)
-    grad_tokens = grad_hidden + token_sum
-
-    def by_owner(values):
-        return jnp.transpose(values.reshape(4, feature_rows // 4, 8, -1), (2, 0, 1, 3))
-
-    head_sums = jnp.transpose(qk_sums.reshape(2, heads, 8, -1), (2, 0, 1, 3))[:, None]
-    is_own = (jnp.arange(4) == tp_rank)[None, :, None, None, None]
-    payload = jnp.concatenate(
-        [
-            jnp.where(is_own, head_sums, 0.0),
-            by_owner(grad_again)[:, :, None],
-            by_owner(grad_mgain)[:, :, None],
-        ],
-        axis=2,
-    ).reshape(32, -1)
-    payload = after(payload, in_near)
-    gain_sums = jnp.sum(
-        lax.all_to_all(payload, ("dp", "seq", "tp"), 0, 0, tiled=True), axis=0
-    ).reshape(4, heads, -1)
+    token_sums, (_, near) = scatter_line(token_slots, (far_sent, near))
+    in_sums = [near[2], to_neighbour(near[0], 1), to_neighbour(near[1], 2)]
+    in_sums, ff_sums = lax.optimization_barrier((in_sums, ff_sums))
+    *in_sums, gain_sums = plane_totals(in_sums, head_span)
+    grad_tokens = grad_hidden
+    for part in token_sums:
+        grad_tokens = grad_tokens + part.astype(jnp.float32)
+
+    gain_sums = gain_sums[:gain_rows_used].reshape(4, heads, -1)
     return (
-        outputs.reshape(seqs, own_length, d_model),
-        grad_tokens.reshape(seqs, own_length, d_model),
-        joined(in_halves, 0, head_span),
-        joined(in_halves, head_span, 2 * head_span),
-        joined(in_halves, 2 * head_span, 3 * head_span),
-        joined(in_halves, 3 * head_span, 4 * head_span).T,
+        outputs.reshape(cotangent.shape),
+        grad_tokens.reshape(cotangent.shape),
+        *in_sums,
         ff_sums[0],
         ff_sums[1],
         ff_sums[2],

time: 672 us -> 625 us (0.930)
  blocking collectives: 69.5 us -> 24.4 us
  other arithmetic: 51.6 us -> 17.2 us
  Pallas kernels: 138 us -> 154 us
  local copies, waits for them, and re-layouts: 39.7 us -> 47.1 us
    all_to_all x2 -> x0, blocking collectives: 49.1 us -> none  [the longest x1 31.6 us: on_plane(): part_grads = lax.all_to_all(part_grads, 'seq', 0, 0, tiled=True)]
    all_to_all x1, waiting for transfers between devices: 0.01 us -> 20.9 us  [on_plane(): parts = lax.all_to_all(parts, 'seq', 0, 0, tiled=True)]
    ppermute x9, waiting for transfers between devices: 17.8 us -> 0.02 us  [gather_line(): up = lax.ppermute(up, 'tp', [(i, i + 1) for i in range(t - 1, 3)])]
    pallas_call x2 -> x8, Pallas kernels: 25.7 us -> 42.4 us  [the longest x1 21.6 us: feed_forward(): pl.pallas_call(body, grid=(tiles,), in_specs=[fixed] * count + weight_til...]
    all_to_all x1 -> x3, starting transfers between devices: 5.64 us -> 20.3 us  [the longest x1 13.4 us: on_plane(): lax.all_to_all(grad_context.reshape((16,) + grad_context.shape[2:]), ('se...]
    convert_element_type x7 -> x0, other arithmetic: 14.3 us -> none  [the longest x2 4.1 us: add_low(): return (mine.astype(jnp.float32) + got.astype(jnp.float32)).astype(LOW)]
    ppermute x12, waiting for transfers between devices: 9.16 us -> 23.2 us  [scatter_line(): down = lax.ppermute(down, 'tp', [(i, i - 1) for i in range(4 - t, 4)])]
    ppermute x14 -> x12, waiting for transfers between devices: 36.9 us -> 24.7 us  [to_neighbour(): return lax.ppermute(values, 'seq', [(i, i ^ flip) for i in range(4)])]
  transfers between devices with their start and end apart: 74 -> 76, of which waited for: 32 -> 37; matrix products, arithmetic and copies ran while one was open for 8% -> 5% of each run, Pallas kernels for 16% -> 23%
where the time goes in v3:
time: 625 us; the launch traced here: 614 us
  waiting for transfers between devices  209 us (33%)
  Pallas kernels  154 us (25%)
  starting transfers between devices  147 us (24%)
  local copies, waits for them, and re-layouts  47.1 us (8%)
  blocking collectives  24.4 us (4%)
  other arithmetic  17.2 us (3%)
  between operations  15.3 us (2%)
    ppermute x9, waiting for transfers between devices, gather_line(): down = lax.ppermute(down, 'tp', [(i, i - 1) for i in range(1, 5 - t)])  73.1 us
    ppermute x12, starting transfers between devices, scatter_line(): up = lax.ppermute(up, 'tp', [(i, i + 1) for i in range(t)])  55.9 us
    ppermute x12, waiting for transfers between devices, scatter_line(): up = lax.ppermute(up, 'tp', [(i, i + 1) for i in range(t)])  40.6 us
    unnamed x113, local copies, waits for them, and re-layouts  37.7 us
    ppermute x12, waiting for transfers between devices, to_neighbour(): return lax.ppermute(values, 'seq', [(i, i ^ flip) for i in range(4)])  24.7 us
    psum x2, blocking collectives, sum_line(): return lax.optimization_barrier(lax.psum(flat, 'tp'))  24.4 us
    pallas_call x1, Pallas kernels, feed_forward_back(): pl.pallas_call(body, grid=(tiles,), in_specs=[pl.BlockSpec((rows, width),...  23.4 us
    ppermute x12, waiting for transfers between devices, scatter_line(): down = lax.ppermute(down, 'tp', [(i, i - 1) for i in range(4 - t, 4)])  23.2 us
  transfers between devices with their start and end apart: 76, of which 37 were waited for; matrix products, arithmetic and copies ran while one was open for 5% of the time, Pallas kernels for 23%

profile of v3, /device:TPU:0, one launch (start us, length us, event | category | flops | bytes accessed | tf_op | source)
XLA Modules:
  0.0 614.3 jit_solution(17238457629351939393)
XLA Ops:
  36.8 8.3 %collective-permute-done.2.refs_3_ = bf16[128,1536]{1,0:T(8,128)(2,1)S(1)} collective-permute-done((bf16[128,1536]{1,0:T(8,128)(2,1)S(1)}, bf16[128,1536]{1,0:T(8,128)(2,1)S(1)}, u32[]{:S(2)}, u32[]{:S(2)}) %collective-permute-start.2) | collective-permute-done | bytes 393248 | tf_op jit(solution)/shard_map/ppermute | solution.py:408
  50.0 9.3 %project_in.1 = (f32[512,1536]{1,0:T(8,128)}, bf16[2048,1536]{1,0:T(8,128)(2,1)}) custom-call(s32[8]{0:T(128)S(1)} %iota_xor_fusion.order_ref, bf16[512,2048]{1,0:T(8,128)(2,1)} %bitcast.41, bf16[256,1536]{1,0:T(8,128)(2,1)S(1)} %constant_dynamic-update-slice_fusion.refs_0_, bf16[256,1536]{1,0:T(8,128)(2,1)S(1)} %collective-permute-done.refs_1_, ...), custom_call_target="tpu_custom_call" | custom-call | tf_op jit(solution)/shard_map/project_in/pallas_call | solution.py:472
  61.6 11.9 %psum.14 = f32[8,128]{1,0:T(8,128)S(1)} all-reduce(f32[8,128]{1,0:T(8,128)S(1)} %reshape.122), channel_id=1, replica_groups=mesh['dp'=2,'seq'=4,'tp'=4] {'tp'}, use_global_device_ids=true, to_apply=%region_2.3 | all-reduce | flops 1024 | bytes 8192 | tf_op jit(solution)/shard_map/psum | solution.py:615
  93.6 20.9 %all-to-all-done.1.parts_ref = bf16[4,3,2,256,128]{4,3,2,1,0:T(8,128)(2,1)S(1)} async-done(((bf16[4,3,2,256,128]{4,3,2,1,0:T(8,128)(2,1)}), bf16[4,3,2,256,128]{4,3,2,1,0:T(8,128)(2,1)S(1)}, u32[]{:S(2)}, u32[]{:S(2)}) %all-to-all-start.1) | async-done | bytes 1572896 | tf_op jit(solution)/shard_map/all_to_all | solution.py:1355
  131.9 7.1 %all-to-all-done.2.context_ref = bf16[4,2,256,128]{3,2,1,0:T(8,128)(2,1)S(1)} async-done(((bf16[4,2,256,128]{3,2,1,0:T(8,128)(2,1)}), bf16[4,2,256,128]{3,2,1,0:T(8,128)(2,1)S(1)}, u32[]{:S(2)}, u32[]{:S(2)}) %all-to-all-start.2) | async-done | bytes 524320 | tf_op jit(solution)/shard_map/all_to_all | solution.py:1359
  146.6 10.2 %collective-permute-done.18 = bf16[128,2048]{1,0:T(8,128)(2,1)S(1)} collective-permute-done((bf16[128,2048]{1,0:T(8,128)(2,1)S(1)}, bf16[128,2048]{1,0:T(8,128)(2,1)S(1)}, u32[]{:S(2)}, u32[]{:S(2)}) %collective-permute-start.18) | collective-permute-done | bytes 524320 | tf_op jit(solution)/shard_map/ppermute | solution.py:604
  163.0 9.3 %collective-permute-done.20 = bf16[128,2048]{1,0:T(8,128)(2,1)S(1)} collective-permute-done((bf16[128,2048]{1,0:T(8,128)(2,1)S(1)}, bf16[128,2048]{1,0:T(8,128)(2,1)S(1)}, u32[]{:S(2)}, u32[]{:S(2)}) %collective-permute-start.20) | collective-permute-done | bytes 524320 | tf_op jit(solution)/shard_map/ppermute | solution.py:604
  200.9 6.5 %collective-permute-done.27.refs_4_ = bf16[128,2048]{1,0:T(8,128)(2,1)S(1)} collective-permute-done((bf16[128,2048]{1,0:T(8,128)(2,1)S(1)}, bf16[128,2048]{1,0:T(8,128)(2,1)S(1)}, u32[]{:S(2)}, u32[]{:S(2)}) %collective-permute-start.27) | collective-permute-done | bytes 524320 | tf_op jit(solution)/shard_map/ppermute | solution.py:591
  209.5 10.0 %collective-permute-done.28.refs_5_ = bf16[128,2048]{1,0:T(8,128)(2,1)S(1)} collective-permute-done((bf16[128,2048]{1,0:T(8,128)(2,1)S(1)}, bf16[128,2048]{1,0:T(8,128)(2,1)S(1)}, u32[]{:S(2)}, u32[]{:S(2)}) %collective-permute-start.28) | collective-permute-done | bytes 524320 | tf_op jit(solution)/shard_map/ppermute | solution.py:591
  223.2 7.3 %collective-permute-done.29.refs_6_ = bf16[128,2048]{1,0:T(8,128)(2,1)S(1)} collective-permute-done((bf16[128,2048]{1,0:T(8,128)(2,1)S(1)}, bf16[128,2048]{1,0:T(8,128)(2,1)S(1)}, u32[]{:S(2)}, u32[]{:S(2)}) %collective-permute-start.29) | collective-permute-done | bytes 524320 | tf_op jit(solution)/shard_map/ppermute | solution.py:591
  232.4 21.6 %feed_forward.1 = (bf16[512,2048]{1,0:T(8,128)(2,1)}, bf16[512,2048]{1,0:T(8,128)(2,1)}, bf16[512,2048]{1,0:T(8,128)(2,1)}, bf16[512,2048]{1,0:T(8,128)(2,1)}, b...) custom-call(bf16[128,2048]{1,0:T(8,128)(2,1)S(1)} %get-tuple-element, ...), custom_call_target="tpu_custom_call" | custom-call | tf_op jit(solution)/shard_map/feed_forward/pallas_call | solution.py:1161
  256.1 6.6 %collective-permute-done.30 = bf16[128,2048]{1,0:T(8,128)(2,1)S(1)} collective-permute-done((bf16[128,2048]{1,0:T(8,128)(2,1)S(1)}, bf16[128,2048]{1,0:T(8,128)(2,1)S(1)}, u32[]{:S(2)}, u32[]{:S(2)}) %collective-permute-start.30) | collective-permute-done | bytes 524320 | tf_op jit(solution)/shard_map/ppermute | solution.py:604
  268.9 6.6 %collective-permute-done.32 = bf16[128,2048]{1,0:T(8,128)(2,1)S(1)} collective-permute-done((bf16[128,2048]{1,0:T(8,128)(2,1)S(1)}, bf16[128,2048]{1,0:T(8,128)(2,1)S(1)}, u32[]{:S(2)}, u32[]{:S(2)}) %collective-permute-start.32) | collective-permute-done | bytes 524320 | tf_op jit(solution)/shard_map/ppermute | solution.py:604
  278.7 12.7 %collective-permute-start.34 = (bf16[128,2048]{1,0:T(8,128)(2,1)}, bf16[128,2048]{1,0:T(8,128)(2,1)}, u32[]{:S(2)}, u32[]{:S(2)}) collective-permute-start(bf16[128,2048]{1,0:T(8,128)(2,1)} %add_convert_fusion.5), channel_id=1, source_target_pairs={{0,1},{1,2},{2,3},{4,5},{5,6},{6,7},{8,9},{9,10},{10,11},{12,13},{... | collective-permute-start | bytes 1572872 | tf_op jit(solution)/shard_map/ppermute | solution.py:604
  308.5 9.4 %collective-permute-done.39.refs_4_ = bf16[128,2048]{1,0:T(8,128)(2,1)S(1)} collective-permute-done((bf16[128,2048]{1,0:T(8,128)(2,1)}, bf16[128,2048]{1,0:T(8,128)(2,1)S(1)}, u32[]{:S(2)}, u32[]{:S(2)}) %collective-permute-start.39) | collective-permute-done | bytes 524320 | tf_op jit(solution)/shard_map/ppermute | solution.py:591
  319.9 12.2 %collective-permute-done.40.refs_5_ = bf16[128,2048]{1,0:T(8,128)(2,1)S(1)} collective-permute-done((bf16[128,2048]{1,0:T(8,128)(2,1)S(1)}, bf16[128,2048]{1,0:T(8,128)(2,1)S(1)}, u32[]{:S(2)}, u32[]{:S(2)}) %collective-permute-start.40) | collective-permute-done | bytes 524320 | tf_op jit(solution)/shard_map/ppermute | solution.py:591
  334.1 9.1 %collective-permute-done.41.refs_6_ = bf16[128,2048]{1,0:T(8,128)(2,1)S(1)} collective-permute-done((bf16[128,2048]{1,0:T(8,128)(2,1)S(1)}, bf16[128,2048]{1,0:T(8,128)(2,1)S(1)}, u32[]{:S(2)}, u32[]{:S(2)}) %collective-permute-start.41) | collective-permute-done | bytes 524320 | tf_op jit(solution)/shard_map/ppermute | solution.py:591
  344.2 8.3 %down_grad.1 = (bf16[512,2048]{1,0:T(8,128)(2,1)}, bf16[2048,2048]{1,0:T(8,128)(2,1)}) custom-call(bf16[128,2048]{1,0:T(8,128)(2,1)S(1)} %copy-done.30, bf16[128,2048]{1,0:T(8,128)(2,1)S(1)} %collective-permute-done.36.refs_1_, bf16[128,2048]{1,0:T(8,128)(2,1)S(1)} %collective-permute-done.37.refs_2_, bf16[128,2048]{1,0:T(8,128)(2,1)S(1)} %collective-permute-done.38.refs_3_, ...), custom_call_target="tpu_custom_call" | custom-call | tf_op jit(solution)/shard_map/down_grad/pallas_call | solution.py:1241
  352.6 23.4 %feed_forward_back.1 = (bf16[512,2048]{1,0:T(8,128)(2,1)}, bf16[512,2048]{1,0:T(8,128)(2,1)}, bf16[128,2048]{1,0:T(8,128)(2,1)S(1)}, bf16[128,2048]{1,0:T(8,128)...) custom-call(bf16[512,2048]{1,0:T(8,128)(2,1)} %get-tuple-element.196.rows_ref, ...), custom_call_target="tpu_custom_call" | custom-call | tf_op jit(solution)/shard_map/feed_forward_back/pallas_call | solution.py:1210
  378.4 8.2 %weight_grad.2.refs_0_ = bf16[2048,4096]{1,0:T(8,128)(2,1)} custom-call(bf16[512,2048]{1,0:T(8,128)(2,1)S(1)} %copy-done.3, bf16[512,2048]{1,0:T(8,128)(2,1)} %get-tuple-element.204.right_ref), custom_call_target="tpu_custom_call" | custom-call | tf_op jit(solution)/shard_map/weight_grad/pallas_call | solution.py:1268
  395.8 8.2 %weight_grad.3 = bf16[2048,4096]{1,0:T(8,128)(2,1)} custom-call(bf16[512,2048]{1,0:T(8,128)(2,1)S(1)} %copy-done.3, bf16[512,2048]{1,0:T(8,128)(2,1)} %get-tuple-element.207.right_ref, bf16[2048,4096]{1,0:T(8,128)(2,1)} %weight_grad.2.refs_0_), custom_call_target="tpu_custom_call", output_to_operand_aliasing={{}: (2, {})} | custom-call | tf_op jit(solution)/shard_map/weight_grad/pallas_call | solution.py:1268
  422.2 6.1 project_out_back.1
  428.3 13.4 %all-to-all-start.3 = ((bf16[16,2,64,128]{3,2,1,0:T(8,128)(2,1)}), bf16[16,2,64,128]{3,2,1,0:T(8,128)(2,1)S(1)}, u32[]{:S(2)}, u32[]{:S(2)}) async-start(bf16[16,2,64,128]{3,2,1,0:T(8,128)(2,1)} %bitcast.10), calls=%async_computation.3 | async-start | bytes 1048576 | tf_op jit(solution)/shard_map/all_to_all | solution.py:1391
  458.4 7.1 %attend_back.1 = bf16[4,3,2,256,128]{4,3,2,1,0:T(8,128)(2,1)S(1)} custom-call(bf16[4,3,2,256,128]{4,3,2,1,0:T(8,128)(2,1)} %copy-done, bf16[4,4,2,64,128]{4,3,2,1,0:T(8,128)(2,1)S(1)} %bitcast.32, f32[4,2,256,1]{3,2,1,0:T(8,128)S(1)} %copy-done.15), custom_call_target="tpu_custom_call" | custom-call | tf_op jit(solution)/shard_map/attend_back/pallas_call | solution.py:746
  472.4 9.5 %collective-permute-done.52.refs_5_ = bf16[128,2048]{1,0:T(8,128)(2,1)S(1)} collective-permute-done((bf16[128,2048]{1,0:T(8,128)(2,1)}, bf16[128,2048]{1,0:T(8,128)(2,1)S(1)}, u32[]{:S(2)}, u32[]{:S(2)}) %collective-permute-start.52) | collective-permute-done | bytes 524320 | tf_op jit(solution)/shard_map/ppermute | solution.py:591
  483.8 9.1 %collective-permute-done.53.refs_6_ = bf16[128,2048]{1,0:T(8,128)(2,1)S(1)} collective-permute-done((bf16[128,2048]{1,0:T(8,128)(2,1)S(1)}, bf16[128,2048]{1,0:T(8,128)(2,1)S(1)}, u32[]{:S(2)}, u32[]{:S(2)}) %collective-permute-start.53) | collective-permute-done | bytes 524320 | tf_op jit(solution)/shard_map/ppermute | solution.py:591
  504.9 12.4 %psum.15 = f32[8,128]{1,0:T(8,128)S(1)} all-reduce(f32[8,128]{1,0:T(8,128)S(1)} %reshape_reshape.3), channel_id=1, replica_groups=mesh['dp'=2,'seq'=4,'tp'=4] {'tp'}, use_global_device_ids=true, to_apply=%region_3.4 | all-reduce | flops 1024 | bytes 8192 | tf_op jit(solution)/shard_map/psum | solution.py:615
  519.2 9.8 %project_in_back.1 = (bf16[512,1536]{1,0:T(8,128)(2,1)}, bf16[128,2048]{1,0:T(8,128)(2,1)S(1)}, bf16[128,2048]{1,0:T(8,128)(2,1)S(1)}, bf16[128,2048]{1,0:T(8,128)(2,1)S(1)}, bf16[128,2048]{1,0:T(8,128)(2,1)S(1)}) custom-call(s32[4]{0:T(128)S(1)} %and_select_fusion.slots_ref, bf16[4,3,2,256,128]{4,3,2,1,0:T(8,128)(2,1)} %copy-done.1, ...), custom_call_target="tpu_custom_call" | custom-call | tf_op jit(solution)/shard_map/project_in_back/pallas_call | solution.py:937
  530.4 6.5 %grad_blocks.3 = bf16[1024,2176]{1,0:T(8,128)(2,1)} custom-call(s32[8]{0:T(128)S(1)} %iota_xor_fusion.order_ref, bf16[512,2048]{1,0:T(8,128)(2,1)} %bitcast.42, bf16[512,2048]{1,0:T(8,128)(2,1)} %rows_of.1.refs_1_, bf16[512,1536]{1,0:T(8,128)(2,1)S(1)} %copy-done.2, bf16[512,512]{1,0:T(8,128)(2,1)S(1)} %get-tuple-element.228.refs_3_, f32[2048,128]{1,0:T(8,128)S(1)} %bitcast.29), custom_call_target="tpu_custom_call" | custom-call | tf_op jit(solution)/shard_map/grad_blocks/pallas_call | solution.py:567
  556.9 11.2 %collective-permute-done.59.refs_6_ = bf16[128,2176]{1,0:T(8,128)(2,1)S(1)} collective-permute-done((bf16[128,2176]{1,0:T(8,128)(2,1)S(1)}, bf16[128,2176]{1,0:T(8,128)(2,1)S(1)}, u32[]{:S(2)}, u32[]{:S(2)}) %collective-permute-start.59) | collective-permute-done | bytes 557088 | tf_op jit(solution)/shard_map/ppermute | solution.py:408
  568.2 7.9 %grad_blocks.5 = (bf16[256,2176]{1,0:T(8,128)(2,1)}, bf16[256,2176]{1,0:T(8,128)(2,1)}, bf16[256,2176]{1,0:T(8,128)(2,1)}) custom-call(s32[8]{0:T(128)S(1)} %iota_xor_fusion.order_ref, bf16[512,2048]{1,0:T(8,128)(2,1)} %bitcast.44, bf16[512,2048]{1,0:T(8,128)(2,1)} %rows_of.1.refs_1_, bf16[512,1536]{1,0:T(8,128)(2,1)} %get-tuple-element.227.refs_2_, ...), custom_call_target="tpu_custom_call" | custom-call | tf_op jit(solution)/shard_map/grad_blocks/pallas_call | solution.py:567
  584.3 9.2 %collective-permute-done.62 = bf16[128,2048]{1,0:T(8,128)(2,1)S(1)} collective-permute-done((bf16[128,2048]{1,0:T(8,128)(2,1)S(1)}, bf16[128,2048]{1,0:T(8,128)(2,1)S(1)}, u32[]{:S(2)}, u32[]{:S(2)}) %collective-permute-start.62) | collective-permute-done | bytes 524320 | tf_op jit(solution)/shard_map/ppermute | solution.py:605
  (323 shorter events, 269.8 us)
Async XLA Ops:
  7.2 40.0 %all-gather.4.cloned.1.call-start = ((), (), s32[]{:S(2)}) async-start(), calls=%async_computation.8 | async-start | bytes 1310720 | tf_op jit(solution)/shard_map/all_gather | solution.py:1337
  10.2 26.6 %collective-permute-start.4 = (bf16[256,1536]{1,0:T(8,128)(2,1)S(1)}, bf16[256,1536]{1,0:T(8,128)(2,1)}, u32[]{:S(2)}, u32[]{:S(2)}) collective-permute-start(bf16[256,1536]{1,0:T(8,128)(2,1)S(1)} %constant_dynamic-update-slice_fusion.refs_0_), channel_id=1, source_target_pairs={{0,16},{16,0},{1,17},{17,1},{2,18},{18,2},{3,19},{19,3},{4,20},{20... | collective-permute-start | bytes 2359304 | tf_op jit(solution)/shard_map/ppermute | solution.py:412
  10.7 22.4 %collective-permute-start.1 = (bf16[256,1536]{1,0:T(8,128)(2,1)S(1)}, bf16[256,1536]{1,0:T(8,128)(2,1)S(1)}, u32[]{:S(2)}, u32[]{:S(2)}) collective-permute-start(bf16[256,1536]{1,0:T(8,128)(2,1)S(1)} %constant_dynamic-update-slice_fusion.refs_0_), channel_id=1, source_target_pairs={{0,8},{4,12},{8,0},{12,4},{1,9},{5,13},{9,1},{13,5},{2,10},{6,14},... | collective-permute-start | bytes 2359304 | tf_op jit(solution)/shard_map/ppermute | solution.py:408
  13.3 19.8 %collective-permute-start = (bf16[256,1536]{1,0:T(8,128)(2,1)S(1)}, bf16[256,1536]{1,0:T(8,128)(2,1)S(1)}, u32[]{:S(2)}, u32[]{:S(2)}) collective-permute-start(bf16[256,1536]{1,0:T(8,128)(2,1)S(1)} %constant_dynamic-update-slice_fusion.refs_0_), channel_id=1, source_target_pairs={{0,4},{4,0},{8,12},{12,8},{1,5},{5,1},{9,13},{13,9},{2,6},{6,2},{1... | collective-permute-start | bytes 2359304 | tf_op jit(solution)/shard_map/ppermute | solution.py:408
  22.0 209.3 %all-gather.6.cloned.1.call-start = ((), (), s32[]{:S(2)}) async-start(), calls=%async_computation.9 | async-start | bytes 28311552 | tf_op jit(solution)/shard_map/all_gather | solution.py:1341
  47.8 35.8 %collective-permute-start.13 = (bf16[512,256]{1,0:T(8,128)(2,1)S(1)}, bf16[512,256]{1,0:T(8,128)(2,1)}, u32[]{:S(2)}, u32[]{:S(2)}) collective-permute-start(bf16[512,256]{1,0:T(8,128)(2,1)S(1)} %copy-done.12), channel_id=1, source_target_pairs={{0,16},{16,0},{1,17},{17,1},{2,18},{18,2},{3,19},{19,3},{4,20},{20... | collective-permute-start | bytes 786440 | tf_op jit(solution)/shard_map/ppermute | solution.py:412
  47.9 25.6 %collective-permute-start.10 = (bf16[512,256]{1,0:T(8,128)(2,1)S(1)}, bf16[512,256]{1,0:T(8,128)(2,1)}, u32[]{:S(2)}, u32[]{:S(2)}) collective-permute-start(bf16[512,256]{1,0:T(8,128)(2,1)S(1)} %copy-done.12), channel_id=1, source_target_pairs={{0,8},{4,12},{8,0},{12,4},{1,9},{5,13},{9,1},{13,5},{2,10},{6,14},... | collective-permute-start | bytes 786440 | tf_op jit(solution)/shard_map/ppermute | solution.py:408
  49.4 24.1 %collective-permute-start.9 = (bf16[512,256]{1,0:T(8,128)(2,1)S(1)}, bf16[512,256]{1,0:T(8,128)(2,1)}, u32[]{:S(2)}, u32[]{:S(2)}) collective-permute-start(bf16[512,256]{1,0:T(8,128)(2,1)S(1)} %copy-done.12), channel_id=1, source_target_pairs={{0,4},{4,0},{8,12},{12,8},{1,5},{5,1},{9,13},{13,9},{2,6},{6,2},{1... | collective-permute-start | bytes 786440 | tf_op jit(solution)/shard_map/ppermute | solution.py:408
  87.1 27.3 %all-to-all-start.1 = ((bf16[4,3,2,256,128]{4,3,2,1,0:T(8,128)(2,1)}), bf16[4,3,2,256,128]{4,3,2,1,0:T(8,128)(2,1)S(1)}, u32[]{:S(2)}, u32[]{:S(2)}) async-start(bf16[4,3,2,256,128]{4,3,2,1,0:T(8,128)(2,1)} %copy-done.6), calls=%async_computation.1 | async-start | bytes 3145728 | tf_op jit(solution)/shard_map/all_to_all | solution.py:1355
  121.0 18.0 %all-to-all-start.2 = ((bf16[4,2,256,128]{3,2,1,0:T(8,128)(2,1)}), bf16[4,2,256,128]{3,2,1,0:T(8,128)(2,1)S(1)}, u32[]{:S(2)}, u32[]{:S(2)}) async-start(bf16[4,2,256,128]{3,2,1,0:T(8,128)(2,1)} %copy-done.20), calls=%async_computation.2 | async-start | bytes 1048576 | tf_op jit(solution)/shard_map/all_to_all | solution.py:1359
  124.5 177.5 %all-gather.8.cloned.1.call-start = ((), (), s32[]{:S(2)}) async-start(), calls=%async_computation.10 | async-start | bytes 9437184 | tf_op jit(solution)/shard_map/all_gather | solution.py:1365
  194.6 401.3 %reduce-scatter.5.cloned.1.call-start = ((), (), s32[]{:S(2)}) async-start(), calls=%async_computation.12 | async-start | bytes 9437184 | tf_op jit(solution)/shard_map/reduce_scatter | solution.py:1380
  277.4 18.6 %collective-permute-start.35 = (bf16[128,2048]{1,0:T(8,128)(2,1)}, bf16[128,2048]{1,0:T(8,128)(2,1)S(1)}, u32[]{:S(2)}, u32[]{:S(2)}) collective-permute-start(bf16[128,2048]{1,0:T(8,128)(2,1)} %add_convert_fusion.4), channel_id=1, source_target_pairs={{1,0},{2,1},{3,2},{5,4},{6,5},{7,6},{9,8},{10,9},{11,10},{13,12},{... | collective-permute-start | bytes 1572872 | tf_op jit(solution)/shard_map/ppermute | solution.py:605
  278.7 18.9 %collective-permute-start.34 = (bf16[128,2048]{1,0:T(8,128)(2,1)}, bf16[128,2048]{1,0:T(8,128)(2,1)}, u32[]{:S(2)}, u32[]{:S(2)}) collective-permute-start(bf16[128,2048]{1,0:T(8,128)(2,1)} %add_convert_fusion.5), channel_id=1, source_target_pairs={{0,1},{1,2},{2,3},{4,5},{5,6},{6,7},{8,9},{9,10},{10,11},{12,13},{... | collective-permute-start | bytes 1572872 | tf_op jit(solution)/shard_map/ppermute | solution.py:604
  302.0 15.9 %collective-permute-start.39 = (bf16[128,2048]{1,0:T(8,128)(2,1)}, bf16[128,2048]{1,0:T(8,128)(2,1)S(1)}, u32[]{:S(2)}, u32[]{:S(2)}) collective-permute-start(bf16[128,2048]{1,0:T(8,128)(2,1)} %copy-done.29), channel_id=1, source_target_pairs={{1,0},{2,1},{3,2},{5,4},{6,5},{7,6},{9,8},{10,9},{11,10},{13,12},{... | collective-permute-start | bytes 1572872 | tf_op jit(solution)/shard_map/ppermute | solution.py:591
  303.3 15.9 %collective-permute-start.36 = (bf16[128,2048]{1,0:T(8,128)(2,1)}, bf16[128,2048]{1,0:T(8,128)(2,1)S(1)}, u32[]{:S(2)}, u32[]{:S(2)}) collective-permute-start(bf16[128,2048]{1,0:T(8,128)(2,1)} %copy-done.29), channel_id=1, source_target_pairs={{0,1},{1,2},{2,3},{4,5},{5,6},{6,7},{8,9},{9,10},{10,11},{12,13},{... | collective-permute-start | bytes 1572872 | tf_op jit(solution)/shard_map/ppermute | solution.py:590
  352.6 243.4 %reduce-scatter.3.cloned.1.call-start = ((), (), s32[]{:S(2)}) async-start(), calls=%async_computation.11 | async-start | bytes 18874368 | tf_op jit(solution)/shard_map/reduce_scatter | solution.py:1380
  389.2 14.8 %collective-permute-start.45 = (bf16[128,2048]{1,0:T(8,128)(2,1)}, bf16[128,2048]{1,0:T(8,128)(2,1)S(1)}, u32[]{:S(2)}, u32[]{:S(2)}) collective-permute-start(bf16[128,2048]{1,0:T(8,128)(2,1)} %get-tuple-element.263), channel_id=1, source_target_pairs={{2,1},{3,2},{6,5},{7,6},{10,9},{11,10},{14,13},{15,14},{18,17},{19... | collective-permute-start | bytes 1572872 | tf_op jit(solution)/shard_map/ppermute | solution.py:605
  389.9 15.8 %collective-permute-start.44 = (bf16[128,2048]{1,0:T(8,128)(2,1)}, bf16[128,2048]{1,0:T(8,128)(2,1)}, u32[]{:S(2)}, u32[]{:S(2)}) collective-permute-start(bf16[128,2048]{1,0:T(8,128)(2,1)} %get-tuple-element.264), channel_id=1, source_target_pairs={{0,1},{1,2},{4,5},{5,6},{8,9},{9,10},{12,13},{13,14},{16,17},{17,1... | collective-permute-start | bytes 1572872 | tf_op jit(solution)/shard_map/ppermute | solution.py:604
  428.3 25.5 %all-to-all-start.3 = ((bf16[16,2,64,128]{3,2,1,0:T(8,128)(2,1)}), bf16[16,2,64,128]{3,2,1,0:T(8,128)(2,1)S(1)}, u32[]{:S(2)}, u32[]{:S(2)}) async-start(bf16[16,2,64,128]{3,2,1,0:T(8,128)(2,1)} %bitcast.10), calls=%async_computation.3 | async-start | bytes 1048576 | tf_op jit(solution)/shard_map/all_to_all | solution.py:1391
  441.6 28.7 %collective-permute-start.51 = (bf16[128,2048]{1,0:T(8,128)(2,1)S(1)}, bf16[128,2048]{1,0:T(8,128)(2,1)}, u32[]{:S(2)}, u32[]{:S(2)}) collective-permute-start(bf16[128,2048]{1,0:T(8,128)(2,1)S(1)} %get-tuple-element.213.grad_ref.refs_0_), channel_id=1, source_target_pairs={{1,0},{2,1},{3,2},{5,4},{6,5},{7,6},{9,8},{10,9},{11,10},{13,12},{... | collective-permute-start | bytes 1572872 | tf_op jit(solution)/shard_map/ppermute | solution.py:591
  442.9 28.7 %collective-permute-start.48 = (bf16[128,2048]{1,0:T(8,128)(2,1)S(1)}, bf16[128,2048]{1,0:T(8,128)(2,1)}, u32[]{:S(2)}, u32[]{:S(2)}) collective-permute-start(bf16[128,2048]{1,0:T(8,128)(2,1)S(1)} %get-tuple-element.213.grad_ref.refs_0_), channel_id=1, source_target_pairs={{0,1},{1,2},{2,3},{4,5},{5,6},{6,7},{8,9},{9,10},{10,11},{12,13},{... | collective-permute-start | bytes 1572872 | tf_op jit(solution)/shard_map/ppermute | solution.py:590
  466.7 32.6 %all-to-all-start.4 = ((bf16[4,3,2,256,128]{4,3,2,1,0:T(8,128)(2,1)}), bf16[4,3,2,256,128]{4,3,2,1,0:T(8,128)(2,1)S(1)}, u32[]{:S(2)}, u32[]{:S(2)}) async-start(bf16[4,3,2,256,128]{4,3,2,1,0:T(8,128)(2,1)} %copy-done.5), calls=%async_computation.4 | async-start | bytes 3145728 | tf_op jit(solution)/shard_map/all_to_all | solution.py:1395
  536.8 14.6 %collective-permute-start.55 = (bf16[128,2048]{1,0:T(8,128)(2,1)S(1)}, bf16[128,2048]{1,0:T(8,128)(2,1)S(1)}, u32[]{:S(2)}, u32[]{:S(2)}) collective-permute-start(bf16[128,2048]{1,0:T(8,128)(2,1)S(1)} %get-tuple-element.223), channel_id=1, source_target_pairs={{3,2},{7,6},{11,10},{15,14},{19,18},{23,22},{27,26},{31,30}} | collective-permute-start | bytes 1572872 | tf_op jit(solution)/shard_map/ppermute | solution.py:605
  549.9 18.3 %collective-permute-start.59 = (bf16[128,2176]{1,0:T(8,128)(2,1)S(1)}, bf16[128,2176]{1,0:T(8,128)(2,1)S(1)}, u32[]{:S(2)}, u32[]{:S(2)}) collective-permute-start(bf16[128,2176]{1,0:T(8,128)(2,1)S(1)} %get-tuple-element.231), channel_id=1, source_target_pairs={{0,4},{4,0},{8,12},{12,8},{1,5},{5,1},{9,13},{13,9},{2,6},{6,2},{1... | collective-permute-start | bytes 1671176 | tf_op jit(solution)/shard_map/ppermute | solution.py:408
  551.3 16.9 %collective-permute-start.60 = (bf16[128,2176]{1,0:T(8,128)(2,1)S(1)}, bf16[128,2176]{1,0:T(8,128)(2,1)S(1)}, u32[]{:S(2)}, u32[]{:S(2)}) collective-permute-start(bf16[128,2176]{1,0:T(8,128)(2,1)S(1)} %get-tuple-element.232), channel_id=1, source_target_pairs={{0,8},{4,12},{8,0},{12,4},{1,9},{5,13},{9,1},{13,5},{2,10},{6,14},... | collective-permute-start | bytes 1671176 | tf_op jit(solution)/shard_map/ppermute | solution.py:408
  551.7 24.4 %collective-permute-start.58 = (bf16[128,2048]{1,0:T(8,128)(2,1)S(1)}, bf16[128,2048]{1,0:T(8,128)(2,1)S(1)}, u32[]{:S(2)}, u32[]{:S(2)}) collective-permute-start(bf16[128,2048]{1,0:T(8,128)(2,1)S(1)} %get-tuple-element.261), channel_id=1, source_target_pairs={{2,1},{3,2},{6,5},{7,6},{10,9},{11,10},{14,13},{15,14},{18,17},{19... | collective-permute-start | bytes 1572872 | tf_op jit(solution)/shard_map/ppermute | solution.py:605
  552.4 23.7 %collective-permute-start.57 = (bf16[128,2048]{1,0:T(8,128)(2,1)S(1)}, bf16[128,2048]{1,0:T(8,128)(2,1)S(1)}, u32[]{:S(2)}, u32[]{:S(2)}) collective-permute-start(bf16[128,2048]{1,0:T(8,128)(2,1)S(1)} %get-tuple-element.262), channel_id=1, source_target_pairs={{0,1},{1,2},{4,5},{5,6},{8,9},{9,10},{12,13},{13,14},{16,17},{17,1... | collective-permute-start | bytes 1572872 | tf_op jit(solution)/shard_map/ppermute | solution.py:604
  576.1 26.6 %collective-permute-start.63 = (bf16[256,2176]{1,0:T(8,128)(2,1)}, bf16[256,2176]{1,0:T(8,128)(2,1)S(1)}, u32[]{:S(2)}, u32[]{:S(2)}) collective-permute-start(bf16[256,2176]{1,0:T(8,128)(2,1)} %get-tuple-element.241), channel_id=1, source_target_pairs={{0,4},{4,0},{8,12},{12,8},{1,5},{5,1},{9,13},{13,9},{2,6},{6,2},{1... | collective-permute-start | bytes 3342344 | tf_op jit(solution)/shard_map/ppermute | solution.py:408
  577.6 26.2 %collective-permute-start.64 = (bf16[256,2176]{1,0:T(8,128)(2,1)}, bf16[256,2176]{1,0:T(8,128)(2,1)}, u32[]{:S(2)}, u32[]{:S(2)}) collective-permute-start(bf16[256,2176]{1,0:T(8,128)(2,1)} %get-tuple-element.242), channel_id=1, source_target_pairs={{0,8},{4,12},{8,0},{12,4},{1,9},{5,13},{9,1},{13,5},{2,10},{6,14},... | collective-permute-start | bytes 3342344 | tf_op jit(solution)/shard_map/ppermute | solution.py:408
  578.4 15.1 %collective-permute-start.62 = (bf16[128,2048]{1,0:T(8,128)(2,1)S(1)}, bf16[128,2048]{1,0:T(8,128)(2,1)S(1)}, u32[]{:S(2)}, u32[]{:S(2)}) collective-permute-start(bf16[128,2048]{1,0:T(8,128)(2,1)S(1)} %add_convert_fusion), channel_id=1, source_target_pairs={{1,0},{2,1},{3,2},{5,4},{6,5},{7,6},{9,8},{10,9},{11,10},{13,12},{... | collective-permute-start | bytes 1572872 | tf_op jit(solution)/shard_map/ppermute | solution.py:605
  579.7 15.0 %collective-permute-start.61 = (bf16[128,2048]{1,0:T(8,128)(2,1)S(1)}, bf16[128,2048]{1,0:T(8,128)(2,1)S(1)}, u32[]{:S(2)}, u32[]{:S(2)}) collective-permute-start(bf16[128,2048]{1,0:T(8,128)(2,1)S(1)} %add_convert_fusion.1), channel_id=1, source_target_pairs={{0,1},{1,2},{2,3},{4,5},{5,6},{6,7},{8,9},{9,10},{10,11},{12,13},{... | collective-permute-start | bytes 1572872 | tf_op jit(solution)/shard_map/ppermute | solution.py:604
  (97 other events, 842.5 us)
Sparse Core Ops, SparseCore 0:
  16.7 27.3 all-gather.3
  47.4 149.7 all-gather.5
  199.1 54.3 all-gather.7
  352.7 76.0 reduce-scatter.4
  432.6 128.5 reduce-scatter.2

commit v4 on v3

--- a/solution.py
+++ b/solution.py
@@ -400,8 +400,10 @@
 
 
 LOW = jnp.bfloat16
-VMEM_LIMIT = 50 * 1024 * 1024
-PARAMS = pltpu.CompilerParams(vmem_limit_bytes=VMEM_LIMIT)
+
+
+def vmem(mebibytes):
+    return pltpu.CompilerParams(vmem_limit_bytes=mebibytes * 1024 * 1024)
 
 
 def to_neighbour(values, flip):
@@ -454,7 +456,7 @@
         + [pl.BlockSpec(memory_space=pltpu.VMEM)] * 10,
         out_specs=pl.BlockSpec(memory_space=pltpu.VMEM),
         out_shape=jax.ShapeDtypeStruct((height, 8 * block), pieces[0].dtype),
-        compiler_params=PARAMS,
+        compiler_params=vmem(50),
         name="assemble_columns",
     )(order, *pieces)
 
@@ -485,7 +487,7 @@
             jax.ShapeDtypeStruct((rows, columns), jnp.float32),
             jax.ShapeDtypeStruct((width, columns), LOW),
         ],
-        compiler_params=PARAMS,
+        compiler_params=vmem(50),
         name="project_in",
     )(order, rows_low, *pieces)
 
@@ -570,7 +572,7 @@
             num_scalar_prefetch=1, grid=(count,), in_specs=in_specs, out_specs=out_specs
         ),
         out_shape=out_shape,
-        compiler_params=PARAMS,
+        compiler_params=vmem(24),
         name="grad_blocks",
     )(order, *lefts, *rights, extra, *more)
 
@@ -611,8 +613,9 @@
 
 
 def sum_line(values):
-    flat = lax.optimization_barrier(values.reshape(-1, 128))
-    return lax.optimization_barrier(lax.psum(flat, "tp"))
+    flat = lax.optimization_barrier(values.reshape(1, -1, 128))
+    flat = lax.all_to_all(jnp.broadcast_to(flat, (4,) + flat.shape[1:]), "tp", 0, 0, tiled=True)
+    return jnp.sum(lax.optimization_barrier(flat), axis=0)
 
 
 def contract(left, right, left_dim, right_dim):
@@ -662,7 +665,7 @@
         ],
         out_specs=pl.BlockSpec((heads, 3, seqs, own, head_dim), lambda t: (0, 0, 0, t, 0)),
         out_shape=jax.ShapeDtypeStruct((heads, 3, seqs, length, head_dim), LOW),
-        compiler_params=PARAMS,
+        compiler_params=vmem(50),
         name="prepare",
     )(raw, squares, gains, cosines, sines)
 
@@ -709,7 +712,7 @@
             jax.ShapeDtypeStruct((blocks, seqs, length, head_dim), LOW),
             jax.ShapeDtypeStruct((blocks, seqs, length, 1), jnp.float32),
         ],
-        compiler_params=PARAMS,
+        compiler_params=vmem(50),
         name="attend",
     )(parts)
 
@@ -757,7 +760,7 @@
             pltpu.VMEM((blocks * length, head_dim), jnp.float32),
             pltpu.VMEM((blocks * length, head_dim), jnp.float32),
         ],
-        compiler_params=PARAMS,
+        compiler_params=vmem(50),
         name="attend_back",
     )(parts, grad_context, log_total)
 
@@ -797,7 +800,7 @@
         ),
         out_shape=[jax.ShapeDtypeStruct((4 * own_rows, span), LOW)]
         + [jax.ShapeDtypeStruct((own_rows, width), LOW)] * 4,
-        compiler_params=PARAMS,
+        compiler_params=vmem(50),
         name="project_out",
     )(slots, context, weights)
 
@@ -823,7 +826,7 @@
         ],
         out_specs=pl.BlockSpec((heads, 1, seqs, own, head_dim), lambda j: (0, j, 0, 0, 0)),
         out_shape=jax.ShapeDtypeStruct((heads, 4, seqs, own, head_dim), LOW),
-        compiler_params=PARAMS,
+        compiler_params=vmem(50),
         name="project_out_back",
     )(grads, weights)
 
@@ -837,7 +840,7 @@
     return pl.pallas_call(
         body,
         out_shape=jax.ShapeDtypeStruct((4 * own, width), LOW),
-        compiler_params=PARAMS,
+        compiler_params=vmem(14),
         name="rows_of",
     )(*pieces)
 
@@ -895,7 +898,7 @@
             jax.ShapeDtypeStruct((2, seqs, length, 1), jnp.float32),
             jax.ShapeDtypeStruct((1, 2 * span), jnp.float32),
         ],
-        compiler_params=PARAMS,
+        compiler_params=vmem(14),
         name="unprepare",
     )(grads, raw, squares, gains, cosines, sines)
 
@@ -953,7 +956,7 @@
         ),
         out_shape=[jax.ShapeDtypeStruct((rows, 3 * span), LOW)]
         + [jax.ShapeDtypeStruct((own_rows, d_model), LOW)] * 4,
-        compiler_params=PARAMS,
+        compiler_params=vmem(32),
         name="project_in_back",
     )(slots, grads, scaled, raw, squares, dots, weights)
 
@@ -995,7 +998,7 @@
             full,
             jax.ShapeDtypeStruct((rows, 1), jnp.float32),
         ],
-        compiler_params=PARAMS,
+        compiler_params=vmem(50),
         name="attn_norm",
     )(*parts, tokens, gains)
 
@@ -1022,7 +1025,7 @@
         body,
         out_shape=[jax.ShapeDtypeStruct((rows, width), LOW)] * 2
         + [jax.ShapeDtypeStruct((1, width), jnp.float32)],
-        compiler_params=PARAMS,
+        compiler_params=vmem(50),
         name="mlp_norm",
     )(*parts, hidden, cotangent, gains)
 
@@ -1053,7 +1056,7 @@
             jax.ShapeDtypeStruct((rows, width), LOW),
             jax.ShapeDtypeStruct((1, width), jnp.float32),
         ],
-        compiler_params=PARAMS,
+        compiler_params=vmem(50),
         name="attn_norm_back",
     )(*parts, cotangent, unit, inv, gains)
 
@@ -1080,7 +1083,7 @@
         + [pl.BlockSpec((tile, height), lambda j: (j, 0))],
         out_shape=[jax.ShapeDtypeStruct((height, units), jnp.float32)] * 2
         + [jax.ShapeDtypeStruct((units, height), jnp.float32)],
-        compiler_params=PARAMS,
+        compiler_params=vmem(50),
         name="ff_totals",
     )(gate_up, gate_up, down)
 
@@ -1107,7 +1110,7 @@
             jax.ShapeDtypeStruct((span, height), jnp.float32),
             jax.ShapeDtypeStruct((height, more), jnp.float32),
         ],
-        compiler_params=PARAMS,
+        compiler_params=vmem(50),
         name="plane_totals",
     )(*sums)
 
@@ -1167,7 +1170,7 @@
         + [jax.ShapeDtypeStruct((rows, hidden_units), LOW)] * 3
         + [jax.ShapeDtypeStruct((own, width), LOW)] * parts,
         scratch_shapes=[pltpu.VMEM((rows, width), jnp.float32)],
-        compiler_params=PARAMS,
+        compiler_params=vmem(50),
         name="feed_forward",
     )(*pieces, weights, weights, weights)
 
@@ -1217,7 +1220,7 @@
         out_shape=[jax.ShapeDtypeStruct((rows, hidden_units), LOW)] * 2
         + [jax.ShapeDtypeStruct((own, width), LOW)] * parts,
         scratch_shapes=[pltpu.VMEM((rows, width), jnp.float32)],
-        compiler_params=PARAMS,
+        compiler_params=vmem(50),
         name="feed_forward_back",
     )(rows_low, gate, up, weights, weights, weights)
 
@@ -1251,7 +1254,7 @@
             jax.ShapeDtypeStruct((rows, width), LOW),
             jax.ShapeDtypeStruct((width, columns), LOW),
         ],
-        compiler_params=PARAMS,
+        compiler_params=vmem(50),
         name="down_grad",
     )(*pieces, mixed)
 
@@ -1276,7 +1279,7 @@
         out_specs=pl.BlockSpec((tile, columns), lambda j: (j, place)),
         out_shape=jax.ShapeDtypeStruct((width, all_columns), LOW),
         input_output_aliases={2: 0} if given else {},
-        compiler_params=PARAMS,
+        compiler_params=vmem(50),
         name="weight_grad",
     )(left, right, *given)
 
@@ -1346,7 +1349,8 @@
             jnp.sum(jnp.square(raw[:, head_span : 2 * head_span]), axis=-1),
         ]
     )
-    squares, out_firsts = lax.optimization_barrier((sum_line(squares), out_firsts))
+    raw, out_firsts = lax.optimization_barrier((raw, out_firsts))
+    squares = sum_line(squares)
     squares = squares.reshape(2, seqs, length, 1)
     out_pieces, _ = gather_plane(w_out, out_firsts)
     raw = raw.reshape(seqs, length, 3 * head_span)

time: 625 us -> 614 us (0.982)
  blocking collectives: 24.4 us -> 0 us
  waiting for transfers between devices: 209 us -> 225 us
  Pallas kernels: 154 us -> 143 us
  starting transfers between devices: 147 us -> 158 us
    psum x2 -> x0, blocking collectives: 24.4 us -> none  [sum_line(): return lax.optimization_barrier(lax.psum(flat, 'tp'))]
    all_to_all x0 -> x2, starting transfers between devices: none -> 11.3 us  [sum_line(): lax.all_to_all(jnp.broadcast_to(flat, (4,) + flat.shape[1:]), 'tp', 0, 0,...]
    all_to_all x0 -> x2, waiting for transfers between devices: none -> 8.36 us  [sum_line(): lax.all_to_all(jnp.broadcast_to(flat, (4,) + flat.shape[1:]), 'tp', 0, 0,...]
    pallas_call x3, Pallas kernels: 17.6 us -> 10.7 us  [grad_blocks(): pl.pallas_call(body, grid_spec=pltpu.PrefetchScalarGridSpec(num_scalar_pr...]
  transfers between devices with their start and end apart: 76 -> 78, of which waited for: 37 -> 36; matrix products, arithmetic and copies ran while one was open for 5% -> 5% of each run, Pallas kernels for 23% -> 22%
where the time goes in v4:
time: 614 us; the launch traced here: 603 us
  waiting for transfers between devices  225 us (37%)
  starting transfers between devices  158 us (26%)
  Pallas kernels  143 us (23%)
  local copies, waits for them, and re-layouts  43.9 us (7%)
  other arithmetic  16.7 us (3%)
  between operations  15.5 us (3%)
    ppermute x9, waiting for transfers between devices, gather_line(): down = lax.ppermute(down, 'tp', [(i, i - 1) for i in range(1, 5 - t)])  70.4 us
    ppermute x12, starting transfers between devices, scatter_line(): up = lax.ppermute(up, 'tp', [(i, i + 1) for i in range(t)])  56.9 us
    ppermute x12, waiting for transfers between devices, scatter_line(): up = lax.ppermute(up, 'tp', [(i, i + 1) for i in range(t)])  45.8 us
    unnamed x113, local copies, waits for them, and re-layouts  33.4 us
    ppermute x12, waiting for transfers between devices, to_neighbour(): return lax.ppermute(values, 'seq', [(i, i ^ flip) for i in range(4)])  26.4 us
    ppermute x12, waiting for transfers between devices, scatter_line(): down = lax.ppermute(down, 'tp', [(i, i - 1) for i in range(4 - t, 4)])  25.8 us
    all_to_all x1, waiting for transfers between devices, on_plane(): parts = lax.all_to_all(parts, 'seq', 0, 0, tiled=True)  25 us
    pallas_call x1, Pallas kernels, feed_forward_back(): pl.pallas_call(body, grid=(tiles,), in_specs=[pl.BlockSpec((rows, width),...  23.3 us
  transfers between devices with their start and end apart: 78, of which 36 were waited for; matrix products, arithmetic and copies ran while one was open for 5% of the time, Pallas kernels for 22%

profile of v4, /device:TPU:0, one launch (start us, length us, event | category | flops | bytes accessed | tf_op | source)
XLA Modules:
  0.0 602.8 jit_solution(6053985989628317051)
XLA Ops:
  26.8 6.2 %all-to-all-done = bf16[8,2,320]{2,1,0:T(2,128)(2,1)S(1)} async-done(((bf16[8,2,320]{2,1,0:T(2,128)(2,1)}), bf16[8,2,320]{2,1,0:T(2,128)(2,1)S(1)}, u32[]{:S(2)}, u32[]{:S(2)}) %all-to-all-start) | async-done | bytes 10272 | tf_op jit(solution)/shard_map/all_to_all | solution.py:1315
  37.3 8.3 %collective-permute-done.2.refs_3_ = bf16[128,1536]{1,0:T(8,128)(2,1)S(1)} collective-permute-done((bf16[128,1536]{1,0:T(8,128)(2,1)S(1)}, bf16[128,1536]{1,0:T(8,128)(2,1)S(1)}, u32[]{:S(2)}, u32[]{:S(2)}) %collective-permute-start.2) | collective-permute-done | bytes 393248 | tf_op jit(solution)/shard_map/ppermute | solution.py:410
  51.8 9.3 %project_in.1 = (f32[512,1536]{1,0:T(8,128)}, bf16[2048,1536]{1,0:T(8,128)(2,1)}) custom-call(s32[8]{0:T(128)S(1)} %iota_xor_fusion.order_ref, bf16[512,2048]{1,0:T(8,128)(2,1)} %bitcast.34, bf16[256,1536]{1,0:T(8,128)(2,1)S(1)} %constant_dynamic-update-slice_fusion.refs_0_, bf16[256,1536]{1,0:T(8,128)(2,1)S(1)} %collective-permute-done.refs_1_, ...), custom_call_target="tpu_custom_call" | custom-call | tf_op jit(solution)/shard_map/project_in/pallas_call | solution.py:474
  89.5 25.0 %all-to-all-done.2.parts_ref = bf16[4,3,2,256,128]{4,3,2,1,0:T(8,128)(2,1)S(1)} async-done(((bf16[4,3,2,256,128]{4,3,2,1,0:T(8,128)(2,1)}), bf16[4,3,2,256,128]{4,3,2,1,0:T(8,128)(2,1)S(1)}, u32[]{:S(2)}, u32[]{:S(2)}) %all-to-all-start.2) | async-done | bytes 1572896 | tf_op jit(solution)/shard_map/all_to_all | solution.py:1359
  131.0 8.1 %all-to-all-done.3.context_ref = bf16[4,2,256,128]{3,2,1,0:T(8,128)(2,1)S(1)} async-done(((bf16[4,2,256,128]{3,2,1,0:T(8,128)(2,1)}), bf16[4,2,256,128]{3,2,1,0:T(8,128)(2,1)S(1)}, u32[]{:S(2)}, u32[]{:S(2)}) %all-to-all-start.3) | async-done | bytes 524320 | tf_op jit(solution)/shard_map/all_to_all | solution.py:1363
  146.7 9.8 %collective-permute-done.18 = bf16[128,2048]{1,0:T(8,128)(2,1)S(1)} collective-permute-done((bf16[128,2048]{1,0:T(8,128)(2,1)S(1)}, bf16[128,2048]{1,0:T(8,128)(2,1)S(1)}, u32[]{:S(2)}, u32[]{:S(2)}) %collective-permute-start.18) | collective-permute-done | bytes 524320 | tf_op jit(solution)/shard_map/ppermute | solution.py:606
  162.6 9.0 %collective-permute-done.20 = bf16[128,2048]{1,0:T(8,128)(2,1)S(1)} collective-permute-done((bf16[128,2048]{1,0:T(8,128)(2,1)S(1)}, bf16[128,2048]{1,0:T(8,128)(2,1)S(1)}, u32[]{:S(2)}, u32[]{:S(2)}) %collective-permute-start.20) | collective-permute-done | bytes 524320 | tf_op jit(solution)/shard_map/ppermute | solution.py:606
  196.9 6.2 %collective-permute-done.27.refs_4_ = bf16[128,2048]{1,0:T(8,128)(2,1)S(1)} collective-permute-done((bf16[128,2048]{1,0:T(8,128)(2,1)S(1)}, bf16[128,2048]{1,0:T(8,128)(2,1)S(1)}, u32[]{:S(2)}, u32[]{:S(2)}) %collective-permute-start.27) | collective-permute-done | bytes 524320 | tf_op jit(solution)/shard_map/ppermute | solution.py:593
  205.1 10.2 %collective-permute-done.28.refs_5_ = bf16[128,2048]{1,0:T(8,128)(2,1)S(1)} collective-permute-done((bf16[128,2048]{1,0:T(8,128)(2,1)S(1)}, bf16[128,2048]{1,0:T(8,128)(2,1)S(1)}, u32[]{:S(2)}, u32[]{:S(2)}) %collective-permute-start.28) | collective-permute-done | bytes 524320 | tf_op jit(solution)/shard_map/ppermute | solution.py:593
  218.2 8.1 %collective-permute-done.29.refs_6_ = bf16[128,2048]{1,0:T(8,128)(2,1)S(1)} collective-permute-done((bf16[128,2048]{1,0:T(8,128)(2,1)S(1)}, bf16[128,2048]{1,0:T(8,128)(2,1)S(1)}, u32[]{:S(2)}, u32[]{:S(2)}) %collective-permute-start.29) | collective-permute-done | bytes 524320 | tf_op jit(solution)/shard_map/ppermute | solution.py:593
  227.1 22.9 %feed_forward.1 = (bf16[512,2048]{1,0:T(8,128)(2,1)}, bf16[512,2048]{1,0:T(8,128)(2,1)}, bf16[512,2048]{1,0:T(8,128)(2,1)}, bf16[512,2048]{1,0:T(8,128)(2,1)}, b...) custom-call(bf16[128,2048]{1,0:T(8,128)(2,1)S(1)} %get-tuple-element, ...), custom_call_target="tpu_custom_call" | custom-call | tf_op jit(solution)/shard_map/feed_forward/pallas_call | solution.py:1164
  252.0 8.1 %collective-permute-done.30 = bf16[128,2048]{1,0:T(8,128)(2,1)S(1)} collective-permute-done((bf16[128,2048]{1,0:T(8,128)(2,1)S(1)}, bf16[128,2048]{1,0:T(8,128)(2,1)S(1)}, u32[]{:S(2)}, u32[]{:S(2)}) %collective-permute-start.30) | collective-permute-done | bytes 524320 | tf_op jit(solution)/shard_map/ppermute | solution.py:606
  266.3 7.3 %collective-permute-done.32 = bf16[128,2048]{1,0:T(8,128)(2,1)S(1)} collective-permute-done((bf16[128,2048]{1,0:T(8,128)(2,1)S(1)}, bf16[128,2048]{1,0:T(8,128)(2,1)S(1)}, u32[]{:S(2)}, u32[]{:S(2)}) %collective-permute-start.32) | collective-permute-done | bytes 524320 | tf_op jit(solution)/shard_map/ppermute | solution.py:606
  276.0 12.3 %collective-permute-start.34 = (bf16[128,2048]{1,0:T(8,128)(2,1)}, bf16[128,2048]{1,0:T(8,128)(2,1)S(1)}, u32[]{:S(2)}, u32[]{:S(2)}) collective-permute-start(bf16[128,2048]{1,0:T(8,128)(2,1)} %add_convert_fusion.5), channel_id=1, source_target_pairs={{0,1},{1,2},{2,3},{4,5},{5,6},{6,7},{8,9},{9,10},{10,11},{12,13},{... | collective-permute-start | bytes 1572872 | tf_op jit(solution)/shard_map/ppermute | solution.py:606
  289.9 6.1 %collective-permute-done.35.down_ref = bf16[128,2048]{1,0:T(8,128)(2,1)S(1)} collective-permute-done((bf16[128,2048]{1,0:T(8,128)(2,1)S(1)}, bf16[128,2048]{1,0:T(8,128)(2,1)S(1)}, u32[]{:S(2)}, u32[]{:S(2)}) %collective-permute-start.35) | collective-permute-done | bytes 524320 | tf_op jit(solution)/shard_map/ppermute | solution.py:607
  307.6 7.7 %collective-permute-done.39.refs_4_ = bf16[128,2048]{1,0:T(8,128)(2,1)S(1)} collective-permute-done((bf16[128,2048]{1,0:T(8,128)(2,1)S(1)}, bf16[128,2048]{1,0:T(8,128)(2,1)S(1)}, u32[]{:S(2)}, u32[]{:S(2)}) %collective-permute-start.39) | collective-permute-done | bytes 524320 | tf_op jit(solution)/shard_map/ppermute | solution.py:593
  317.4 10.7 %collective-permute-done.40.refs_5_ = bf16[128,2048]{1,0:T(8,128)(2,1)S(1)} collective-permute-done((bf16[128,2048]{1,0:T(8,128)(2,1)S(1)}, bf16[128,2048]{1,0:T(8,128)(2,1)S(1)}, u32[]{:S(2)}, u32[]{:S(2)}) %collective-permute-start.40) | collective-permute-done | bytes 524320 | tf_op jit(solution)/shard_map/ppermute | solution.py:593
  330.1 9.1 %collective-permute-done.41.refs_6_ = bf16[128,2048]{1,0:T(8,128)(2,1)S(1)} collective-permute-done((bf16[128,2048]{1,0:T(8,128)(2,1)S(1)}, bf16[128,2048]{1,0:T(8,128)(2,1)S(1)}, u32[]{:S(2)}, u32[]{:S(2)}) %collective-permute-start.41) | collective-permute-done | bytes 524320 | tf_op jit(solution)/shard_map/ppermute | solution.py:593
  339.1 8.4 %down_grad.1 = (bf16[512,2048]{1,0:T(8,128)(2,1)}, bf16[2048,2048]{1,0:T(8,128)(2,1)}) custom-call(bf16[128,2048]{1,0:T(8,128)(2,1)S(1)} %get-tuple-element.194.refs_0_, bf16[128,2048]{1,0:T(8,128)(2,1)S(1)} %collective-permute-done.36.refs_1_, bf16[128,2048]{1,0:T(8,128)(2,1)S(1)} %collective-permute-done.37.refs_2_, ...), custom_call_target="tpu_custom_call" | custom-call | tf_op jit(solution)/shard_map/down_grad/pallas_call | solution.py:1244
  347.6 23.3 %feed_forward_back.1 = (bf16[512,2048]{1,0:T(8,128)(2,1)}, bf16[512,2048]{1,0:T(8,128)(2,1)}, bf16[128,2048]{1,0:T(8,128)(2,1)S(1)}, bf16[128,2048]{1,0:T(8,128)...) custom-call(bf16[512,2048]{1,0:T(8,128)(2,1)} %get-tuple-element.196.rows_ref, ...), custom_call_target="tpu_custom_call" | custom-call | tf_op jit(solution)/shard_map/feed_forward_back/pallas_call | solution.py:1213
  373.4 8.2 %weight_grad.2.refs_0_ = bf16[2048,4096]{1,0:T(8,128)(2,1)} custom-call(bf16[512,2048]{1,0:T(8,128)(2,1)S(1)} %copy-done.6, bf16[512,2048]{1,0:T(8,128)(2,1)} %get-tuple-element.204.right_ref), custom_call_target="tpu_custom_call" | custom-call | tf_op jit(solution)/shard_map/weight_grad/pallas_call | solution.py:1271
  388.7 8.4 %weight_grad.3 = bf16[2048,4096]{1,0:T(8,128)(2,1)} custom-call(bf16[512,2048]{1,0:T(8,128)(2,1)S(1)} %copy-done.6, bf16[512,2048]{1,0:T(8,128)(2,1)} %get-tuple-element.207.right_ref, bf16[2048,4096]{1,0:T(8,128)(2,1)} %weight_grad.2.refs_0_), custom_call_target="tpu_custom_call", output_to_operand_aliasing={{}: (2, {})} | custom-call | tf_op jit(solution)/shard_map/weight_grad/pallas_call | solution.py:1271
  417.1 6.2 %project_out_back.1 = bf16[4,4,2,64,128]{4,3,2,1,0:T(8,128)(2,1)} custom-call(bf16[128,2048]{1,0:T(8,128)(2,1)} %get-tuple-element.213.grad_ref.refs_0_, bf16[2048,2048]{1,0:T(8,128)(2,1)} %all-gather.8.cloned.1.call-done.weight_ref), custom_call_target="tpu_custom_call" | custom-call | tf_op jit(solution)/shard_map/project_out_back/pallas_call | solution.py:820
  423.3 8.3 %all-to-all-start.4 = ((bf16[16,2,64,128]{3,2,1,0:T(8,128)(2,1)}), bf16[16,2,64,128]{3,2,1,0:T(8,128)(2,1)S(1)}, u32[]{:S(2)}, u32[]{:S(2)}) async-start(bf16[16,2,64,128]{3,2,1,0:T(8,128)(2,1)} %bitcast.11), calls=%async_computation.4 | async-start | bytes 1048576 | tf_op jit(solution)/shard_map/all_to_all | solution.py:1395
  447.0 7.9 %attend_back.1 = bf16[4,3,2,256,128]{4,3,2,1,0:T(8,128)(2,1)} custom-call(bf16[4,3,2,256,128]{4,3,2,1,0:T(8,128)(2,1)} %copy-done.5, bf16[4,4,2,64,128]{4,3,2,1,0:T(8,128)(2,1)S(1)} %bitcast.41, f32[4,2,256,1]{3,2,1,0:T(8,128)S(1)} %copy-done.23), custom_call_target="tpu_custom_call" | custom-call | tf_op jit(solution)/shard_map/attend_back/pallas_call | solution.py:749
  461.6 9.3 %collective-permute-done.52.refs_5_ = bf16[128,2048]{1,0:T(8,128)(2,1)S(1)} collective-permute-done((bf16[128,2048]{1,0:T(8,128)(2,1)}, bf16[128,2048]{1,0:T(8,128)(2,1)S(1)}, u32[]{:S(2)}, u32[]{:S(2)}) %collective-permute-start.52) | collective-permute-done | bytes 524320 | tf_op jit(solution)/shard_map/ppermute | solution.py:593
  472.9 9.2 %collective-permute-done.53.refs_6_ = bf16[128,2048]{1,0:T(8,128)(2,1)S(1)} collective-permute-done((bf16[128,2048]{1,0:T(8,128)(2,1)S(1)}, bf16[128,2048]{1,0:T(8,128)(2,1)S(1)}, u32[]{:S(2)}, u32[]{:S(2)}) %collective-permute-start.53) | collective-permute-done | bytes 524320 | tf_op jit(solution)/shard_map/ppermute | solution.py:593
  493.5 6.4 %all-to-all-start.7 = ((f32[4,8,128]{2,1,0:T(8,128)}), f32[4,8,128]{2,1,0:T(8,128)S(1)}, u32[]{:S(2)}, u32[]{:S(2)}) async-start(f32[4,8,128]{2,1,0:T(8,128)} %broadcast_in_dim.28), calls=%async_computation.7 | async-start | bytes 32768 | tf_op jit(solution)/shard_map/all_to_all | solution.py:617
  513.3 7.1 %project_in_back.1 = (bf16[512,1536]{1,0:T(8,128)(2,1)S(1)}, bf16[128,2048]{1,0:T(8,128)(2,1)S(1)}, bf16[128,2048]{1,0:T(8,128)(2,1)S(1)}, bf16[128,2048]{1,0:T(8,128)(2,1)S(1)}, bf16[128,2048]{1,0:T(8,128)(2,1)S(1)}) custom-call(s32[4]{0:T(128)S(1)} %and_select_fusion.slots_ref, bf16[4,3,2,256,128]{4,3,2,1,0:T(8,128)(2,1)} %all-to-all-done.5.grad_ref, ...), custom_call_target="tpu_custom_call" | custom-call | tf_op jit(solution)/shard_map/project_in_back/pallas_call | solution.py:940
  545.5 14.8 %collective-permute-done.59.refs_6_ = bf16[128,2176]{1,0:T(8,128)(2,1)S(1)} collective-permute-done((bf16[128,2176]{1,0:T(8,128)(2,1)S(1)}, bf16[128,2176]{1,0:T(8,128)(2,1)S(1)}, u32[]{:S(2)}, u32[]{:S(2)}) %collective-permute-start.59) | collective-permute-done | bytes 557088 | tf_op jit(solution)/shard_map/ppermute | solution.py:410
  560.2 5.5 grad_blocks.5
  574.0 9.1 %collective-permute-done.62 = bf16[128,2048]{1,0:T(8,128)(2,1)S(1)} collective-permute-done((bf16[128,2048]{1,0:T(8,128)(2,1)S(1)}, bf16[128,2048]{1,0:T(8,128)(2,1)S(1)}, u32[]{:S(2)}, u32[]{:S(2)}) %collective-permute-start.62) | collective-permute-done | bytes 524320 | tf_op jit(solution)/shard_map/ppermute | solution.py:607
  (329 shorter events, 271.1 us)
Async XLA Ops:
  7.2 40.6 %all-gather.4.cloned.1.call-start = ((), (), s32[]{:S(2)}) async-start(), calls=%async_computation.10 | async-start | bytes 1310720 | tf_op jit(solution)/shard_map/all_gather | solution.py:1340
  10.2 27.1 %collective-permute-start.4 = (bf16[256,1536]{1,0:T(8,128)(2,1)S(1)}, bf16[256,1536]{1,0:T(8,128)(2,1)}, u32[]{:S(2)}, u32[]{:S(2)}) collective-permute-start(bf16[256,1536]{1,0:T(8,128)(2,1)S(1)} %constant_dynamic-update-slice_fusion.refs_0_), channel_id=1, source_target_pairs={{0,16},{16,0},{1,17},{17,1},{2,18},{18,2},{3,19},{19,3},{4,20},{20... | collective-permute-start | bytes 2359304 | tf_op jit(solution)/shard_map/ppermute | solution.py:414
  10.7 23.0 %collective-permute-start.1 = (bf16[256,1536]{1,0:T(8,128)(2,1)S(1)}, bf16[256,1536]{1,0:T(8,128)(2,1)S(1)}, u32[]{:S(2)}, u32[]{:S(2)}) collective-permute-start(bf16[256,1536]{1,0:T(8,128)(2,1)S(1)} %constant_dynamic-update-slice_fusion.refs_0_), channel_id=1, source_target_pairs={{0,8},{4,12},{8,0},{12,4},{1,9},{5,13},{9,1},{13,5},{2,10},{6,14},... | collective-permute-start | bytes 2359304 | tf_op jit(solution)/shard_map/ppermute | solution.py:410
  13.3 20.4 %collective-permute-start = (bf16[256,1536]{1,0:T(8,128)(2,1)S(1)}, bf16[256,1536]{1,0:T(8,128)(2,1)S(1)}, u32[]{:S(2)}, u32[]{:S(2)}) collective-permute-start(bf16[256,1536]{1,0:T(8,128)(2,1)S(1)} %constant_dynamic-update-slice_fusion.refs_0_), channel_id=1, source_target_pairs={{0,4},{4,0},{8,12},{12,8},{1,5},{5,1},{9,13},{13,9},{2,6},{6,2},{1... | collective-permute-start | bytes 2359304 | tf_op jit(solution)/shard_map/ppermute | solution.py:410
  22.0 205.1 %all-gather.6.cloned.1.call-start = ((), (), s32[]{:S(2)}) async-start(), calls=%async_computation.11 | async-start | bytes 28311552 | tf_op jit(solution)/shard_map/all_gather | solution.py:1344
  47.9 34.5 %collective-permute-start.13 = (bf16[512,256]{1,0:T(8,128)(2,1)S(1)}, bf16[512,256]{1,0:T(8,128)(2,1)}, u32[]{:S(2)}, u32[]{:S(2)}) collective-permute-start(bf16[512,256]{1,0:T(8,128)(2,1)S(1)} %copy-done.21), channel_id=1, source_target_pairs={{0,16},{16,0},{1,17},{17,1},{2,18},{18,2},{3,19},{19,3},{4,20},{20... | collective-permute-start | bytes 786440 | tf_op jit(solution)/shard_map/ppermute | solution.py:414
  61.2 21.2 %collective-permute-start.15 = (bf16[512,256]{1,0:T(8,128)(2,1)S(1)}, bf16[512,256]{1,0:T(8,128)(2,1)S(1)}, u32[]{:S(2)}, u32[]{:S(2)}) collective-permute-start(bf16[512,256]{1,0:T(8,128)(2,1)S(1)} %collective-permute-done.10.refs_2_), channel_id=1, source_target_pairs={{0,16},{16,0},{1,17},{17,1},{2,18},{18,2},{3,19},{19,3},{4,20},{20... | collective-permute-start | bytes 786440 | tf_op jit(solution)/shard_map/ppermute | solution.py:414
  61.2 21.1 %collective-permute-start.14 = (bf16[512,256]{1,0:T(8,128)(2,1)S(1)}, bf16[512,256]{1,0:T(8,128)(2,1)S(1)}, u32[]{:S(2)}, u32[]{:S(2)}) collective-permute-start(bf16[512,256]{1,0:T(8,128)(2,1)S(1)} %collective-permute-done.9.refs_1_), channel_id=1, source_target_pairs={{0,16},{16,0},{1,17},{17,1},{2,18},{18,2},{3,19},{19,3},{4,20},{20... | collective-permute-start | bytes 786440 | tf_op jit(solution)/shard_map/ppermute | solution.py:414
  63.6 18.7 %collective-permute-start.12 = (bf16[256,256]{1,0:T(8,128)(2,1)S(1)}, bf16[256,256]{1,0:T(8,128)(2,1)S(1)}, u32[]{:S(2)}, u32[]{:S(2)}) collective-permute-start(bf16[256,256]{1,0:T(8,128)(2,1)S(1)} %slice.51), channel_id=1, source_target_pairs={{0,8},{4,12},{8,0},{12,4},{1,9},{5,13},{9,1},{13,5},{2,10},{6,14},... | collective-permute-start | bytes 393224 | tf_op jit(solution)/shard_map/ppermute | solution.py:410
  64.6 17.8 %collective-permute-start.11 = (bf16[256,256]{1,0:T(8,128)(2,1)S(1)}, bf16[256,256]{1,0:T(8,128)(2,1)S(1)}, u32[]{:S(2)}, u32[]{:S(2)}) collective-permute-start(bf16[256,256]{1,0:T(8,128)(2,1)S(1)} %slice.50), channel_id=1, source_target_pairs={{0,4},{4,0},{8,12},{12,8},{1,5},{5,1},{9,13},{13,9},{2,6},{6,2},{1... | collective-permute-start | bytes 393224 | tf_op jit(solution)/shard_map/ppermute | solution.py:410
  83.1 31.5 %all-to-all-start.2 = ((bf16[4,3,2,256,128]{4,3,2,1,0:T(8,128)(2,1)}), bf16[4,3,2,256,128]{4,3,2,1,0:T(8,128)(2,1)S(1)}, u32[]{:S(2)}, u32[]{:S(2)}) async-start(bf16[4,3,2,256,128]{4,3,2,1,0:T(8,128)(2,1)} %prepare.1), calls=%async_computation.2 | async-start | bytes 3145728 | tf_op jit(solution)/shard_map/all_to_all | solution.py:1359
  121.2 17.9 %all-to-all-start.3 = ((bf16[4,2,256,128]{3,2,1,0:T(8,128)(2,1)}), bf16[4,2,256,128]{3,2,1,0:T(8,128)(2,1)S(1)}, u32[]{:S(2)}, u32[]{:S(2)}) async-start(bf16[4,2,256,128]{3,2,1,0:T(8,128)(2,1)} %copy-done.25), calls=%async_computation.3 | async-start | bytes 1048576 | tf_op jit(solution)/shard_map/all_to_all | solution.py:1363
  124.7 176.2 %all-gather.8.cloned.1.call-start = ((), (), s32[]{:S(2)}) async-start(), calls=%async_computation.12 | async-start | bytes 9437184 | tf_op jit(solution)/shard_map/all_gather | solution.py:1369
  190.5 395.1 %reduce-scatter.5.cloned.1.call-start = ((), (), s32[]{:S(2)}) async-start(), calls=%async_computation.14 | async-start | bytes 9437184 | tf_op jit(solution)/shard_map/reduce_scatter | solution.py:1384
  274.7 21.3 %collective-permute-start.35 = (bf16[128,2048]{1,0:T(8,128)(2,1)S(1)}, bf16[128,2048]{1,0:T(8,128)(2,1)S(1)}, u32[]{:S(2)}, u32[]{:S(2)}) collective-permute-start(bf16[128,2048]{1,0:T(8,128)(2,1)S(1)} %add_convert_fusion.4), channel_id=1, source_target_pairs={{1,0},{2,1},{3,2},{5,4},{6,5},{7,6},{9,8},{10,9},{11,10},{13,12},{... | collective-permute-start | bytes 1572872 | tf_op jit(solution)/shard_map/ppermute | solution.py:607
  276.0 22.3 %collective-permute-start.34 = (bf16[128,2048]{1,0:T(8,128)(2,1)}, bf16[128,2048]{1,0:T(8,128)(2,1)S(1)}, u32[]{:S(2)}, u32[]{:S(2)}) collective-permute-start(bf16[128,2048]{1,0:T(8,128)(2,1)} %add_convert_fusion.5), channel_id=1, source_target_pairs={{0,1},{1,2},{2,3},{4,5},{5,6},{6,7},{8,9},{9,10},{10,11},{12,13},{... | collective-permute-start | bytes 1572872 | tf_op jit(solution)/shard_map/ppermute | solution.py:606
  300.9 14.5 %collective-permute-start.39 = (bf16[128,2048]{1,0:T(8,128)(2,1)S(1)}, bf16[128,2048]{1,0:T(8,128)(2,1)S(1)}, u32[]{:S(2)}, u32[]{:S(2)}) collective-permute-start(bf16[128,2048]{1,0:T(8,128)(2,1)S(1)} %get-tuple-element.194.refs_0_), channel_id=1, source_target_pairs={{1,0},{2,1},{3,2},{5,4},{6,5},{7,6},{9,8},{10,9},{11,10},{13,12},{... | collective-permute-start | bytes 1572872 | tf_op jit(solution)/shard_map/ppermute | solution.py:593
  302.2 14.5 %collective-permute-start.36 = (bf16[128,2048]{1,0:T(8,128)(2,1)S(1)}, bf16[128,2048]{1,0:T(8,128)(2,1)S(1)}, u32[]{:S(2)}, u32[]{:S(2)}) collective-permute-start(bf16[128,2048]{1,0:T(8,128)(2,1)S(1)} %get-tuple-element.194.refs_0_), channel_id=1, source_target_pairs={{0,1},{1,2},{2,3},{4,5},{5,6},{6,7},{8,9},{9,10},{10,11},{12,13},{... | collective-permute-start | bytes 1572872 | tf_op jit(solution)/shard_map/ppermute | solution.py:592
  347.6 238.0 %reduce-scatter.3.cloned.1.call-start = ((), (), s32[]{:S(2)}) async-start(), calls=%async_computation.13 | async-start | bytes 18874368 | tf_op jit(solution)/shard_map/reduce_scatter | solution.py:1384
  383.4 16.2 %collective-permute-start.44 = (bf16[128,2048]{1,0:T(8,128)(2,1)S(1)}, bf16[128,2048]{1,0:T(8,128)(2,1)}, u32[]{:S(2)}, u32[]{:S(2)}) collective-permute-start(bf16[128,2048]{1,0:T(8,128)(2,1)S(1)} %get-tuple-element.264), channel_id=1, source_target_pairs={{0,1},{1,2},{4,5},{5,6},{8,9},{9,10},{12,13},{13,14},{16,17},{17,1... | collective-permute-start | bytes 1572872 | tf_op jit(solution)/shard_map/ppermute | solution.py:606
  423.3 20.4 %all-to-all-start.4 = ((bf16[16,2,64,128]{3,2,1,0:T(8,128)(2,1)}), bf16[16,2,64,128]{3,2,1,0:T(8,128)(2,1)S(1)}, u32[]{:S(2)}, u32[]{:S(2)}) async-start(bf16[16,2,64,128]{3,2,1,0:T(8,128)(2,1)} %bitcast.11), calls=%async_computation.4 | async-start | bytes 1048576 | tf_op jit(solution)/shard_map/all_to_all | solution.py:1395
  431.6 27.7 %collective-permute-start.51 = (bf16[128,2048]{1,0:T(8,128)(2,1)}, bf16[128,2048]{1,0:T(8,128)(2,1)}, u32[]{:S(2)}, u32[]{:S(2)}) collective-permute-start(bf16[128,2048]{1,0:T(8,128)(2,1)} %get-tuple-element.213.grad_ref.refs_0_), channel_id=1, source_target_pairs={{1,0},{2,1},{3,2},{5,4},{6,5},{7,6},{9,8},{10,9},{11,10},{13,12},{... | collective-permute-start | bytes 1572872 | tf_op jit(solution)/shard_map/ppermute | solution.py:593
  432.9 28.0 %collective-permute-start.48 = (bf16[128,2048]{1,0:T(8,128)(2,1)}, bf16[128,2048]{1,0:T(8,128)(2,1)}, u32[]{:S(2)}, u32[]{:S(2)}) collective-permute-start(bf16[128,2048]{1,0:T(8,128)(2,1)} %get-tuple-element.213.grad_ref.refs_0_), channel_id=1, source_target_pairs={{0,1},{1,2},{2,3},{4,5},{5,6},{6,7},{8,9},{9,10},{10,11},{12,13},{... | collective-permute-start | bytes 1572872 | tf_op jit(solution)/shard_map/ppermute | solution.py:592
  454.9 30.0 %all-to-all-start.5 = ((bf16[4,3,2,256,128]{4,3,2,1,0:T(8,128)(2,1)}), bf16[4,3,2,256,128]{4,3,2,1,0:T(8,128)(2,1)}, u32[]{:S(2)}, u32[]{:S(2)}) async-start(bf16[4,3,2,256,128]{4,3,2,1,0:T(8,128)(2,1)} %attend_back.1), calls=%async_computation.5 | async-start | bytes 3145728 | tf_op jit(solution)/shard_map/all_to_all | solution.py:1399
  533.2 27.0 %collective-permute-start.59 = (bf16[128,2176]{1,0:T(8,128)(2,1)S(1)}, bf16[128,2176]{1,0:T(8,128)(2,1)S(1)}, u32[]{:S(2)}, u32[]{:S(2)}) collective-permute-start(bf16[128,2176]{1,0:T(8,128)(2,1)S(1)} %get-tuple-element.231), channel_id=1, source_target_pairs={{0,4},{4,0},{8,12},{12,8},{1,5},{5,1},{9,13},{13,9},{2,6},{6,2},{1... | collective-permute-start | bytes 1671176 | tf_op jit(solution)/shard_map/ppermute | solution.py:410
  535.2 25.0 %collective-permute-start.60 = (bf16[128,2176]{1,0:T(8,128)(2,1)S(1)}, bf16[128,2176]{1,0:T(8,128)(2,1)S(1)}, u32[]{:S(2)}, u32[]{:S(2)}) collective-permute-start(bf16[128,2176]{1,0:T(8,128)(2,1)S(1)} %get-tuple-element.232), channel_id=1, source_target_pairs={{0,8},{4,12},{8,0},{12,4},{1,9},{5,13},{9,1},{13,5},{2,10},{6,14},... | collective-permute-start | bytes 1671176 | tf_op jit(solution)/shard_map/ppermute | solution.py:410
  539.7 26.0 %collective-permute-start.58 = (bf16[128,2048]{1,0:T(8,128)(2,1)S(1)}, bf16[128,2048]{1,0:T(8,128)(2,1)S(1)}, u32[]{:S(2)}, u32[]{:S(2)}) collective-permute-start(bf16[128,2048]{1,0:T(8,128)(2,1)S(1)} %get-tuple-element.261), channel_id=1, source_target_pairs={{2,1},{3,2},{6,5},{7,6},{10,9},{11,10},{14,13},{15,14},{18,17},{19... | collective-permute-start | bytes 1572872 | tf_op jit(solution)/shard_map/ppermute | solution.py:607
  540.4 25.3 %collective-permute-start.57 = (bf16[128,2048]{1,0:T(8,128)(2,1)S(1)}, bf16[128,2048]{1,0:T(8,128)(2,1)S(1)}, u32[]{:S(2)}, u32[]{:S(2)}) collective-permute-start(bf16[128,2048]{1,0:T(8,128)(2,1)S(1)} %get-tuple-element.262), channel_id=1, source_target_pairs={{0,1},{1,2},{4,5},{5,6},{8,9},{9,10},{12,13},{13,14},{16,17},{17,1... | collective-permute-start | bytes 1572872 | tf_op jit(solution)/shard_map/ppermute | solution.py:606
  565.7 26.6 %collective-permute-start.63 = (bf16[256,2176]{1,0:T(8,128)(2,1)}, bf16[256,2176]{1,0:T(8,128)(2,1)S(1)}, u32[]{:S(2)}, u32[]{:S(2)}) collective-permute-start(bf16[256,2176]{1,0:T(8,128)(2,1)} %get-tuple-element.241), channel_id=1, source_target_pairs={{0,4},{4,0},{8,12},{12,8},{1,5},{5,1},{9,13},{13,9},{2,6},{6,2},{1... | collective-permute-start | bytes 3342344 | tf_op jit(solution)/shard_map/ppermute | solution.py:410
  567.3 26.3 %collective-permute-start.64 = (bf16[256,2176]{1,0:T(8,128)(2,1)}, bf16[256,2176]{1,0:T(8,128)(2,1)S(1)}, u32[]{:S(2)}, u32[]{:S(2)}) collective-permute-start(bf16[256,2176]{1,0:T(8,128)(2,1)} %get-tuple-element.242), channel_id=1, source_target_pairs={{0,8},{4,12},{8,0},{12,4},{1,9},{5,13},{9,1},{13,5},{2,10},{6,14},... | collective-permute-start | bytes 3342344 | tf_op jit(solution)/shard_map/ppermute | solution.py:410
  568.1 15.0 %collective-permute-start.62 = (bf16[128,2048]{1,0:T(8,128)(2,1)S(1)}, bf16[128,2048]{1,0:T(8,128)(2,1)S(1)}, u32[]{:S(2)}, u32[]{:S(2)}) collective-permute-start(bf16[128,2048]{1,0:T(8,128)(2,1)S(1)} %add_convert_fusion), channel_id=1, source_target_pairs={{1,0},{2,1},{3,2},{5,4},{6,5},{7,6},{9,8},{10,9},{11,10},{13,12},{... | collective-permute-start | bytes 1572872 | tf_op jit(solution)/shard_map/ppermute | solution.py:607
  569.4 14.9 %collective-permute-start.61 = (bf16[128,2048]{1,0:T(8,128)(2,1)S(1)}, bf16[128,2048]{1,0:T(8,128)(2,1)S(1)}, u32[]{:S(2)}, u32[]{:S(2)}) collective-permute-start(bf16[128,2048]{1,0:T(8,128)(2,1)S(1)} %add_convert_fusion.1), channel_id=1, source_target_pairs={{0,1},{1,2},{2,3},{4,5},{5,6},{6,7},{8,9},{9,10},{10,11},{12,13},{... | collective-permute-start | bytes 1572872 | tf_op jit(solution)/shard_map/ppermute | solution.py:606
  (99 other events, 932.9 us)
Sparse Core Ops, SparseCore 0:
  16.7 27.3 all-gather.3
  48.0 150.8 all-gather.5
  200.7 54.3 all-gather.7
  347.7 78.4 reduce-scatter.4
  430.0 131.5 reduce-scatter.2

commit v5 on v4

--- a/solution.py
+++ b/solution.py
@@ -573,6 +573,11 @@
         ),
         out_shape=out_shape,
         compiler_params=vmem(24),
+        cost_estimate=pl.CostEstimate(
+            flops=2 * rows * block * count * width,
+            bytes_accessed=4 * block * count * width + 2 * rows * (width + d_model),
+            transcendentals=0,
+        ),
         name="grad_blocks",
     )(order, *lefts, *rights, extra, *more)
 
@@ -1171,6 +1176,11 @@
         + [jax.ShapeDtypeStruct((own, width), LOW)] * parts,
         scratch_shapes=[pltpu.VMEM((rows, width), jnp.float32)],
         compiler_params=vmem(50),
+        cost_estimate=pl.CostEstimate(
+            flops=6 * rows * width * hidden_units,
+            bytes_accessed=6 * width * hidden_units + 8 * rows * hidden_units,
+            transcendentals=0,
+        ),
         name="feed_forward",
     )(*pieces, weights, weights, weights)
 
@@ -1221,6 +1231,11 @@
         + [jax.ShapeDtypeStruct((own, width), LOW)] * parts,
         scratch_shapes=[pltpu.VMEM((rows, width), jnp.float32)],
         compiler_params=vmem(50),
+        cost_estimate=pl.CostEstimate(
+            flops=6 * rows * width * hidden_units,
+            bytes_accessed=6 * width * hidden_units + 8 * rows * hidden_units,
+            transcendentals=0,
+        ),
         name="feed_forward_back",
     )(rows_low, gate, up, weights, weights, weights)
 
@@ -1255,6 +1270,11 @@
             jax.ShapeDtypeStruct((width, columns), LOW),
         ],
         compiler_params=vmem(50),
+        cost_estimate=pl.CostEstimate(
+            flops=2 * rows * width * columns,
+            bytes_accessed=2 * (width * columns + rows * (width + columns)),
+            transcendentals=0,
+        ),
         name="down_grad",
     )(*pieces, mixed)
 
@@ -1280,6 +1300,11 @@
         out_shape=jax.ShapeDtypeStruct((width, all_columns), LOW),
         input_output_aliases={2: 0} if given else {},
         compiler_params=vmem(50),
+        cost_estimate=pl.CostEstimate(
+            flops=2 * rows * width * columns,
+            bytes_accessed=2 * (width * columns + rows * (width + columns)),
+            transcendentals=0,
+        ),
         name="weight_grad",
     )(left, right, *given)
 

time: 614 us -> 614 us (level)
  no operation moved by 1% of the time
where the time goes in v5:
time: 614 us; the launch traced here: 603 us
  waiting for transfers between devices  225 us (37%)
  starting transfers between devices  158 us (26%)
  Pallas kernels  143 us (23%)
  local copies, waits for them, and re-layouts  43.9 us (7%)
  other arithmetic  16.7 us (3%)
  between operations  15.5 us (3%)
    ppermute x9, waiting for transfers between devices, gather_line(): down = lax.ppermute(down, 'tp', [(i, i - 1) for i in range(1, 5 - t)])  70.4 us
    ppermute x12, starting transfers between devices, scatter_line(): up = lax.ppermute(up, 'tp', [(i, i + 1) for i in range(t)])  56.9 us
    ppermute x12, waiting for transfers between devices, scatter_line(): up = lax.ppermute(up, 'tp', [(i, i + 1) for i in range(t)])  45.8 us
    unnamed x113, local copies, waits for them, and re-layouts  33.4 us
    ppermute x12, waiting for transfers between devices, to_neighbour(): return lax.ppermute(values, 'seq', [(i, i ^ flip) for i in range(4)])  26.4 us
    ppermute x12, waiting for transfers between devices, scatter_line(): down = lax.ppermute(down, 'tp', [(i, i - 1) for i in range(4 - t, 4)])  25.8 us
    all_to_all x1, waiting for transfers between devices, on_plane(): parts = lax.all_to_all(parts, 'seq', 0, 0, tiled=True)  25 us
    pallas_call x1, Pallas kernels, feed_forward_back(): pl.pallas_call(body, grid=(tiles,), in_specs=[pl.BlockSpec((rows, width),...  23.3 us
  transfers between devices with their start and end apart: 78, of which 36 were waited for; matrix products, arithmetic and copies ran while one was open for 5% of the time, Pallas kernels for 22%

profile of v5, /device:TPU:0, one launch (start us, length us, event | category | flops | bytes accessed | tf_op | source)
XLA Modules:
  0.0 602.8 jit_solution(6053985989628317051)
XLA Ops:
  26.8 6.2 %all-to-all-done = bf16[8,2,320]{2,1,0:T(2,128)(2,1)S(1)} async-done(((bf16[8,2,320]{2,1,0:T(2,128)(2,1)}), bf16[8,2,320]{2,1,0:T(2,128)(2,1)S(1)}, u32[]{:S(2)}, u32[]{:S(2)}) %all-to-all-start) | async-done | bytes 10272 | tf_op jit(solution)/shard_map/all_to_all | solution.py:1340
  37.3 8.3 %collective-permute-done.2.refs_3_ = bf16[128,1536]{1,0:T(8,128)(2,1)S(1)} collective-permute-done((bf16[128,1536]{1,0:T(8,128)(2,1)S(1)}, bf16[128,1536]{1,0:T(8,128)(2,1)S(1)}, u32[]{:S(2)}, u32[]{:S(2)}) %collective-permute-start.2) | collective-permute-done | bytes 393248 | tf_op jit(solution)/shard_map/ppermute | solution.py:410
  51.8 9.3 %project_in.1 = (f32[512,1536]{1,0:T(8,128)}, bf16[2048,1536]{1,0:T(8,128)(2,1)}) custom-call(s32[8]{0:T(128)S(1)} %iota_xor_fusion.order_ref, bf16[512,2048]{1,0:T(8,128)(2,1)} %bitcast.34, bf16[256,1536]{1,0:T(8,128)(2,1)S(1)} %constant_dynamic-update-slice_fusion.refs_0_, bf16[256,1536]{1,0:T(8,128)(2,1)S(1)} %collective-permute-done.refs_1_, ...), custom_call_target="tpu_custom_call" | custom-call | tf_op jit(solution)/shard_map/project_in/pallas_call | solution.py:474
  89.5 25.0 %all-to-all-done.2.parts_ref = bf16[4,3,2,256,128]{4,3,2,1,0:T(8,128)(2,1)S(1)} async-done(((bf16[4,3,2,256,128]{4,3,2,1,0:T(8,128)(2,1)}), bf16[4,3,2,256,128]{4,3,2,1,0:T(8,128)(2,1)S(1)}, u32[]{:S(2)}, u32[]{:S(2)}) %all-to-all-start.2) | async-done | bytes 1572896 | tf_op jit(solution)/shard_map/all_to_all | solution.py:1384
  131.0 8.1 %all-to-all-done.3.context_ref = bf16[4,2,256,128]{3,2,1,0:T(8,128)(2,1)S(1)} async-done(((bf16[4,2,256,128]{3,2,1,0:T(8,128)(2,1)}), bf16[4,2,256,128]{3,2,1,0:T(8,128)(2,1)S(1)}, u32[]{:S(2)}, u32[]{:S(2)}) %all-to-all-start.3) | async-done | bytes 524320 | tf_op jit(solution)/shard_map/all_to_all | solution.py:1388
  146.7 9.8 %collective-permute-done.18 = bf16[128,2048]{1,0:T(8,128)(2,1)S(1)} collective-permute-done((bf16[128,2048]{1,0:T(8,128)(2,1)S(1)}, bf16[128,2048]{1,0:T(8,128)(2,1)S(1)}, u32[]{:S(2)}, u32[]{:S(2)}) %collective-permute-start.18) | collective-permute-done | bytes 524320 | tf_op jit(solution)/shard_map/ppermute | solution.py:611
  162.6 9.0 %collective-permute-done.20 = bf16[128,2048]{1,0:T(8,128)(2,1)S(1)} collective-permute-done((bf16[128,2048]{1,0:T(8,128)(2,1)S(1)}, bf16[128,2048]{1,0:T(8,128)(2,1)S(1)}, u32[]{:S(2)}, u32[]{:S(2)}) %collective-permute-start.20) | collective-permute-done | bytes 524320 | tf_op jit(solution)/shard_map/ppermute | solution.py:611
  196.9 6.2 %collective-permute-done.27.refs_4_ = bf16[128,2048]{1,0:T(8,128)(2,1)S(1)} collective-permute-done((bf16[128,2048]{1,0:T(8,128)(2,1)S(1)}, bf16[128,2048]{1,0:T(8,128)(2,1)S(1)}, u32[]{:S(2)}, u32[]{:S(2)}) %collective-permute-start.27) | collective-permute-done | bytes 524320 | tf_op jit(solution)/shard_map/ppermute | solution.py:598
  205.1 10.2 %collective-permute-done.28.refs_5_ = bf16[128,2048]{1,0:T(8,128)(2,1)S(1)} collective-permute-done((bf16[128,2048]{1,0:T(8,128)(2,1)S(1)}, bf16[128,2048]{1,0:T(8,128)(2,1)S(1)}, u32[]{:S(2)}, u32[]{:S(2)}) %collective-permute-start.28) | collective-permute-done | bytes 524320 | tf_op jit(solution)/shard_map/ppermute | solution.py:598
  218.2 8.1 %collective-permute-done.29.refs_6_ = bf16[128,2048]{1,0:T(8,128)(2,1)S(1)} collective-permute-done((bf16[128,2048]{1,0:T(8,128)(2,1)S(1)}, bf16[128,2048]{1,0:T(8,128)(2,1)S(1)}, u32[]{:S(2)}, u32[]{:S(2)}) %collective-permute-start.29) | collective-permute-done | bytes 524320 | tf_op jit(solution)/shard_map/ppermute | solution.py:598
  227.1 22.9 %feed_forward.1 = (bf16[512,2048]{1,0:T(8,128)(2,1)}, bf16[512,2048]{1,0:T(8,128)(2,1)}, bf16[512,2048]{1,0:T(8,128)(2,1)}, bf16[512,2048]{1,0:T(8,128)(2,1)}, b...) custom-call(bf16[128,2048]{1,0:T(8,128)(2,1)S(1)} %get-tuple-element, ...), custom_call_target="tpu_custom_call" | custom-call | flops 12884901888 | bytes 33554432 | tf_op jit(solution)/shard_map/feed_forward/pallas_call | solution.py:1169
  252.0 8.1 %collective-permute-done.30 = bf16[128,2048]{1,0:T(8,128)(2,1)S(1)} collective-permute-done((bf16[128,2048]{1,0:T(8,128)(2,1)S(1)}, bf16[128,2048]{1,0:T(8,128)(2,1)S(1)}, u32[]{:S(2)}, u32[]{:S(2)}) %collective-permute-start.30) | collective-permute-done | bytes 524320 | tf_op jit(solution)/shard_map/ppermute | solution.py:611
  266.3 7.3 %collective-permute-done.32 = bf16[128,2048]{1,0:T(8,128)(2,1)S(1)} collective-permute-done((bf16[128,2048]{1,0:T(8,128)(2,1)S(1)}, bf16[128,2048]{1,0:T(8,128)(2,1)S(1)}, u32[]{:S(2)}, u32[]{:S(2)}) %collective-permute-start.32) | collective-permute-done | bytes 524320 | tf_op jit(solution)/shard_map/ppermute | solution.py:611
  276.0 12.3 %collective-permute-start.34 = (bf16[128,2048]{1,0:T(8,128)(2,1)}, bf16[128,2048]{1,0:T(8,128)(2,1)S(1)}, u32[]{:S(2)}, u32[]{:S(2)}) collective-permute-start(bf16[128,2048]{1,0:T(8,128)(2,1)} %add_convert_fusion.5), channel_id=1, source_target_pairs={{0,1},{1,2},{2,3},{4,5},{5,6},{6,7},{8,9},{9,10},{10,11},{12,13},{... | collective-permute-start | bytes 1572872 | tf_op jit(solution)/shard_map/ppermute | solution.py:611
  289.9 6.1 %collective-permute-done.35.down_ref = bf16[128,2048]{1,0:T(8,128)(2,1)S(1)} collective-permute-done((bf16[128,2048]{1,0:T(8,128)(2,1)S(1)}, bf16[128,2048]{1,0:T(8,128)(2,1)S(1)}, u32[]{:S(2)}, u32[]{:S(2)}) %collective-permute-start.35) | collective-permute-done | bytes 524320 | tf_op jit(solution)/shard_map/ppermute | solution.py:612
  307.6 7.7 %collective-permute-done.39.refs_4_ = bf16[128,2048]{1,0:T(8,128)(2,1)S(1)} collective-permute-done((bf16[128,2048]{1,0:T(8,128)(2,1)S(1)}, bf16[128,2048]{1,0:T(8,128)(2,1)S(1)}, u32[]{:S(2)}, u32[]{:S(2)}) %collective-permute-start.39) | collective-permute-done | bytes 524320 | tf_op jit(solution)/shard_map/ppermute | solution.py:598
  317.4 10.7 %collective-permute-done.40.refs_5_ = bf16[128,2048]{1,0:T(8,128)(2,1)S(1)} collective-permute-done((bf16[128,2048]{1,0:T(8,128)(2,1)S(1)}, bf16[128,2048]{1,0:T(8,128)(2,1)S(1)}, u32[]{:S(2)}, u32[]{:S(2)}) %collective-permute-start.40) | collective-permute-done | bytes 524320 | tf_op jit(solution)/shard_map/ppermute | solution.py:598
  330.1 9.1 %collective-permute-done.41.refs_6_ = bf16[128,2048]{1,0:T(8,128)(2,1)S(1)} collective-permute-done((bf16[128,2048]{1,0:T(8,128)(2,1)S(1)}, bf16[128,2048]{1,0:T(8,128)(2,1)S(1)}, u32[]{:S(2)}, u32[]{:S(2)}) %collective-permute-start.41) | collective-permute-done | bytes 524320 | tf_op jit(solution)/shard_map/ppermute | solution.py:598
  339.1 8.4 %down_grad.1 = (bf16[512,2048]{1,0:T(8,128)(2,1)}, bf16[2048,2048]{1,0:T(8,128)(2,1)}) custom-call(bf16[128,2048]{1,0:T(8,128)(2,1)S(1)} %get-tuple-element.194.refs_0_, bf16[128,2048]{1,0:T(8,128)(2,1)S(1)} %collective-permute-done.36.refs_1_, bf16[128,2048]{1,0:T(8,128)(2,1)S(1)} %collective-permute-done.37.refs_2_, ...), custom_call_target="tpu_custom_call" | custom-call | flops 4294967296 | bytes 12582912 | tf_op jit(solution)/shard_map/down_grad/pallas_call | solution.py:1259
  347.6 23.3 %feed_forward_back.1 = (bf16[512,2048]{1,0:T(8,128)(2,1)}, bf16[512,2048]{1,0:T(8,128)(2,1)}, bf16[128,2048]{1,0:T(8,128)(2,1)S(1)}, bf16[128,2048]{1,0:T(8,128)...) custom-call(bf16[512,2048]{1,0:T(8,128)(2,1)} %get-tuple-element.196.rows_ref, ...), custom_call_target="tpu_custom_call" | custom-call | flops 12884901888 | bytes 33554432 | tf_op jit(solution)/shard_map/feed_forward_back/pallas_call | solution.py:1223
  373.4 8.2 %weight_grad.2.refs_0_ = bf16[2048,4096]{1,0:T(8,128)(2,1)} custom-call(bf16[512,2048]{1,0:T(8,128)(2,1)S(1)} %copy-done.6, bf16[512,2048]{1,0:T(8,128)(2,1)} %get-tuple-element.204.right_ref), custom_call_target="tpu_custom_call" | custom-call | flops 4294967296 | bytes 12582912 | tf_op jit(solution)/shard_map/weight_grad/pallas_call | solution.py:1291
  388.7 8.4 %weight_grad.3 = bf16[2048,4096]{1,0:T(8,128)(2,1)} custom-call(bf16[512,2048]{1,0:T(8,128)(2,1)S(1)} %copy-done.6, bf16[512,2048]{1,0:T(8,128)(2,1)} %get-tuple-element.207.right_ref, bf16[2048,4096]{1,0:T(8,128)(2,1)} %weight_grad.2.refs_0_), custom_call_target="tpu_custom_call", output_to_operand_aliasing={{}: (2, {})} | custom-call | flops 4294967296 | bytes 12582912 | tf_op jit(solution)/shard_map/weight_grad/pallas_call | solution.py:1291
  417.1 6.2 %project_out_back.1 = bf16[4,4,2,64,128]{4,3,2,1,0:T(8,128)(2,1)} custom-call(bf16[128,2048]{1,0:T(8,128)(2,1)} %get-tuple-element.213.grad_ref.refs_0_, bf16[2048,2048]{1,0:T(8,128)(2,1)} %all-gather.8.cloned.1.call-done.weight_ref), custom_call_target="tpu_custom_call" | custom-call | tf_op jit(solution)/shard_map/project_out_back/pallas_call | solution.py:825
  423.3 8.3 %all-to-all-start.4 = ((bf16[16,2,64,128]{3,2,1,0:T(8,128)(2,1)}), bf16[16,2,64,128]{3,2,1,0:T(8,128)(2,1)S(1)}, u32[]{:S(2)}, u32[]{:S(2)}) async-start(bf16[16,2,64,128]{3,2,1,0:T(8,128)(2,1)} %bitcast.11), calls=%async_computation.4 | async-start | bytes 1048576 | tf_op jit(solution)/shard_map/all_to_all | solution.py:1420
  447.0 7.9 %attend_back.1 = bf16[4,3,2,256,128]{4,3,2,1,0:T(8,128)(2,1)} custom-call(bf16[4,3,2,256,128]{4,3,2,1,0:T(8,128)(2,1)} %copy-done.5, bf16[4,4,2,64,128]{4,3,2,1,0:T(8,128)(2,1)S(1)} %bitcast.41, f32[4,2,256,1]{3,2,1,0:T(8,128)S(1)} %copy-done.23), custom_call_target="tpu_custom_call" | custom-call | tf_op jit(solution)/shard_map/attend_back/pallas_call | solution.py:754
  461.6 9.3 %collective-permute-done.52.refs_5_ = bf16[128,2048]{1,0:T(8,128)(2,1)S(1)} collective-permute-done((bf16[128,2048]{1,0:T(8,128)(2,1)}, bf16[128,2048]{1,0:T(8,128)(2,1)S(1)}, u32[]{:S(2)}, u32[]{:S(2)}) %collective-permute-start.52) | collective-permute-done | bytes 524320 | tf_op jit(solution)/shard_map/ppermute | solution.py:598
  472.9 9.2 %collective-permute-done.53.refs_6_ = bf16[128,2048]{1,0:T(8,128)(2,1)S(1)} collective-permute-done((bf16[128,2048]{1,0:T(8,128)(2,1)S(1)}, bf16[128,2048]{1,0:T(8,128)(2,1)S(1)}, u32[]{:S(2)}, u32[]{:S(2)}) %collective-permute-start.53) | collective-permute-done | bytes 524320 | tf_op jit(solution)/shard_map/ppermute | solution.py:598
  493.5 6.4 %all-to-all-start.7 = ((f32[4,8,128]{2,1,0:T(8,128)}), f32[4,8,128]{2,1,0:T(8,128)S(1)}, u32[]{:S(2)}, u32[]{:S(2)}) async-start(f32[4,8,128]{2,1,0:T(8,128)} %broadcast_in_dim.28), calls=%async_computation.7 | async-start | bytes 32768 | tf_op jit(solution)/shard_map/all_to_all | solution.py:622
  513.3 7.1 %project_in_back.1 = (bf16[512,1536]{1,0:T(8,128)(2,1)S(1)}, bf16[128,2048]{1,0:T(8,128)(2,1)S(1)}, bf16[128,2048]{1,0:T(8,128)(2,1)S(1)}, bf16[128,2048]{1,0:T(8,128)(2,1)S(1)}, bf16[128,2048]{1,0:T(8,128)(2,1)S(1)}) custom-call(s32[4]{0:T(128)S(1)} %and_select_fusion.slots_ref, bf16[4,3,2,256,128]{4,3,2,1,0:T(8,128)(2,1)} %all-to-all-done.5.grad_ref, ...), custom_call_target="tpu_custom_call" | custom-call | tf_op jit(solution)/shard_map/project_in_back/pallas_call | solution.py:945
  545.5 14.8 %collective-permute-done.59.refs_6_ = bf16[128,2176]{1,0:T(8,128)(2,1)S(1)} collective-permute-done((bf16[128,2176]{1,0:T(8,128)(2,1)S(1)}, bf16[128,2176]{1,0:T(8,128)(2,1)S(1)}, u32[]{:S(2)}, u32[]{:S(2)}) %collective-permute-start.59) | collective-permute-done | bytes 557088 | tf_op jit(solution)/shard_map/ppermute | solution.py:410
  560.2 5.5 grad_blocks.5
  574.0 9.1 %collective-permute-done.62 = bf16[128,2048]{1,0:T(8,128)(2,1)S(1)} collective-permute-done((bf16[128,2048]{1,0:T(8,128)(2,1)S(1)}, bf16[128,2048]{1,0:T(8,128)(2,1)S(1)}, u32[]{:S(2)}, u32[]{:S(2)}) %collective-permute-start.62) | collective-permute-done | bytes 524320 | tf_op jit(solution)/shard_map/ppermute | solution.py:612
  (329 shorter events, 271.1 us)
Async XLA Ops:
  7.2 40.6 %all-gather.4.cloned.1.call-start = ((), (), s32[]{:S(2)}) async-start(), calls=%async_computation.10 | async-start | bytes 1310720 | tf_op jit(solution)/shard_map/all_gather | solution.py:1365
  10.2 27.1 %collective-permute-start.4 = (bf16[256,1536]{1,0:T(8,128)(2,1)S(1)}, bf16[256,1536]{1,0:T(8,128)(2,1)}, u32[]{:S(2)}, u32[]{:S(2)}) collective-permute-start(bf16[256,1536]{1,0:T(8,128)(2,1)S(1)} %constant_dynamic-update-slice_fusion.refs_0_), channel_id=1, source_target_pairs={{0,16},{16,0},{1,17},{17,1},{2,18},{18,2},{3,19},{19,3},{4,20},{20... | collective-permute-start | bytes 2359304 | tf_op jit(solution)/shard_map/ppermute | solution.py:414
  10.7 23.0 %collective-permute-start.1 = (bf16[256,1536]{1,0:T(8,128)(2,1)S(1)}, bf16[256,1536]{1,0:T(8,128)(2,1)S(1)}, u32[]{:S(2)}, u32[]{:S(2)}) collective-permute-start(bf16[256,1536]{1,0:T(8,128)(2,1)S(1)} %constant_dynamic-update-slice_fusion.refs_0_), channel_id=1, source_target_pairs={{0,8},{4,12},{8,0},{12,4},{1,9},{5,13},{9,1},{13,5},{2,10},{6,14},... | collective-permute-start | bytes 2359304 | tf_op jit(solution)/shard_map/ppermute | solution.py:410
  13.3 20.4 %collective-permute-start = (bf16[256,1536]{1,0:T(8,128)(2,1)S(1)}, bf16[256,1536]{1,0:T(8,128)(2,1)S(1)}, u32[]{:S(2)}, u32[]{:S(2)}) collective-permute-start(bf16[256,1536]{1,0:T(8,128)(2,1)S(1)} %constant_dynamic-update-slice_fusion.refs_0_), channel_id=1, source_target_pairs={{0,4},{4,0},{8,12},{12,8},{1,5},{5,1},{9,13},{13,9},{2,6},{6,2},{1... | collective-permute-start | bytes 2359304 | tf_op jit(solution)/shard_map/ppermute | solution.py:410
  22.0 205.1 %all-gather.6.cloned.1.call-start = ((), (), s32[]{:S(2)}) async-start(), calls=%async_computation.11 | async-start | bytes 28311552 | tf_op jit(solution)/shard_map/all_gather | solution.py:1369
  47.9 34.5 %collective-permute-start.13 = (bf16[512,256]{1,0:T(8,128)(2,1)S(1)}, bf16[512,256]{1,0:T(8,128)(2,1)}, u32[]{:S(2)}, u32[]{:S(2)}) collective-permute-start(bf16[512,256]{1,0:T(8,128)(2,1)S(1)} %copy-done.21), channel_id=1, source_target_pairs={{0,16},{16,0},{1,17},{17,1},{2,18},{18,2},{3,19},{19,3},{4,20},{20... | collective-permute-start | bytes 786440 | tf_op jit(solution)/shard_map/ppermute | solution.py:414
  61.2 21.2 %collective-permute-start.15 = (bf16[512,256]{1,0:T(8,128)(2,1)S(1)}, bf16[512,256]{1,0:T(8,128)(2,1)S(1)}, u32[]{:S(2)}, u32[]{:S(2)}) collective-permute-start(bf16[512,256]{1,0:T(8,128)(2,1)S(1)} %collective-permute-done.10.refs_2_), channel_id=1, source_target_pairs={{0,16},{16,0},{1,17},{17,1},{2,18},{18,2},{3,19},{19,3},{4,20},{20... | collective-permute-start | bytes 786440 | tf_op jit(solution)/shard_map/ppermute | solution.py:414
  61.2 21.1 %collective-permute-start.14 = (bf16[512,256]{1,0:T(8,128)(2,1)S(1)}, bf16[512,256]{1,0:T(8,128)(2,1)S(1)}, u32[]{:S(2)}, u32[]{:S(2)}) collective-permute-start(bf16[512,256]{1,0:T(8,128)(2,1)S(1)} %collective-permute-done.9.refs_1_), channel_id=1, source_target_pairs={{0,16},{16,0},{1,17},{17,1},{2,18},{18,2},{3,19},{19,3},{4,20},{20... | collective-permute-start | bytes 786440 | tf_op jit(solution)/shard_map/ppermute | solution.py:414
  63.6 18.7 %collective-permute-start.12 = (bf16[256,256]{1,0:T(8,128)(2,1)S(1)}, bf16[256,256]{1,0:T(8,128)(2,1)S(1)}, u32[]{:S(2)}, u32[]{:S(2)}) collective-permute-start(bf16[256,256]{1,0:T(8,128)(2,1)S(1)} %slice.51), channel_id=1, source_target_pairs={{0,8},{4,12},{8,0},{12,4},{1,9},{5,13},{9,1},{13,5},{2,10},{6,14},... | collective-permute-start | bytes 393224 | tf_op jit(solution)/shard_map/ppermute | solution.py:410
  64.6 17.8 %collective-permute-start.11 = (bf16[256,256]{1,0:T(8,128)(2,1)S(1)}, bf16[256,256]{1,0:T(8,128)(2,1)S(1)}, u32[]{:S(2)}, u32[]{:S(2)}) collective-permute-start(bf16[256,256]{1,0:T(8,128)(2,1)S(1)} %slice.50), channel_id=1, source_target_pairs={{0,4},{4,0},{8,12},{12,8},{1,5},{5,1},{9,13},{13,9},{2,6},{6,2},{1... | collective-permute-start | bytes 393224 | tf_op jit(solution)/shard_map/ppermute | solution.py:410
  83.1 31.5 %all-to-all-start.2 = ((bf16[4,3,2,256,128]{4,3,2,1,0:T(8,128)(2,1)}), bf16[4,3,2,256,128]{4,3,2,1,0:T(8,128)(2,1)S(1)}, u32[]{:S(2)}, u32[]{:S(2)}) async-start(bf16[4,3,2,256,128]{4,3,2,1,0:T(8,128)(2,1)} %prepare.1), calls=%async_computation.2 | async-start | bytes 3145728 | tf_op jit(solution)/shard_map/all_to_all | solution.py:1384
  121.2 17.9 %all-to-all-start.3 = ((bf16[4,2,256,128]{3,2,1,0:T(8,128)(2,1)}), bf16[4,2,256,128]{3,2,1,0:T(8,128)(2,1)S(1)}, u32[]{:S(2)}, u32[]{:S(2)}) async-start(bf16[4,2,256,128]{3,2,1,0:T(8,128)(2,1)} %copy-done.25), calls=%async_computation.3 | async-start | bytes 1048576 | tf_op jit(solution)/shard_map/all_to_all | solution.py:1388
  124.7 176.2 %all-gather.8.cloned.1.call-start = ((), (), s32[]{:S(2)}) async-start(), calls=%async_computation.12 | async-start | bytes 9437184 | tf_op jit(solution)/shard_map/all_gather | solution.py:1394
  190.5 395.1 %reduce-scatter.5.cloned.1.call-start = ((), (), s32[]{:S(2)}) async-start(), calls=%async_computation.14 | async-start | bytes 9437184 | tf_op jit(solution)/shard_map/reduce_scatter | solution.py:1409
  274.7 21.3 %collective-permute-start.35 = (bf16[128,2048]{1,0:T(8,128)(2,1)S(1)}, bf16[128,2048]{1,0:T(8,128)(2,1)S(1)}, u32[]{:S(2)}, u32[]{:S(2)}) collective-permute-start(bf16[128,2048]{1,0:T(8,128)(2,1)S(1)} %add_convert_fusion.4), channel_id=1, source_target_pairs={{1,0},{2,1},{3,2},{5,4},{6,5},{7,6},{9,8},{10,9},{11,10},{13,12},{... | collective-permute-start | bytes 1572872 | tf_op jit(solution)/shard_map/ppermute | solution.py:612
  276.0 22.3 %collective-permute-start.34 = (bf16[128,2048]{1,0:T(8,128)(2,1)}, bf16[128,2048]{1,0:T(8,128)(2,1)S(1)}, u32[]{:S(2)}, u32[]{:S(2)}) collective-permute-start(bf16[128,2048]{1,0:T(8,128)(2,1)} %add_convert_fusion.5), channel_id=1, source_target_pairs={{0,1},{1,2},{2,3},{4,5},{5,6},{6,7},{8,9},{9,10},{10,11},{12,13},{... | collective-permute-start | bytes 1572872 | tf_op jit(solution)/shard_map/ppermute | solution.py:611
  300.9 14.5 %collective-permute-start.39 = (bf16[128,2048]{1,0:T(8,128)(2,1)S(1)}, bf16[128,2048]{1,0:T(8,128)(2,1)S(1)}, u32[]{:S(2)}, u32[]{:S(2)}) collective-permute-start(bf16[128,2048]{1,0:T(8,128)(2,1)S(1)} %get-tuple-element.194.refs_0_), channel_id=1, source_target_pairs={{1,0},{2,1},{3,2},{5,4},{6,5},{7,6},{9,8},{10,9},{11,10},{13,12},{... | collective-permute-start | bytes 1572872 | tf_op jit(solution)/shard_map/ppermute | solution.py:598
  302.2 14.5 %collective-permute-start.36 = (bf16[128,2048]{1,0:T(8,128)(2,1)S(1)}, bf16[128,2048]{1,0:T(8,128)(2,1)S(1)}, u32[]{:S(2)}, u32[]{:S(2)}) collective-permute-start(bf16[128,2048]{1,0:T(8,128)(2,1)S(1)} %get-tuple-element.194.refs_0_), channel_id=1, source_target_pairs={{0,1},{1,2},{2,3},{4,5},{5,6},{6,7},{8,9},{9,10},{10,11},{12,13},{... | collective-permute-start | bytes 1572872 | tf_op jit(solution)/shard_map/ppermute | solution.py:597
  347.6 238.0 %reduce-scatter.3.cloned.1.call-start = ((), (), s32[]{:S(2)}) async-start(), calls=%async_computation.13 | async-start | bytes 18874368 | tf_op jit(solution)/shard_map/reduce_scatter | solution.py:1409
  383.4 16.2 %collective-permute-start.44 = (bf16[128,2048]{1,0:T(8,128)(2,1)S(1)}, bf16[128,2048]{1,0:T(8,128)(2,1)}, u32[]{:S(2)}, u32[]{:S(2)}) collective-permute-start(bf16[128,2048]{1,0:T(8,128)(2,1)S(1)} %get-tuple-element.264), channel_id=1, source_target_pairs={{0,1},{1,2},{4,5},{5,6},{8,9},{9,10},{12,13},{13,14},{16,17},{17,1... | collective-permute-start | bytes 1572872 | tf_op jit(solution)/shard_map/ppermute | solution.py:611
  423.3 20.4 %all-to-all-start.4 = ((bf16[16,2,64,128]{3,2,1,0:T(8,128)(2,1)}), bf16[16,2,64,128]{3,2,1,0:T(8,128)(2,1)S(1)}, u32[]{:S(2)}, u32[]{:S(2)}) async-start(bf16[16,2,64,128]{3,2,1,0:T(8,128)(2,1)} %bitcast.11), calls=%async_computation.4 | async-start | bytes 1048576 | tf_op jit(solution)/shard_map/all_to_all | solution.py:1420
  431.6 27.7 %collective-permute-start.51 = (bf16[128,2048]{1,0:T(8,128)(2,1)}, bf16[128,2048]{1,0:T(8,128)(2,1)}, u32[]{:S(2)}, u32[]{:S(2)}) collective-permute-start(bf16[128,2048]{1,0:T(8,128)(2,1)} %get-tuple-element.213.grad_ref.refs_0_), channel_id=1, source_target_pairs={{1,0},{2,1},{3,2},{5,4},{6,5},{7,6},{9,8},{10,9},{11,10},{13,12},{... | collective-permute-start | bytes 1572872 | tf_op jit(solution)/shard_map/ppermute | solution.py:598
  432.9 28.0 %collective-permute-start.48 = (bf16[128,2048]{1,0:T(8,128)(2,1)}, bf16[128,2048]{1,0:T(8,128)(2,1)}, u32[]{:S(2)}, u32[]{:S(2)}) collective-permute-start(bf16[128,2048]{1,0:T(8,128)(2,1)} %get-tuple-element.213.grad_ref.refs_0_), channel_id=1, source_target_pairs={{0,1},{1,2},{2,3},{4,5},{5,6},{6,7},{8,9},{9,10},{10,11},{12,13},{... | collective-permute-start | bytes 1572872 | tf_op jit(solution)/shard_map/ppermute | solution.py:597
  454.9 30.0 %all-to-all-start.5 = ((bf16[4,3,2,256,128]{4,3,2,1,0:T(8,128)(2,1)}), bf16[4,3,2,256,128]{4,3,2,1,0:T(8,128)(2,1)}, u32[]{:S(2)}, u32[]{:S(2)}) async-start(bf16[4,3,2,256,128]{4,3,2,1,0:T(8,128)(2,1)} %attend_back.1), calls=%async_computation.5 | async-start | bytes 3145728 | tf_op jit(solution)/shard_map/all_to_all | solution.py:1424
  533.2 27.0 %collective-permute-start.59 = (bf16[128,2176]{1,0:T(8,128)(2,1)S(1)}, bf16[128,2176]{1,0:T(8,128)(2,1)S(1)}, u32[]{:S(2)}, u32[]{:S(2)}) collective-permute-start(bf16[128,2176]{1,0:T(8,128)(2,1)S(1)} %get-tuple-element.231), channel_id=1, source_target_pairs={{0,4},{4,0},{8,12},{12,8},{1,5},{5,1},{9,13},{13,9},{2,6},{6,2},{1... | collective-permute-start | bytes 1671176 | tf_op jit(solution)/shard_map/ppermute | solution.py:410
  535.2 25.0 %collective-permute-start.60 = (bf16[128,2176]{1,0:T(8,128)(2,1)S(1)}, bf16[128,2176]{1,0:T(8,128)(2,1)S(1)}, u32[]{:S(2)}, u32[]{:S(2)}) collective-permute-start(bf16[128,2176]{1,0:T(8,128)(2,1)S(1)} %get-tuple-element.232), channel_id=1, source_target_pairs={{0,8},{4,12},{8,0},{12,4},{1,9},{5,13},{9,1},{13,5},{2,10},{6,14},... | collective-permute-start | bytes 1671176 | tf_op jit(solution)/shard_map/ppermute | solution.py:410
  539.7 26.0 %collective-permute-start.58 = (bf16[128,2048]{1,0:T(8,128)(2,1)S(1)}, bf16[128,2048]{1,0:T(8,128)(2,1)S(1)}, u32[]{:S(2)}, u32[]{:S(2)}) collective-permute-start(bf16[128,2048]{1,0:T(8,128)(2,1)S(1)} %get-tuple-element.261), channel_id=1, source_target_pairs={{2,1},{3,2},{6,5},{7,6},{10,9},{11,10},{14,13},{15,14},{18,17},{19... | collective-permute-start | bytes 1572872 | tf_op jit(solution)/shard_map/ppermute | solution.py:612
  540.4 25.3 %collective-permute-start.57 = (bf16[128,2048]{1,0:T(8,128)(2,1)S(1)}, bf16[128,2048]{1,0:T(8,128)(2,1)S(1)}, u32[]{:S(2)}, u32[]{:S(2)}) collective-permute-start(bf16[128,2048]{1,0:T(8,128)(2,1)S(1)} %get-tuple-element.262), channel_id=1, source_target_pairs={{0,1},{1,2},{4,5},{5,6},{8,9},{9,10},{12,13},{13,14},{16,17},{17,1... | collective-permute-start | bytes 1572872 | tf_op jit(solution)/shard_map/ppermute | solution.py:611
  565.7 26.6 %collective-permute-start.63 = (bf16[256,2176]{1,0:T(8,128)(2,1)}, bf16[256,2176]{1,0:T(8,128)(2,1)S(1)}, u32[]{:S(2)}, u32[]{:S(2)}) collective-permute-start(bf16[256,2176]{1,0:T(8,128)(2,1)} %get-tuple-element.241), channel_id=1, source_target_pairs={{0,4},{4,0},{8,12},{12,8},{1,5},{5,1},{9,13},{13,9},{2,6},{6,2},{1... | collective-permute-start | bytes 3342344 | tf_op jit(solution)/shard_map/ppermute | solution.py:410
  567.3 26.3 %collective-permute-start.64 = (bf16[256,2176]{1,0:T(8,128)(2,1)}, bf16[256,2176]{1,0:T(8,128)(2,1)S(1)}, u32[]{:S(2)}, u32[]{:S(2)}) collective-permute-start(bf16[256,2176]{1,0:T(8,128)(2,1)} %get-tuple-element.242), channel_id=1, source_target_pairs={{0,8},{4,12},{8,0},{12,4},{1,9},{5,13},{9,1},{13,5},{2,10},{6,14},... | collective-permute-start | bytes 3342344 | tf_op jit(solution)/shard_map/ppermute | solution.py:410
  568.1 15.0 %collective-permute-start.62 = (bf16[128,2048]{1,0:T(8,128)(2,1)S(1)}, bf16[128,2048]{1,0:T(8,128)(2,1)S(1)}, u32[]{:S(2)}, u32[]{:S(2)}) collective-permute-start(bf16[128,2048]{1,0:T(8,128)(2,1)S(1)} %add_convert_fusion), channel_id=1, source_target_pairs={{1,0},{2,1},{3,2},{5,4},{6,5},{7,6},{9,8},{10,9},{11,10},{13,12},{... | collective-permute-start | bytes 1572872 | tf_op jit(solution)/shard_map/ppermute | solution.py:612
  569.4 14.9 %collective-permute-start.61 = (bf16[128,2048]{1,0:T(8,128)(2,1)S(1)}, bf16[128,2048]{1,0:T(8,128)(2,1)S(1)}, u32[]{:S(2)}, u32[]{:S(2)}) collective-permute-start(bf16[128,2048]{1,0:T(8,128)(2,1)S(1)} %add_convert_fusion.1), channel_id=1, source_target_pairs={{0,1},{1,2},{2,3},{4,5},{5,6},{6,7},{8,9},{9,10},{10,11},{12,13},{... | collective-permute-start | bytes 1572872 | tf_op jit(solution)/shard_map/ppermute | solution.py:611
  (99 other events, 932.9 us)
Sparse Core Ops, SparseCore 0:
  16.7 27.3 all-gather.3
  48.0 150.8 all-gather.5
  200.7 54.3 all-gather.7
  347.7 78.4 reduce-scatter.4
  430.0 131.5 reduce-scatter.2
